TPU v7x, 32 devices: a whole 2x2x4 slice. The times are simulated.
32 devices in a mesh: row: 4 (over z), col: 8 (over y, x, core).
Axes of the slice: x: 2, y: 2, z: 4, core: 2. Of those that a mesh axis runs over, the one named last changes fastest.
Arguments:
- stress: float32 [8192, 512], P(('row', 'col')), may hold values from -2.5 to 2.5
- friction_state: float32 [8192, 512], P(('row', 'col')), may hold values from -0.5 to 0.5
- direct: float32 [8192, 512], P(('row', 'col')), may hold values from 0.5 to 1
- evolve: float32 [8192, 512], P(('row', 'col')), may hold values from 0.5 to 1
- relax_rate: float32 [8192, 512], P(('row', 'col')), may hold values from 0.2 to 1
- load_rate: float32 [8192, 512], P(('row', 'col')), may hold values from -4 to 4
- row_perm: int32 [64], P('row'), may hold values from 0 to 63, as said below
- patch_rows: int32 [64], P(('row', 'col')), may hold values from 0 to 15, as said below
- near_cols: int32 [64, 8, 7], P('row', 'col'), may hold values from -1 to 7, as said below
- near_blocks: bfloat16 [64, 8, 7, 128, 128], P('row', 'col'), may hold values from -0.0625 to 0.0625
- far_cols: int32 [64, 8, 9], P('row', 'col'), may hold values from 0 to 7
- far_ranks: int32 [64, 8, 9], P('row', 'col'), may hold values from 8 to 32
- far_left: bfloat16 [64, 8, 9, 32, 128], P('row', 'col'), may hold values from -0.125 to 0.125
- far_right: bfloat16 [64, 8, 9, 32, 128], P('row', 'col'), may hold values from -0.5 to 0.5
Outputs:
- stress_next: float32 [8192, 512], P(('row', 'col'))
- state_next: float32 [8192, 512], P(('row', 'col'))
Inputs may be any that keep to these rules, and one draw needn't show every extreme that they name: `row_perm`: A permutation of the 64 blocks; each index of row holds, at positions r * 16 to (r + 1) * 16 - 1, exactly 2 blocks of every column group. `patch_rows`: for each index r of row, entries r * 16 to (r + 1) * 16 - 1 are a permutation of 0 to 15. `near_cols`: in each block row and column group the live slots come first, 1 to 7 of them, distinct; 7 live slots occur in every draw.
All inputs are finite; a program needn't handle non-finite values.
Results may differ from a plain program's by a relative error of at most 0.0038.
Values may be sent and summed in bfloat16 or wider, within the bound.
No kernel may reach another device: no remote copies, remote signals or barrier semaphores. Data moves between devices by JAX's collectives and lax.ppermute only.
A program may use at most 256 MiB of HBM per device.

v0:
```python
import jax
import jax.numpy as jnp
from jax import lax
from jax.sharding import PartitionSpec as P

TIME_STEP = 0.1
SECTION_SHIFT = 2.0 / 3.0
FIRST_WEIGHT = 0.25
SECOND_WEIGHT = 0.75


def slip_velocity(stress, friction_state, direct):
    return 2.0 * jnp.sinh(stress / direct) * jnp.exp(-friction_state / direct)


def shards(
    stress,
    friction_state,
    direct,
    evolve,
    relax_rate,
    load_rate,
    row_perm,
    patch_rows,
    near_cols,
    near_blocks,
    far_cols,
    far_ranks,
    far_left,
    far_right,
):
    col_count = lax.axis_size("col")
    col_index = lax.axis_index("col")
    row_count = lax.axis_size("row")
    rows_dev = row_perm.shape[0]
    patch_count = patch_rows.shape[0]
    group_width = rows_dev * row_count // col_count
    cell_block = near_blocks.shape[-1]
    members = stress.shape[1]
    rank_size = far_left.shape[3]
    chosen = jnp.nonzero(row_perm // group_width == col_index, size=patch_count)[0].astype(
        jnp.int32
    )
    chosen_ids = row_perm[chosen] % group_width
    cols_near = near_cols[:, 0]
    live_mask = (cols_near >= 0).astype(jnp.bfloat16)[:, :, None, None]
    safe_near = jnp.maximum(cols_near, 0)
    cols_far = far_cols[:, 0]
    keep_rank = (
        jnp.arange(rank_size, dtype=jnp.int32)[None, None, :, None]
        < far_ranks[:, 0][:, :, None, None]
    )
    blocks_near = near_blocks[:, 0]
    left_factors = far_left[:, 0]
    right_factors = far_right[:, 0]

    def traction_of(vel_b):
        local_rates = vel_b.reshape(patch_count, cell_block, members)
        gathered, patch_all = (
            lax.all_gather(local_rates, "col", axis=0, tiled=True),
            lax.all_gather(patch_rows, "col", axis=0, tiled=True),
        )
        by_row = (
            jnp.zeros((rows_dev, cell_block, members), jnp.bfloat16).at[patch_all].set(gathered)
        )
        mine_vals = by_row[chosen]
        group_vals, group_ids = (
            lax.all_gather(mine_vals, "row", axis=0, tiled=True),
            lax.all_gather(chosen_ids, "row", axis=0, tiled=True),
        )
        in_group = (
            jnp.zeros((group_width, cell_block, members), jnp.bfloat16)
            .at[group_ids]
            .set(group_vals)
        )
        near_x = in_group[safe_near] * live_mask
        partial_value = jnp.einsum(
            "ikab,ikbe->iae", blocks_near, near_x, preferred_element_type=jnp.float32
        )
        coeffs = jnp.einsum(
            "ikrb,ikbe->ikre", right_factors, in_group[cols_far], preferred_element_type=jnp.float32
        )
        coeffs = jnp.where(keep_rank, coeffs, 0.0).astype(jnp.bfloat16)
        partial_value = partial_value + jnp.einsum(
            "ikrb,ikre->ibe", left_factors, coeffs, preferred_element_type=jnp.float32
        )
        summed = lax.psum(partial_value, "col")
        own_part = summed[patch_rows]
        return own_part.reshape(patch_count * cell_block, members)

    def rates(stress_now, state_now):
        velocity = slip_velocity(stress_now, state_now, direct)
        traction = traction_of(velocity.astype(jnp.bfloat16))
        return (load_rate - traction, relax_rate * (jnp.exp(-state_now / evolve) - velocity))

    first_stress, first_state = rates(stress, friction_state)
    stress_mid = stress + TIME_STEP * SECTION_SHIFT * first_stress
    state_mid = friction_state + TIME_STEP * SECTION_SHIFT * first_state
    second_stress, second_state = rates(stress_mid, state_mid)
    stress_next = stress + TIME_STEP * (FIRST_WEIGHT * first_stress + SECOND_WEIGHT * second_stress)
    state_next = friction_state + TIME_STEP * (
        FIRST_WEIGHT * first_state + SECOND_WEIGHT * second_state
    )
    return (stress_next, state_next)


def solution(mesh):
    placed = (
        P(("row", "col"), None),
        P(("row", "col"), None),
        P(("row", "col"), None),
        P(("row", "col"), None),
        P(("row", "col"), None),
        P(("row", "col"), None),
        P("row"),
        P(("row", "col")),
        P("row", "col", None),
        P("row", "col", None, None, None),
        P("row", "col", None),
        P("row", "col", None),
        P("row", "col", None, None, None),
        P("row", "col", None, None, None),
    )
    return jax.shard_map(
        shards,
        mesh=mesh,
        in_specs=placed,
        out_specs=(P(("row", "col"), None), P(("row", "col"), None)),
        check_vma=False,
    )
```

profile of v0, /device:TPU:0, one launch (start us, length us, event | category | flops | bytes accessed | tf_op | source)
XLA Modules:
  0.0 443.9 jit_solution(2984738201044279427)
XLA Ops:
  7.2 2.9 fusion.58
  10.2 1.2 dynamic-slice.1
  12.8 9.5 %all-reduce.1 = s32[16]{0:T(128)S(1)} all-reduce(s32[16]{0:T(128)S(1)} %dynamic-update-slice.1), channel_id=1, replica_groups=mesh['row'=4,'col'=8] {'col'}, use_global_device_ids=true, to_apply=%add.1 | all-reduce | flops 16 | bytes 128
  22.3 1.3 fusion.60
  25.2 15.9 %all-gather.7.cloned.1.call-done = bf16[16,128,512]{2,1,0:T(8,128)(2,1)} async-done(((bf16[2,128,512]{2,1,0:T(8,128)(2,1)}), bf16[16,128,512]{2,1,0:T(8,128)(2,1)}) %all-gather.7.cloned.1.call-update) | async-done | bytes 2097168 | tf_op jit(solution)/shard_map/all_gather | solution.py:60
  41.4 3.4 scatter_fusion
  44.8 1.3 gather_fusion.1
  48.2 8.3 %all-reduce = s32[8]{0:T(128)S(1)} all-reduce(s32[8]{0:T(128)S(1)} %fusion.49), channel_id=1, replica_groups=mesh['row'=4,'col'=8] {'row'}, use_global_device_ids=true, to_apply=%add | all-reduce | flops 8 | bytes 64
  57.2 17.0 %all-gather.11.cloned.1.call-done = bf16[8,128,512]{2,1,0:T(8,128)(2,1)} async-done(((bf16[2,128,512]{2,1,0:T(8,128)(2,1)}), bf16[8,128,512]{2,1,0:T(8,128)(2,1)}) %all-gather.11.cloned.1.call-update) | async-done | bytes 1048592 | tf_op jit(solution)/shard_map/all_gather | solution.py:68
  74.3 2.0 scatter_fusion.1
  76.3 7.6 %gather_fusion.2 = bf16[112,128,512]{2,1,0:T(8,128)(2,1)} fusion(bf16[8,128,512]{2,1,0:T(8,128)(2,1)S(1)} %scatter_fusion.1, s32[1024]{0:T(1024)S(1)} %pad_clamp_fusion.2), kind=kCustom, calls=%fused_computation.2 | custom fusion | bytes 29360576 | tf_op jit(solution)/shard_map/gather | solution.py:76
  83.9 20.7 %copy.38 = bf16[16,7,128,512]{2,3,1,0:T(8,128)(2,1)} copy(bf16[16,7,128,512]{3,2,1,0:T(8,128)(2,1)} %bitcast.90) | data formatting | bytes 29360128 | tf_op jit(solution)/shard_map/gather | solution.py:76
  104.6 9.0 %gather_fusion.3 = bf16[144,128,512]{2,1,0:T(8,128)(2,1)} fusion(bf16[8,128,512]{2,1,0:T(8,128)(2,1)S(1)} %scatter_fusion.1, s32[1024]{0:T(1024)S(1)} %pad_clamp_fusion.1), kind=kCustom, calls=%fused_computation.3 | custom fusion | bytes 37749312 | tf_op jit(solution)/shard_map/gather | solution.py:81
  113.6 12.4 %fusion.2 = f32[16,512,128,1]{2,1,3,0:T(8,128)} fusion(bf16[16,7,128,512]{2,3,1,0:T(8,128)(2,1)} %copy.38, bf16[16,7]{1,0:T(8,128)(2,1)S(1)} %copy.37, bf16[16,1,7,128,128]{4,3,2,1,0:T(8,128)(2,1)} %param.23), kind=kOutput, calls=%fused_computation.16 | convolution fusion | flops 1886388224 | bytes 22544608 | tf_op jit(solution)/shard_map/ikab,ikbe->iae/dot_general | solution.py:77
  125.9 11.3 %fusion.21 = f32[16,128,512]{1,2,0:T(8,128)} fusion(f32[16,512,128,1]{2,1,3,0:T(8,128)} %fusion.2, bf16[16,9,128,512]{3,2,1,0:T(8,128)(2,1)} %bitcast.88, pred[16,9,32]{2,1,0:T(8,128)(4,1)S(1)} %iota_compare_fusion, bf16[16,1,9,32,128]{4,3,2,1,0:T(8,128)(2,1)S(1)} %copy-done, bf16[16,1,9,32,128]{4,3,2,1,0:T(8,128)(2,1)S(1)} %copy-done.2), kind=kOutput, calls=%fused_computation.35 | convolution fusion | flops 1213726720 | bytes 29626880 | tf_op jit(solution)/shard_map/ikrb,ikre->ibe/dot_general | solution.py:84
  137.9 80.1 %all-reduce.5.cloned.1.call-done = f32[16,128,512]{1,2,0:T(8,128)} async-done(((f32[16,128,512]{1,2,0:T(8,128)}), f32[16,128,512]{1,2,0:T(8,128)}) %all-reduce.5.cloned.1.call-update) | async-done | bytes 4194320 | tf_op jit(solution)/shard_map/psum | solution.py:87
  218.0 3.6 gather_fusion.4
  221.5 1.2 copy.41
  222.8 3.5 multiply_add_fusion
  226.4 28.1 %all-gather.9.cloned.1.call-done = bf16[16,128,512]{2,1,0:T(8,128)(2,1)} async-done(((bf16[2,128,512]{2,1,0:T(8,128)(2,1)}), bf16[16,128,512]{2,1,0:T(8,128)(2,1)}) %all-gather.9.cloned.1.call-update) | async-done | bytes 2097168 | tf_op jit(solution)/shard_map/all_gather | solution.py:60
  254.7 3.4 scatter_fusion.2
  258.1 1.3 gather_fusion.5
  259.5 28.0 %all-gather.13.cloned.1.call-done = bf16[8,128,512]{2,1,0:T(8,128)(2,1)} async-done(((bf16[2,128,512]{2,1,0:T(8,128)(2,1)}), bf16[8,128,512]{2,1,0:T(8,128)(2,1)}) %all-gather.13.cloned.1.call-update) | async-done | bytes 1048592 | tf_op jit(solution)/shard_map/all_gather | solution.py:68
  287.6 2.0 scatter_fusion.3
  289.6 7.6 %gather_fusion.6 = bf16[112,128,512]{2,1,0:T(8,128)(2,1)} fusion(bf16[8,128,512]{2,1,0:T(8,128)(2,1)S(1)} %scatter_fusion.3, s32[1024]{0:T(1024)S(1)} %pad_clamp_fusion.2), kind=kCustom, calls=%fused_computation.6 | custom fusion | bytes 29360576 | tf_op jit(solution)/shard_map/gather | solution.py:76
  297.2 9.0 %gather_fusion.7 = bf16[144,128,512]{2,1,0:T(8,128)(2,1)} fusion(bf16[8,128,512]{2,1,0:T(8,128)(2,1)S(1)} %scatter_fusion.3, s32[1024]{0:T(1024)S(1)} %pad_clamp_fusion.1), kind=kCustom, calls=%fused_computation.7 | custom fusion | bytes 37749312 | tf_op jit(solution)/shard_map/gather | solution.py:81
  306.2 20.7 %copy.42 = bf16[16,7,128,512]{2,3,1,0:T(8,128)(2,1)} copy(bf16[16,7,128,512]{3,2,1,0:T(8,128)(2,1)} %bitcast.89) | data formatting | bytes 29360128 | tf_op jit(solution)/shard_map/gather | solution.py:76
  326.9 12.3 %fusion = f32[16,512,128,1]{2,1,3,0:T(8,128)} fusion(bf16[16,7,128,512]{2,3,1,0:T(8,128)(2,1)} %copy.42, bf16[16,7]{1,0:T(8,128)(2,1)S(1)} %copy.37, bf16[16,1,7,128,128]{4,3,2,1,0:T(8,128)(2,1)} %param.23), kind=kOutput, calls=%fused_computation.14 | convolution fusion | flops 1886388224 | bytes 22544608 | tf_op jit(solution)/shard_map/ikab,ikbe->iae/dot_general | solution.py:77
  339.2 11.3 %fusion.20 = f32[16,128,512]{1,2,0:T(8,128)} fusion(f32[16,512,128,1]{2,1,3,0:T(8,128)} %fusion, bf16[16,9,128,512]{3,2,1,0:T(8,128)(2,1)} %bitcast.87, pred[16,9,32]{2,1,0:T(8,128)(4,1)S(1)} %iota_compare_fusion, bf16[16,1,9,32,128]{4,3,2,1,0:T(8,128)(2,1)S(1)} %copy-done, bf16[16,1,9,32,128]{4,3,2,1,0:T(8,128)(2,1)S(1)} %copy-done.3), kind=kOutput, calls=%fused_computation.33 | convolution fusion | flops 1213726720 | bytes 29626880 | tf_op jit(solution)/shard_map/ikrb,ikre->ibe/dot_general | solution.py:84
  350.5 80.7 %all-reduce.7.cloned.1.call-done = f32[16,128,512]{1,2,0:T(8,128)} async-done(((f32[16,128,512]{1,2,0:T(8,128)}), f32[16,128,512]{1,2,0:T(8,128)}) %all-reduce.7.cloned.1.call-update) | async-done | bytes 4194320 | tf_op jit(solution)/shard_map/psum | solution.py:87
  431.2 3.6 gather_fusion.8
  434.7 1.2 copy.43
  (79 shorter events, 7.1 us)
Async XLA Ops:
  7.2 118.8 %copy-start = (bf16[16,1,9,32,128]{4,3,2,1,0:T(8,128)(2,1)S(1)}, bf16[16,1,9,32,128]{4,3,2,1,0:T(8,128)(2,1)}, u32[]{:S(2)}) copy-start(bf16[16,1,9,32,128]{4,3,2,1,0:T(8,128)(2,1)} %param.26) | copy-start | bytes 3538948
  7.2 33.9 %all-gather.7.cloned.1.call-start = ((), (), s32[]{:S(2)}) async-start(), calls=%async_computation | async-start | bytes 2359296 | tf_op jit(solution)/shard_map/all_gather | solution.py:60
  10.1 64.1 %all-gather.11.cloned.1.call-start = ((), (), s32[]{:S(2)}) async-start(), calls=%async_computation.4 | async-start | bytes 1310720 | tf_op jit(solution)/shard_map/all_gather | solution.py:68
  25.2 20.9 %copy-start.1 = (s32[16]{0:T(128)S(1)}, s32[16]{0:T(128)}, u32[]{:S(2)}) copy-start(s32[16]{0:T(128)} %param.20) | copy-start | bytes 196
  41.3 5.5 %copy-start.15 = (u32[32]{0:T(128)S(1)}, u32[32]{0:T(128)}, u32[]{:S(2)}) copy-start(u32[32]{0:T(128)} %constant.105) | copy-start | bytes 388
  41.3 15.1 %copy-start.11 = (s32[16,1,7]{0,1,2:T(1,128)S(1)}, s32[16,1,7]{0,1,2:T(1,128)}, u32[]{:S(2)}) copy-start(s32[16,1,7]{0,1,2:T(1,128)} %param.22) | copy-start | bytes 1348
  41.3 15.4 %copy-start.13 = (s32[16,1,9]{0,1,2:T(1,128)S(1)}, s32[16,1,9]{0,1,2:T(1,128)}, u32[]{:S(2)}) copy-start(s32[16,1,9]{0,1,2:T(1,128)} %param.24) | copy-start | bytes 1732
  41.3 15.6 %copy-start.12 = (s32[16,1,9]{0,1,2:T(1,128)S(1)}, s32[16,1,9]{0,1,2:T(1,128)}, u32[]{:S(2)}) copy-start(s32[16,1,9]{0,1,2:T(1,128)} %param.25) | copy-start | bytes 1732
  46.1 171.9 %all-reduce.5.cloned.1.call-start = ((), (), s32[]{:S(2)}) async-start(), calls=%async_computation.1 | async-start | bytes 8388608 | tf_op jit(solution)/shard_map/psum | solution.py:87
  113.6 12.4 %copy-start.2 = (bf16[16,1,9,32,128]{4,3,2,1,0:T(8,128)(2,1)S(1)}, bf16[16,1,9,32,128]{4,3,2,1,0:T(8,128)(2,1)}, u32[]{:S(2)}) copy-start(bf16[16,1,9,32,128]{4,3,2,1,0:T(8,128)(2,1)} %param.27) | copy-start | bytes 3538948
  137.3 0.7 copy-start.14
  137.3 85.5 %copy-start.6 = (f32[256,512]{1,0:T(8,128)S(1)}, f32[256,512]{1,0:T(8,128)}, u32[]{:S(2)}) copy-start(f32[256,512]{1,0:T(8,128)} %param.14) | copy-start | bytes 1572868
  137.3 85.5 %copy-start.8 = (f32[256,512]{1,0:T(8,128)S(1)}, f32[256,512]{1,0:T(8,128)}, u32[]{:S(2)}) copy-start(f32[256,512]{1,0:T(8,128)} %param.19) | copy-start | bytes 1572868
  137.3 85.5 %copy-start.10 = (f32[256,512]{1,0:T(8,128)S(1)}, f32[256,512]{1,0:T(8,128)}, u32[]{:S(2)}) copy-start(f32[256,512]{1,0:T(8,128)} %param.16) | copy-start | bytes 1572868
  137.3 117.2 %all-gather.9.cloned.1.call-start = ((), (), s32[]{:S(2)}) async-start(), calls=%async_computation.2 | async-start | bytes 2359296 | tf_op jit(solution)/shard_map/all_gather | solution.py:60
  222.8 3.6 copy-start.4
  226.3 61.2 %all-gather.13.cloned.1.call-start = ((), (), s32[]{:S(2)}) async-start(), calls=%async_computation.5 | async-start | bytes 1310720 | tf_op jit(solution)/shard_map/all_gather | solution.py:68
  259.4 171.8 %all-reduce.7.cloned.1.call-start = ((), (), s32[]{:S(2)}) async-start(), calls=%async_computation.3 | async-start | bytes 8388608 | tf_op jit(solution)/shard_map/psum | solution.py:87
  326.9 12.3 %copy-start.3 = (bf16[16,1,9,32,128]{4,3,2,1,0:T(8,128)(2,1)S(1)}, bf16[16,1,9,32,128]{4,3,2,1,0:T(8,128)(2,1)}, u32[]{:S(2)}) copy-start(bf16[16,1,9,32,128]{4,3,2,1,0:T(8,128)(2,1)} %param.27) | copy-start | bytes 3538948
  350.5 85.5 %copy-start.5 = (f32[2,128,512]{2,1,0:T(8,128)S(1)}, f32[2,128,512]{2,1,0:T(8,128)}, u32[]{:S(2)}) copy-start(f32[2,128,512]{2,1,0:T(8,128)} %copy-done.4) | copy-start | bytes 1572868
  350.5 85.5 %copy-start.7 = (f32[256,512]{1,0:T(8,128)S(1)}, f32[256,512]{1,0:T(8,128)}, u32[]{:S(2)}) copy-start(f32[256,512]{1,0:T(8,128)} %param.14) | copy-start | bytes 1572868
  350.5 85.5 %copy-start.9 = (f32[256,512]{1,0:T(8,128)S(1)}, f32[256,512]{1,0:T(8,128)}, u32[]{:S(2)}) copy-start(f32[256,512]{1,0:T(8,128)} %param.19) | copy-start | bytes 1572868
Sparse Core Ops, SparseCore 0:
  10.5 30.5 all-gather.6
  46.2 27.9 all-gather.10
  137.4 80.5 all-reduce.4
  226.5 27.9 all-gather.8
  259.5 27.9 all-gather.12
  350.6 80.5 all-reduce.6
where the time goes:
time: 446 us; the launch traced here: 444 us
  waiting for transfers between devices  250 us (56%)
  local copies, waits for them, and re-layouts  103 us (23%)
  matrix products  47.3 us (11%)
  blocking collectives  17.7 us (4%)
  between operations  15.6 us (3%)
  other arithmetic  10.5 us (2%)
    psum x2, waiting for transfers between devices, traction_of(): summed = lax.psum(partial_value, 'col')  161 us
    gather x4, local copies, waits for them, and re-layouts, traction_of(): near_x = in_group[safe_near] * live_mask  56.6 us
    all_gather x2, waiting for transfers between devices, traction_of(): lax.all_gather(mine_vals, 'row', axis=0, tiled=True)  45.1 us
    all_gather x2, waiting for transfers between devices, traction_of(): lax.all_gather(local_rates, 'col', axis=0, tiled=True)  43.9 us
    dot_general x2, matrix products, traction_of(): jnp.einsum('ikab,ikbe->iae', blocks_near, near_x, preferred_element_type=...  24.7 us
    dot_general x2, matrix products, traction_of(): jnp.einsum('ikrb,ikre->ibe', left_factors, coeffs, preferred_element_type...  22.6 us
    gather x2, local copies, waits for them, and re-layouts, traction_of(): in_group[cols_far]  18 us
    unnamed x2, blocking collectives  17.7 us
  transfers between devices with their start and end apart: 6, of which 6 were waited for; matrix products, arithmetic and copies ran while one was open for 2% of the time, Pallas kernels for 0%

commit v1 on v0

v1 whole, which is shorter than its diff:
```python
import functools

import jax
import jax.numpy as jnp
from jax import lax
from jax.experimental import pallas as pl
from jax.experimental.pallas import tpu as pltpu
from jax.sharding import PartitionSpec as P

TIME_STEP = 0.1
SECTION_SHIFT = 2.0 / 3.0
FIRST_WEIGHT = 0.25
SECOND_WEIGHT = 0.75
MID = TIME_STEP * SECTION_SHIFT
W1 = TIME_STEP * FIRST_WEIGHT
W2 = TIME_STEP * SECOND_WEIGHT
CHUNKS = 1

F32 = jnp.float32
BF16 = jnp.bfloat16
VMEM = pl.BlockSpec(memory_space=pltpu.VMEM)
SMEM = pl.BlockSpec(memory_space=pltpu.SMEM)
ANY = pl.BlockSpec(memory_space=pl.ANY)
LIMIT = 40 * 1024 * 1024


def params(limit=LIMIT):
    return pltpu.CompilerParams(vmem_limit_bytes=limit)


def cost(flops, nbytes, trans=0):
    return pl.CostEstimate(flops=int(flops), bytes_accessed=int(nbytes), transcendentals=int(trans))


def struct(shape, dtype):
    return jax.ShapeDtypeStruct(shape, dtype)


def plan_kernel(n_pair, n_row, patch_count, width, *refs):
    info = refs[0]
    patches = refs[1 : 1 + n_pair]
    perms = refs[1 + n_pair : 1 + n_pair + n_row]
    sel, arr, rows, inv = refs[1 + n_pair + n_row :]
    pair_patches = 2 * patch_count
    rows_dev = perms[0].shape[0]
    for m in range(n_pair):
        for i in range(pair_patches):
            q = patches[m][i]
            inv[q] = m * pair_patches + i
            rows[m * pair_patches + i] = q
    for side in range(2):
        group = info[1 + side]

        def pick(q, count):
            hit = lax.div(perms[0][q], width) == group

            @pl.when(hit)
            def _():
                sel[side * patch_count + count] = inv[q]

            return count + hit.astype(jnp.int32)

        lax.fori_loop(0, rows_dev, pick, jnp.int32(0))
    for s in range(n_row):

        def place(q, count):
            block = perms[s][q]
            hit = lax.div(block, width) == info[1]

            @pl.when(hit)
            def _():
                arr[lax.rem(block, width)] = s * patch_count + count

            return count + hit.astype(jnp.int32)

        lax.fori_loop(0, rows_dev, place, jnp.int32(0))


def make_plan(info, patches, perms, patch_count, width):
    n_pair, n_row = len(patches), len(perms)
    rows_dev = perms[0].shape[0]
    return pl.pallas_call(
        functools.partial(plan_kernel, n_pair, n_row, patch_count, width),
        out_shape=(
            struct((2 * patch_count,), jnp.int32),
            struct((width,), jnp.int32),
            struct((rows_dev,), jnp.int32),
        ),
        in_specs=[SMEM] * (1 + n_pair + n_row),
        out_specs=(SMEM,) * 3,
        scratch_shapes=[pltpu.SMEM((rows_dev,), jnp.int32)],
        cost_estimate=cost(1000, 1000),
        name="plan",
    )(info, *patches, *perms)


def build_kernel(rows, arr, near_cols, far_cols, far_ranks, near, left, right, out, spread, acc):
    slots, cell = near.shape[2], near.shape[3]
    far_slots, rank = left.shape[2], left.shape[3]
    q = rows[pl.program_id(0)]
    spread[...] = jnp.zeros_like(spread)
    ranks = lax.broadcasted_iota(jnp.int32, (rank, cell), 0)
    for k in range(far_slots):
        place = arr[far_cols[q * far_slots + k]]
        kept = jnp.where(ranks < far_ranks[q * far_slots + k], right[0, 0, k].astype(F32), 0.0)
        spread[pl.ds(k * rank, rank), pl.ds(pl.multiple_of(place * cell, cell), cell)] = kept.astype(BF16)
    acc[...] = lax.dot_general(
        left[0, 0].reshape(far_slots * rank, cell),
        spread[...],
        (((0,), (0,)), ((), ())),
        preferred_element_type=F32,
    )
    for k in range(slots):
        col = near_cols[q * slots + k]

        @pl.when(col >= 0)
        def _():
            at = pl.ds(pl.multiple_of(arr[jnp.maximum(col, 0)] * cell, cell), cell)
            acc[:, at] = acc[:, at] + near[0, 0, k].astype(F32)

    out[0] = acc[...].astype(BF16)


def build_matrix(rows, arr, near_cols, far_cols, far_ranks, near, left, right, n_pair):
    rows_dev, _, slots, cell, _ = near.shape
    far_slots, rank = left.shape[2], left.shape[3]
    depth = arr.shape[0] * cell
    per = rows_dev // n_pair

    def by_row(p, rows, *_):
        return (rows[p], 0, 0, 0, 0)

    return pl.pallas_call(
        build_kernel,
        out_shape=struct((n_pair, per * cell, depth), BF16),
        grid_spec=pltpu.PrefetchScalarGridSpec(
            num_scalar_prefetch=5,
            grid=(rows_dev,),
            in_specs=[
                pl.BlockSpec((1, 1, slots, cell, cell), by_row),
                pl.BlockSpec((1, 1, far_slots, rank, cell), by_row),
                pl.BlockSpec((1, 1, far_slots, rank, cell), by_row),
            ],
            out_specs=pl.BlockSpec((1, cell, depth), lambda p, *_: (p // per, p % per, 0)),
            scratch_shapes=[
                pltpu.VMEM((far_slots * rank, depth), BF16),
                pltpu.VMEM((cell, depth), F32),
            ],
        ),
        compiler_params=params(),
        cost_estimate=cost(
            2 * rows_dev * cell * far_slots * rank * depth, 2 * (near.size + left.size + right.size) + 2 * rows_dev * cell * depth
        ),
        name="build_matrix",
    )(rows, arr, near_cols, far_cols, far_ranks, near, left, right)


def pick_kernel(pair_patches, cell, sel, *refs):
    n_pair = len(refs) - 2
    sources, out, sems = refs[:n_pair], refs[n_pair], refs[n_pair + 1]
    for t in range(pair_patches):
        which = lax.div(sel[t], pair_patches)
        block = pl.multiple_of(lax.rem(sel[t], pair_patches) * cell, cell)
        for m in range(n_pair):

            @pl.when(which == m)
            def _():
                pltpu.make_async_copy(
                    sources[m].at[pl.ds(block, cell)], out.at[pl.ds(t * cell, cell)], sems.at[t]
                ).start()

    for t in range(pair_patches):
        pltpu.make_async_copy(
            sources[0].at[pl.ds(0, cell)], out.at[pl.ds(t * cell, cell)], sems.at[t]
        ).wait()


def pick(sel, sources, cell):
    pair_patches = sel.shape[0]
    return pl.pallas_call(
        functools.partial(pick_kernel, pair_patches, cell),
        out_shape=struct(sources[0].shape, BF16),
        in_specs=[SMEM] + [ANY] * len(sources),
        out_specs=ANY,
        scratch_shapes=[pltpu.SemaphoreType.DMA((pair_patches,))],
        cost_estimate=cost(0, 4 * sources[0].size),
        name="pick",
    )(sel, *sources)


def apply_kernel(n_pair, n_row, m_own, m_sib, *refs):
    pieces = refs[:n_row]
    outs = refs[n_row : n_row + n_pair]
    x_own, x_sib = refs[n_row + n_pair :]
    half = pieces[0].shape[0] // 2
    step = pl.program_id(0)

    @pl.when(step == 0)
    def _():
        for s in range(n_row):
            x_own[pl.ds(s * half, half)] = pieces[s][pl.ds(0, half)]
            x_sib[pl.ds(s * half, half)] = pieces[s][pl.ds(half, half)]

    total = jnp.dot(m_own[0], x_own[...], preferred_element_type=F32)
    total = total + jnp.dot(m_sib[0], x_sib[...], preferred_element_type=F32)
    for m in range(n_pair):

        @pl.when(step == m)
        def _():
            outs[m][...] = total.astype(outs[m].dtype)


def apply_matrix(m_own, m_sib, pieces):
    n_pair, high, depth = m_own.shape
    lanes = pieces[0].shape[1]
    block = pl.BlockSpec((1, high, depth), lambda m: (m, 0, 0))
    whole = pl.BlockSpec(pieces[0].shape, lambda m: (0, 0))
    return pl.pallas_call(
        functools.partial(apply_kernel, n_pair, len(pieces)),
        out_shape=tuple(struct((high, lanes), F32 if m == 0 else BF16) for m in range(n_pair)),
        grid=(n_pair,),
        in_specs=[block, block] + [whole] * len(pieces),
        out_specs=tuple(pl.BlockSpec((high, lanes), lambda m: (0, 0)) for _ in range(n_pair)),
        scratch_shapes=[pltpu.VMEM((depth, lanes), BF16)] * 2,
        compiler_params=params(),
        cost_estimate=cost(4 * n_pair * high * depth * lanes, 4 * m_own.size),
        name="apply_matrix",
    )(m_own, m_sib, *pieces)


def start_kernel(chunks, info, stress, state, direct, *outs):
    keep, give = outs[:chunks], outs[chunks:]
    half = stress.shape[1] // 2
    lanes = half // chunks
    side = info[0]
    for own, refs in ((False, give), (True, keep)):
        base = (side if own else 1 - side) * half
        for j in range(chunks):
            at = pl.ds(pl.multiple_of(base + j * lanes, lanes), lanes)
            inverse = 1.0 / direct[:, at]
            stress_now, state_now = stress[:, at], state[:, at]
            velocity = jnp.exp((stress_now - state_now) * inverse) - jnp.exp((-stress_now - state_now) * inverse)
            refs[j][...] = velocity.astype(BF16)


def start(info, stress, state, direct, chunks):
    high, members = stress.shape
    lanes = members // 2 // chunks
    tile = 128
    return pl.pallas_call(
        functools.partial(start_kernel, chunks),
        out_shape=(struct((high, lanes), BF16),) * (2 * chunks),
        grid=(high // tile,),
        in_specs=[SMEM] + [pl.BlockSpec((tile, members), lambda i: (i, 0))] * 3,
        out_specs=(pl.BlockSpec((tile, lanes), lambda i: (i, 0)),) * (2 * chunks),
        cost_estimate=cost(10 * stress.size, 14 * stress.size, 3 * stress.size),
        name="start",
    )(info, stress, state, direct)


def mid_kernel(chunks, info, stress, state, direct, evolve, relax, load, keep, give, base, state_base):
    half = stress.shape[1] // 2
    lanes = half // chunks
    side = info[0]
    for own, ref in ((True, keep), (False, give)):
        first = (side if own else 1 - side) * half
        for j in range(chunks):
            at = pl.ds(pl.multiple_of(first + j * lanes, lanes), lanes)
            inverse = 1.0 / direct[:, at]
            inverse_e = 1.0 / evolve[:, at]
            stress_now, state_now = stress[:, at], state[:, at]
            relax_now, load_now = relax[:, at], load[:, at]
            velocity = jnp.exp((stress_now - state_now) * inverse) - jnp.exp((-stress_now - state_now) * inverse)
            state_rate = relax_now * (jnp.exp(-state_now * inverse_e) - velocity)
            state_mid = state_now + MID * state_rate
            ref[j, 0] = stress_now + MID * load_now
            ref[j, 1] = inverse
            ref[j, 2] = jnp.exp(-state_mid * inverse)
            base[:, at] = stress_now + TIME_STEP * load_now
            state_base[:, at] = state_now + W1 * state_rate + W2 * relax_now * jnp.exp(-state_mid * inverse_e)


def mid(info, stress, state, direct, evolve, relax, load, chunks):
    high, members = stress.shape
    lanes = members // 2 // chunks
    tile = 128
    wide = pl.BlockSpec((tile, members), lambda i: (i, 0))
    split = pl.BlockSpec((chunks, 3, tile, lanes), lambda i: (0, 0, i, 0))
    return pl.pallas_call(
        functools.partial(mid_kernel, chunks),
        out_shape=(struct((chunks, 3, high, lanes), F32),) * 2 + (struct(stress.shape, F32),) * 2,
        grid=(high // tile,),
        in_specs=[SMEM] + [wide] * 6,
        out_specs=(split, split, wide, wide),
        cost_estimate=cost(20 * stress.size, 44 * stress.size, 6 * stress.size),
        name="mid",
    )(info, stress, state, direct, evolve, relax, load)


def merge_kernel(info, keep, recv, out):
    high = keep.shape[0]
    side = info[0]
    out[pl.ds(pl.multiple_of(side * high, high), high)] = keep[...]
    out[pl.ds(pl.multiple_of((1 - side) * high, high), high)] = recv[...]


def merge(info, keep, recv):
    high, lanes = keep.shape
    return pl.pallas_call(
        merge_kernel,
        out_shape=struct((2 * high, lanes), keep.dtype),
        in_specs=[SMEM, VMEM, VMEM],
        out_specs=VMEM,
        cost_estimate=cost(0, 8 * keep.size),
        name="merge",
    )(info, keep, recv)


def second_kernel(info, keep, recv, *refs):
    n_pair = len(refs) - 4
    parts = refs[:n_pair]
    total_out, vel_b, vel_keep, vel_give = refs[n_pair:]
    high = keep.shape[2]
    side = info[0]
    for own, held, vel_out in ((True, keep, vel_keep), (False, recv, vel_give)):
        at = pl.ds(pl.multiple_of((side if own else 1 - side) * high, high), high)
        total = parts[0][at]
        for m in range(1, n_pair):
            total = total + parts[m][at].astype(F32)
        total_out[at] = W1 * total
        scaled = (held[0, 0] - MID * total) * held[0, 1]
        velocity = held[0, 2] * (jnp.exp(scaled) - jnp.exp(-scaled))
        vel_b[at] = velocity.astype(BF16)
        vel_out[...] = velocity


def second(info, keep, recv, parts, chunk):
    high, lanes = parts[0].shape
    held = pl.BlockSpec((1, 3, high // 2, lanes), lambda i: (chunk, 0, 0, 0))
    whole = pl.BlockSpec((high, lanes), lambda i: (0, 0))
    half = pl.BlockSpec((high // 2, lanes), lambda i: (0, 0))
    return pl.pallas_call(
        second_kernel,
        out_shape=(struct((high, lanes), F32), struct((high, lanes), BF16))
        + (struct((high // 2, lanes), F32),) * 2,
        grid=(1,),
        in_specs=[SMEM, held, held] + [whole] * len(parts),
        out_specs=(whole, whole, half, half),
        cost_estimate=cost(10 * high * lanes, 40 * high * lanes, 2 * high * lanes),
        name="second",
    )(info, keep, recv, *parts)


def weigh_kernel(info, first, *refs):
    parts = refs[:-2]
    keep, give = refs[-2:]
    high = keep.shape[0]
    side = info[0]
    for own, ref in ((False, give), (True, keep)):
        at = pl.ds(pl.multiple_of((side if own else 1 - side) * high, high), high)
        total = parts[0][at]
        for part in parts[1:]:
            total = total + part[at].astype(F32)
        ref[...] = first[at] + W2 * total


def weigh(info, first, parts):
    high, lanes = first.shape
    return pl.pallas_call(
        weigh_kernel,
        out_shape=(struct((high // 2, lanes), F32),) * 2,
        in_specs=[SMEM] + [VMEM] * (1 + len(parts)),
        out_specs=(VMEM, VMEM),
        cost_estimate=cost(10 * high * lanes, 20 * high * lanes),
        name="weigh",
    )(info, first, *parts)


def finish_kernel(chunks, scaled, info, base, *refs):
    out = refs[-1]
    factor = refs[0] if scaled else None
    pieces = refs[1:-1] if scaled else refs[:-1]
    half = base.shape[1] // 2
    lanes = half // chunks
    side = info[0]
    for j in range(chunks):
        for own, piece in ((True, pieces[j]), (False, pieces[chunks + j])):
            first = (side if own else 1 - side) * half + j * lanes
            at = pl.ds(pl.multiple_of(first, lanes), lanes)
            change = piece[...]
            if scaled:
                change = W2 * factor[:, at] * change
            out[:, at] = base[:, at] - change


def finish(info, base, factor, keeps, recvs):
    chunks = len(keeps)
    scaled = factor is not None
    extra = [factor] if scaled else []
    return pl.pallas_call(
        functools.partial(finish_kernel, chunks, scaled),
        out_shape=struct(base.shape, F32),
        in_specs=[SMEM] + [VMEM] * (1 + len(extra) + 2 * chunks),
        out_specs=VMEM,
        cost_estimate=cost(3 * base.size, 16 * base.size),
        name="finish",
    )(info, base, *extra, *keeps, *recvs)


def shards(
    stress,
    friction_state,
    direct,
    evolve,
    relax_rate,
    load_rate,
    row_perm,
    patch_rows,
    near_cols,
    near_blocks,
    far_cols,
    far_ranks,
    far_left,
    far_right,
):
    n_col, n_row = lax.axis_size("col"), lax.axis_size("row")
    n_pair = n_col // 2
    rows_dev = row_perm.shape[0]
    patch_count = patch_rows.shape[0]
    width = rows_dev * n_row // n_col
    cell = near_blocks.shape[-1]
    col = lax.axis_index("col")
    side = col % 2
    info = jnp.stack([side, col, col + 1 - 2 * side]).astype(jnp.int32)

    def swap(x):
        return lax.ppermute(x, "col", [(i, i ^ 1) for i in range(n_col)])

    def across(x, m):
        return lax.ppermute(x, "col", [(i, i ^ (2 * m)) for i in range(n_col)])

    def along(x, s):
        return lax.ppermute(x, "row", [(i, (i + s) % n_row) for i in range(n_row)])

    both = jnp.stack([patch_rows, swap(patch_rows)])
    both = jnp.where(side == 0, both, both[::-1]).reshape(-1)
    patches = [both] + [across(both, m) for m in range(1, n_pair)]
    perms = [row_perm] + [along(row_perm, s) for s in range(1, n_row)]
    sel, arr, rows = make_plan(info, patches, perms, patch_count, width)

    started = start(info, stress, friction_state, direct, CHUNKS)
    keep_first, give_first = started[:CHUNKS], started[CHUNKS:]
    keep_mid, give_mid, base, state_base = mid(
        info, stress, friction_state, direct, evolve, relax_rate, load_rate, CHUNKS
    )
    recv_mid = swap(give_mid)
    m_own = build_matrix(
        rows,
        arr,
        near_cols.reshape(-1),
        far_cols.reshape(-1),
        far_ranks.reshape(-1),
        near_blocks,
        far_left,
        far_right,
        n_pair,
    )
    m_sib = swap(m_own)

    def traction_parts(vel_b):
        sources = [vel_b] + [across(vel_b, m) for m in range(1, n_pair)]
        chosen = pick(sel, sources, cell)
        pieces = [chosen] + [along(chosen, s) for s in range(1, n_row)]
        partial = apply_matrix(m_own, m_sib, pieces)
        return [partial[0]] + [across(partial[m], m) for m in range(1, n_pair)]

    keeps, recvs, vel_keeps, vel_recvs = [], [], [], []
    for j in range(CHUNKS):
        vel_b = merge(info, keep_first[j], swap(give_first[j]))
        parts = traction_parts(vel_b)
        first, vel_b, vel_keep, vel_give = second(info, keep_mid, recv_mid, parts, j)
        vel_keeps.append(vel_keep)
        vel_recvs.append(swap(vel_give))
        parts = traction_parts(vel_b)
        keep, give = weigh(info, first, parts)
        keeps.append(keep)
        recvs.append(swap(give))
    state_next = finish(info, state_base, relax_rate, vel_keeps, vel_recvs)
    stress_next = finish(info, base, None, keeps, recvs)
    return (stress_next, state_next)


def solution(mesh):
    cells = P(("row", "col"), None)
    placed = (
        cells,
        cells,
        cells,
        cells,
        cells,
        cells,
        P("row"),
        P(("row", "col")),
        P("row", "col", None),
        P("row", "col", None, None, None),
        P("row", "col", None),
        P("row", "col", None),
        P("row", "col", None, None, None),
        P("row", "col", None, None, None),
    )
    return jax.shard_map(
        shards,
        mesh=mesh,
        in_specs=placed,
        out_specs=(cells, cells),
        check_vma=False,
    )
```

time: 446 us -> 209 us (0.47)
  waiting for transfers between devices: 250 us -> 90.7 us
  local copies, waits for them, and re-layouts: 103 us -> 18.7 us
  Pallas kernels: 0 us -> 60.7 us
  matrix products: 47.3 us -> 0 us
  starting transfers between devices: 0.43 us -> 34.7 us
  blocking collectives: 17.7 us -> 0 us
  between operations: 15.6 us -> 0.86 us
  other arithmetic: 10.5 us -> 1.98 us
    psum x2 -> x0, waiting for transfers between devices: 161 us -> none  [traction_of(): summed = lax.psum(partial_value, 'col')]
    ppermute x0 -> x30, waiting for transfers between devices: none -> 90.7 us  [the longest x9 43.9 us: along(): return lax.ppermute(x, 'row', [(i, (i + s) % n_row) for i in range(n_row)])]
    all_gather x4 -> x0, waiting for transfers between devices: 89 us -> none  [the longest x2 45.1 us: traction_of(): lax.all_gather(mine_vals, 'row', axis=0, tiled=True)]
    gather x13 -> x0, local copies, waits for them, and re-layouts: 87.3 us -> none  [the longest x4 56.6 us: traction_of(): near_x = in_group[safe_near] * live_mask]
    pallas_call x0 -> x13, Pallas kernels: none -> 60.7 us  [the longest x2 19.6 us: pick(): pl.pallas_call(functools.partial(pick_kernel, pair_patches, cell), out_sh...]
    dot_general x4 -> x0, matrix products: 47.3 us -> none  [the longest x2 24.7 us: traction_of(): jnp.einsum('ikab,ikbe->iae', blocks_near, near_x, preferred_element_type=...]
    ppermute x0 -> x30, starting transfers between devices: none -> 34.7 us  [the longest x15 18.4 us: across(): return lax.ppermute(x, 'col', [(i, i ^ 2 * m) for i in range(n_col)])]
    unnamed x2 -> x0, blocking collectives: 17.7 us -> none
  transfers between devices with their start and end apart: 6 -> 30, of which waited for: 6 -> 17; matrix products, arithmetic and copies ran while one was open for 2% -> 2% of each run, Pallas kernels for 0% -> 13%
where the time goes in v1:
time: 209 us; the launch traced here: 208 us
  waiting for transfers between devices  90.7 us (43%)
  Pallas kernels  60.7 us (29%)
  starting transfers between devices  34.7 us (17%)
  local copies, waits for them, and re-layouts  18.7 us (9%)
    ppermute x9, waiting for transfers between devices, along(): return lax.ppermute(x, 'row', [(i, (i + s) % n_row) for i in range(n_row)])  43.9 us
    ppermute x15, waiting for transfers between devices, across(): return lax.ppermute(x, 'col', [(i, i ^ 2 * m) for i in range(n_col)])  41.9 us
    pallas_call x2, Pallas kernels, pick(): pl.pallas_call(functools.partial(pick_kernel, pair_patches, cell), out_sh...  19.6 us
    ppermute x15, starting transfers between devices, across(): return lax.ppermute(x, 'col', [(i, i ^ 2 * m) for i in range(n_col)])  18.4 us
    unnamed x69, local copies, waits for them, and re-layouts  18.3 us
    ppermute x9, starting transfers between devices, along(): return lax.ppermute(x, 'row', [(i, (i + s) % n_row) for i in range(n_row)])  15.8 us
    pallas_call x2, Pallas kernels, apply_matrix(): pl.pallas_call(functools.partial(apply_kernel, n_pair, len(pieces)), out_...  11.2 us
    pallas_call x1, Pallas kernels, build_matrix(): pl.pallas_call(build_kernel, out_shape=struct((n_pair, per * cell, depth)...  10.7 us
  transfers between devices with their start and end apart: 30, of which 17 were waited for; matrix products, arithmetic and copies ran while one was open for 2% of the time, Pallas kernels for 13%

profile of v1, /device:TPU:0, one launch (start us, length us, event | category | flops | bytes accessed | tf_op | source)
XLA Modules:
  0.0 207.7 jit_solution(2844176981919018218)
XLA Ops:
  0.6 4.1 %collective-permute-start.6 = (s32[16]{0:T(128)}, s32[16]{0:T(128)S(1)}, u32[]{:S(2)}, u32[]{:S(2)}) collective-permute-start(s32[16]{0:T(128)} %refs_5_.1), channel_id=1, source_target_pairs={{0,16},{8,24},{16,0},{24,8},{1,17},{9,25},{17,1},{25,9},{2,18},{10... | collective-permute-start | bytes 200 | tf_op jit(solution)/shard_map/ppermute | solution.py:443
  6.3 2.2 %collective-permute-start.7 = (s32[16]{0:T(128)}, s32[16]{0:T(128)S(1)}, u32[]{:S(2)}, u32[]{:S(2)}) collective-permute-start(s32[16]{0:T(128)} %refs_5_.1), channel_id=1, source_target_pairs={{0,24},{8,0},{16,8},{24,16},{1,25},{9,1},{17,9},{25,17},{2,26},{10... | collective-permute-start | bytes 200 | tf_op jit(solution)/shard_map/ppermute | solution.py:443
  13.2 2.4 %collective-permute-start.4 = (s32[4]{0:T(128)S(1)}, s32[4]{0:T(128)S(1)}, u32[]{:S(2)}, u32[]{:S(2)}) collective-permute-start(s32[4]{0:T(128)S(1)} %reshape.16.refs_1_), channel_id=1, source_target_pairs={{0,6},{1,7},{2,4},{3,5},{4,2},{5,3},{6,0},{7,1},{8,14},{9,15},{10,... | collective-permute-start | bytes 56 | tf_op jit(solution)/shard_map/ppermute | solution.py:440
  19.2 2.0 collective-permute-done.2.refs_2_
  22.3 2.4 %plan.1 = (s32[4]{0:T(128)}, s32[8]{0:T(128)}, s32[16]{0:T(128)}) custom-call(s32[3]{0:T(128)} %pad_add_fusion.1.info.refs_0_, s32[4]{0:T(128)} %copy-done.28, s32[4]{0:T(128)} %copy-done.31, s32[4]{0:T(128)} %copy-done.30, s32[4]{0:T(128)} %copy-done.29, s32[16]{0:T(128)} %refs_5_.1, s32[16]{0:T(128)} %copy-done.26, s32[16]{0:T(128)} %copy-done.25, ...), custom_call_target="tpu_custom_call" | custom-call | flops 1000 | bytes 1000 | tf_op jit(solution)/shard_map/plan/pallas_call | solution.py:82
  24.7 2.0 copy-done
  30.5 10.7 %build_matrix.1.m_own = bf16[4,512,1024]{2,1,0:T(8,128)(2,1)} custom-call(s32[16]{0:T(128)S(1)} %copy-done.8, s32[8]{0:T(128)S(1)} %copy-done.7, s32[112]{0:T(128)S(1)} %reshape.17.near_cols, s32[144]{0:T(256)S(1)} %reshape.18.far_cols, s32[144]{0:T(256)S(1)} %reshape.19.far_ranks, bf16[16,1,7,128,128]{4,3,2,1,0:T(8,128)(2,1)S(1)} %copy-done, ...), custom_call_target="tpu_custom_call" | custom-call | flops 1207959552 | bytes 10223616 | tf_op jit(solution)/shard_map/build_matrix/pallas_call | solution.py:133
  41.2 2.1 %start.1 = (bf16[256,256]{1,0:T(8,128)(2,1)}, bf16[256,256]{1,0:T(8,128)(2,1)}) custom-call(s32[3]{0:T(128)} %pad_add_fusion.1.info.refs_0_, f32[256,512]{1,0:T(8,128)} %stress.3, f32[256,512]{1,0:T(8,128)} %state.3, f32[256,512]{1,0:T(8,128)} %direct.3), custom_call_target="tpu_custom_call" | custom-call | flops 1310720 | bytes 1835008 | tf_op jit(solution)/shard_map/start/pallas_call | solution.py:250
  43.8 4.9 %collective-permute-done.9.recv = bf16[256,256]{1,0:T(8,128)(2,1)S(1)} collective-permute-done((bf16[256,256]{1,0:T(8,128)(2,1)}, bf16[256,256]{1,0:T(8,128)(2,1)S(1)}, u32[]{:S(2)}, u32[]{:S(2)}) %collective-permute-start.9) | collective-permute-done | bytes 131104 | tf_op jit(solution)/shard_map/ppermute | solution.py:437
  51.1 2.4 %collective-permute-start.12 = (bf16[512,256]{1,0:T(8,128)(2,1)}, bf16[512,256]{1,0:T(8,128)(2,1)S(1)}, u32[]{:S(2)}, u32[]{:S(2)}) collective-permute-start(bf16[512,256]{1,0:T(8,128)(2,1)} %merge.1.refs_0_), channel_id=1, source_target_pairs={{0,6},{1,7},{2,4},{3,5},{4,2},{5,3},{6,0},{7,1},{8,14},{9,15},{10,... | collective-permute-start | bytes 786440 | tf_op jit(solution)/shard_map/ppermute | solution.py:440
  54.6 3.3 %mid.1 = (f32[1,3,256,256]{3,2,1,0:T(8,128)}, f32[1,3,256,256]{3,2,1,0:T(8,128)}, f32[256,512]{1,0:T(8,128)}, f32[256,512]{1,0:T(8,128)}) custom-call(s32[3]{0:T(128)} %pad_add_fusion.1.info.refs_0_, f32[256,512]{1,0:T(8,128)} %stress.3, f32[256,512]{1,0:T(8,128)} %state.3, f32[256,512]{1,0:T(8,128)} %direct.3, f32[256,512]{1,0:T(8,128)} %evolve.1, ...), custom_call_target="tpu_custom_call" | custom-call | flops 2621440 | bytes 5767168 | tf_op jit(solution)/shard_map/mid/pallas_call | solution.py:289
  57.9 3.5 %collective-permute-done.12.refs_3_ = bf16[512,256]{1,0:T(8,128)(2,1)S(1)} collective-permute-done((bf16[512,256]{1,0:T(8,128)(2,1)}, bf16[512,256]{1,0:T(8,128)(2,1)S(1)}, u32[]{:S(2)}, u32[]{:S(2)}) %collective-permute-start.12) | collective-permute-done | bytes 262176 | tf_op jit(solution)/shard_map/ppermute | solution.py:440
  61.4 4.8 %collective-permute-done.11.refs_2_ = bf16[512,256]{1,0:T(8,128)(2,1)S(1)} collective-permute-done((bf16[512,256]{1,0:T(8,128)(2,1)}, bf16[512,256]{1,0:T(8,128)(2,1)S(1)}, u32[]{:S(2)}, u32[]{:S(2)}) %collective-permute-start.11) | collective-permute-done | bytes 262176 | tf_op jit(solution)/shard_map/ppermute | solution.py:440
  66.9 9.7 %pick.2.refs_0_ = bf16[512,256]{1,0:T(8,128)(2,1)} custom-call(s32[4]{0:T(128)} %get-tuple-element.30.sel, bf16[512,256]{1,0:T(8,128)(2,1)} %merge.1.refs_0_, bf16[512,256]{1,0:T(8,128)(2,1)} %copy-done.16, bf16[512,256]{1,0:T(8,128)(2,1)} %copy-done.15, bf16[512,256]{1,0:T(8,128)(2,1)} %copy-done.13), custom_call_target="tpu_custom_call" | custom-call | bytes 524288 | tf_op jit(solution)/shard_map/pick/pallas_call | solution.py:180
  78.8 6.6 %collective-permute-done.15.refs_3_ = bf16[512,256]{1,0:T(8,128)(2,1)S(1)} collective-permute-done((bf16[512,256]{1,0:T(8,128)(2,1)}, bf16[512,256]{1,0:T(8,128)(2,1)S(1)}, u32[]{:S(2)}, u32[]{:S(2)}) %collective-permute-start.15) | collective-permute-done | bytes 262176 | tf_op jit(solution)/shard_map/ppermute | solution.py:443
  85.4 15.8 %collective-permute-done.14.refs_2_ = bf16[512,256]{1,0:T(8,128)(2,1)S(1)} collective-permute-done((bf16[512,256]{1,0:T(8,128)(2,1)}, bf16[512,256]{1,0:T(8,128)(2,1)S(1)}, u32[]{:S(2)}, u32[]{:S(2)}) %collective-permute-start.14) | collective-permute-done | bytes 262176 | tf_op jit(solution)/shard_map/ppermute | solution.py:443
  102.2 5.6 %apply_matrix.2 = (f32[512,256]{1,0:T(8,128)S(1)}, bf16[512,256]{1,0:T(8,128)(2,1)S(1)}, bf16[512,256]{1,0:T(8,128)(2,1)S(1)}, bf16[512,256]{1,0:T(8,128)(2,1)S(1)}) custom-call(bf16[4,512,1024]{2,1,0:T(8,128)(2,1)} %build_matrix.1.m_own, bf16[4,512,1024]{2,1,0:T(8,128)(2,1)} %collective-permute-done.8.m_sib, bf16[512,256]{1,0:T(8,128)(2,1)S(1)} %copy-done.3, ...), custom_call_target="tpu_custom_call" | custom-call | flops 2147483648 | bytes 8388608 | tf_op jit(solution)/shard_map/apply_matrix/pallas_call | solution.py:218
  112.0 5.8 %collective-permute-done.16.refs_1_ = bf16[512,256]{1,0:T(8,128)(2,1)S(1)} collective-permute-done((bf16[512,256]{1,0:T(8,128)(2,1)S(1)}, bf16[512,256]{1,0:T(8,128)(2,1)S(1)}, u32[]{:S(2)}, u32[]{:S(2)}) %collective-permute-start.16) | collective-permute-done | bytes 262176 | tf_op jit(solution)/shard_map/ppermute | solution.py:440
  117.8 4.9 %collective-permute-done.17.refs_2_ = bf16[512,256]{1,0:T(8,128)(2,1)S(1)} collective-permute-done((bf16[512,256]{1,0:T(8,128)(2,1)S(1)}, bf16[512,256]{1,0:T(8,128)(2,1)S(1)}, u32[]{:S(2)}, u32[]{:S(2)}) %collective-permute-start.17) | collective-permute-done | bytes 262176 | tf_op jit(solution)/shard_map/ppermute | solution.py:440
  123.5 3.1 %second.1 = (f32[512,256]{1,0:T(8,128)}, bf16[512,256]{1,0:T(8,128)(2,1)}, f32[256,256]{1,0:T(8,128)}, f32[256,256]{1,0:T(8,128)}) custom-call(s32[3]{0:T(128)} %pad_add_fusion.1.info.refs_0_, f32[1,3,256,256]{3,2,1,0:T(8,128)} %get-tuple-element.26.keep, f32[1,3,256,256]{3,2,1,0:T(8,128)} %copy-done.9, f32[512,256]{1,0:T(8,128)} %copy-done.5, ...), custom_call_target="tpu_custom_call" | custom-call | flops 1310720 | bytes 5242880 | tf_op jit(solution)/shard_map/second/pallas_call | solution.py:342
  130.1 6.8 %collective-permute-done.21.refs_3_ = bf16[512,256]{1,0:T(8,128)(2,1)S(1)} collective-permute-done((bf16[512,256]{1,0:T(8,128)(2,1)}, bf16[512,256]{1,0:T(8,128)(2,1)S(1)}, u32[]{:S(2)}, u32[]{:S(2)}) %collective-permute-start.21) | collective-permute-done | bytes 262176 | tf_op jit(solution)/shard_map/ppermute | solution.py:440
  136.9 2.8 %collective-permute-done.20.refs_2_ = bf16[512,256]{1,0:T(8,128)(2,1)S(1)} collective-permute-done((bf16[512,256]{1,0:T(8,128)(2,1)}, bf16[512,256]{1,0:T(8,128)(2,1)S(1)}, u32[]{:S(2)}, u32[]{:S(2)}) %collective-permute-start.20) | collective-permute-done | bytes 262176 | tf_op jit(solution)/shard_map/ppermute | solution.py:440
  141.1 9.9 %pick.3.refs_0_ = bf16[512,256]{1,0:T(8,128)(2,1)} custom-call(s32[4]{0:T(128)} %get-tuple-element.30.sel, bf16[512,256]{1,0:T(8,128)(2,1)} %get-tuple-element.38.refs_0_, bf16[512,256]{1,0:T(8,128)(2,1)} %copy-done.19, bf16[512,256]{1,0:T(8,128)(2,1)} %copy-done.18, bf16[512,256]{1,0:T(8,128)(2,1)} %copy-done.17), custom_call_target="tpu_custom_call" | custom-call | bytes 524288 | tf_op jit(solution)/shard_map/pick/pallas_call | solution.py:180
  151.0 3.8 %collective-permute-start.23 = (bf16[512,256]{1,0:T(8,128)(2,1)}, bf16[512,256]{1,0:T(8,128)(2,1)S(1)}, u32[]{:S(2)}, u32[]{:S(2)}) collective-permute-start(bf16[512,256]{1,0:T(8,128)(2,1)} %pick.3.refs_0_), channel_id=1, source_target_pairs={{0,16},{8,24},{16,0},{24,8},{1,17},{9,25},{17,1},{25,9},{2,18},{10... | collective-permute-start | bytes 786440 | tf_op jit(solution)/shard_map/ppermute | solution.py:443
  156.7 2.9 %collective-permute-done.24.refs_3_ = bf16[512,256]{1,0:T(8,128)(2,1)S(1)} collective-permute-done((bf16[512,256]{1,0:T(8,128)(2,1)}, bf16[512,256]{1,0:T(8,128)(2,1)S(1)}, u32[]{:S(2)}, u32[]{:S(2)}) %collective-permute-start.24) | collective-permute-done | bytes 262176 | tf_op jit(solution)/shard_map/ppermute | solution.py:443
  159.6 18.7 %collective-permute-done.23.refs_2_ = bf16[512,256]{1,0:T(8,128)(2,1)S(1)} collective-permute-done((bf16[512,256]{1,0:T(8,128)(2,1)}, bf16[512,256]{1,0:T(8,128)(2,1)S(1)}, u32[]{:S(2)}, u32[]{:S(2)}) %collective-permute-start.23) | collective-permute-done | bytes 262176 | tf_op jit(solution)/shard_map/ppermute | solution.py:443
  179.2 5.6 %apply_matrix.3 = (f32[512,256]{1,0:T(8,128)S(1)}, bf16[512,256]{1,0:T(8,128)(2,1)S(1)}, bf16[512,256]{1,0:T(8,128)(2,1)S(1)}, bf16[512,256]{1,0:T(8,128)(2,1)S(1)}) custom-call(bf16[4,512,1024]{2,1,0:T(8,128)(2,1)} %build_matrix.1.m_own, bf16[4,512,1024]{2,1,0:T(8,128)(2,1)} %collective-permute-done.8.m_sib, bf16[512,256]{1,0:T(8,128)(2,1)S(1)} %copy-done.4, ...), custom_call_target="tpu_custom_call" | custom-call | flops 2147483648 | bytes 8388608 | tf_op jit(solution)/shard_map/apply_matrix/pallas_call | solution.py:218
  189.1 5.7 %collective-permute-done.25.refs_1_ = bf16[512,256]{1,0:T(8,128)(2,1)S(1)} collective-permute-done((bf16[512,256]{1,0:T(8,128)(2,1)S(1)}, bf16[512,256]{1,0:T(8,128)(2,1)S(1)}, u32[]{:S(2)}, u32[]{:S(2)}) %collective-permute-start.25) | collective-permute-done | bytes 262176 | tf_op jit(solution)/shard_map/ppermute | solution.py:440
  194.8 3.4 %collective-permute-done.26.refs_2_ = bf16[512,256]{1,0:T(8,128)(2,1)S(1)} collective-permute-done((bf16[512,256]{1,0:T(8,128)(2,1)S(1)}, bf16[512,256]{1,0:T(8,128)(2,1)S(1)}, u32[]{:S(2)}, u32[]{:S(2)}) %collective-permute-start.26) | collective-permute-done | bytes 262176 | tf_op jit(solution)/shard_map/ppermute | solution.py:440
  199.7 2.3 %weigh.1 = (f32[256,256]{1,0:T(8,128)}, f32[256,256]{1,0:T(8,128)}) custom-call(s32[3]{0:T(128)} %pad_add_fusion.1.info.refs_0_, f32[512,256]{1,0:T(8,128)} %get-tuple-element.37.first, f32[512,256]{1,0:T(8,128)} %copy-done.6, bf16[512,256]{1,0:T(8,128)(2,1)} %copy-done.20, bf16[512,256]{1,0:T(8,128)(2,1)} %copy-done.21, bf16[512,256]{1,0:T(8,128)(2,1)} %copy-done.22), custom_call_target="tpu_custom_call" | custom-call | flops 1310720 | bytes 2621440 | tf_op jit(solution)/shard_map/weigh/pallas_call | solution.py:369
  202.7 2.3 %finish.3 = f32[256,512]{1,0:T(8,128)} custom-call(s32[3]{0:T(128)} %pad_add_fusion.1.info.refs_0_, f32[256,512]{1,0:T(8,128)} %get-tuple-element.45.base, f32[256,512]{1,0:T(8,128)} %refs_0_.1, f32[256,256]{1,0:T(8,128)} %get-tuple-element.46.refs_1_, f32[256,256]{1,0:T(8,128)} %copy-done.11), custom_call_target="tpu_custom_call" | custom-call | flops 393216 | bytes 2097152 | tf_op jit(solution)/shard_map/finish/pallas_call | solution.py:400
  205.7 2.0 finish.2
  (118 shorter events, 42.5 us)
Async XLA Ops:
  0.6 20.6 %collective-permute-start.6 = (s32[16]{0:T(128)}, s32[16]{0:T(128)S(1)}, u32[]{:S(2)}, u32[]{:S(2)}) collective-permute-start(s32[16]{0:T(128)} %refs_5_.1), channel_id=1, source_target_pairs={{0,16},{8,24},{16,0},{24,8},{1,17},{9,25},{17,1},{25,9},{2,18},{10... | collective-permute-start | bytes 200 | tf_op jit(solution)/shard_map/ppermute | solution.py:443
  4.7 16.5 %collective-permute-start.5 = (s32[16]{0:T(128)}, s32[16]{0:T(128)S(1)}, u32[]{:S(2)}, u32[]{:S(2)}) collective-permute-start(s32[16]{0:T(128)} %refs_5_.1), channel_id=1, source_target_pairs={{0,8},{8,16},{16,24},{24,0},{1,9},{9,17},{17,25},{25,1},{2,10},{10... | collective-permute-start | bytes 200 | tf_op jit(solution)/shard_map/ppermute | solution.py:443
  6.3 14.9 %collective-permute-start.7 = (s32[16]{0:T(128)}, s32[16]{0:T(128)S(1)}, u32[]{:S(2)}, u32[]{:S(2)}) collective-permute-start(s32[16]{0:T(128)} %refs_5_.1), channel_id=1, source_target_pairs={{0,24},{8,0},{16,8},{24,16},{1,25},{9,1},{17,9},{25,17},{2,26},{10... | collective-permute-start | bytes 200 | tf_op jit(solution)/shard_map/ppermute | solution.py:443
  8.6 3.2 %collective-permute-start.1 = (s32[2]{0:T(128)}, s32[2]{0:T(128)S(1)}, u32[]{:S(2)}, u32[]{:S(2)}) collective-permute-start(s32[2]{0:T(128)} %param.21), channel_id=1, source_target_pairs={{0,1},{1,0},{2,3},{3,2},{4,5},{5,4},{6,7},{7,6},{8,9},{9,8},{10,11... | collective-permute-start | bytes 32 | tf_op jit(solution)/shard_map/ppermute | solution.py:437
  13.2 4.4 %collective-permute-start.4 = (s32[4]{0:T(128)S(1)}, s32[4]{0:T(128)S(1)}, u32[]{:S(2)}, u32[]{:S(2)}) collective-permute-start(s32[4]{0:T(128)S(1)} %reshape.16.refs_1_), channel_id=1, source_target_pairs={{0,6},{1,7},{2,4},{3,5},{4,2},{5,3},{6,0},{7,1},{8,14},{9,15},{10,... | collective-permute-start | bytes 56 | tf_op jit(solution)/shard_map/ppermute | solution.py:440
  15.7 3.5 %collective-permute-start.3 = (s32[4]{0:T(128)S(1)}, s32[4]{0:T(128)S(1)}, u32[]{:S(2)}, u32[]{:S(2)}) collective-permute-start(s32[4]{0:T(128)S(1)} %reshape.16.refs_1_), channel_id=1, source_target_pairs={{0,4},{1,5},{2,6},{3,7},{4,0},{5,1},{6,2},{7,3},{8,12},{9,13},{10,... | collective-permute-start | bytes 56 | tf_op jit(solution)/shard_map/ppermute | solution.py:440
  17.7 3.5 %collective-permute-start.2 = (s32[4]{0:T(128)S(1)}, s32[4]{0:T(128)S(1)}, u32[]{:S(2)}, u32[]{:S(2)}) collective-permute-start(s32[4]{0:T(128)S(1)} %reshape.16.refs_1_), channel_id=1, source_target_pairs={{0,2},{1,3},{2,0},{3,1},{4,6},{5,7},{6,4},{7,5},{8,10},{9,11},{10,... | collective-permute-start | bytes 56 | tf_op jit(solution)/shard_map/ppermute | solution.py:440
  41.2 60.0 %collective-permute-start.8 = (bf16[4,512,1024]{2,1,0:T(8,128)(2,1)}, bf16[4,512,1024]{2,1,0:T(8,128)(2,1)}, u32[]{:S(2)}, u32[]{:S(2)}) collective-permute-start(bf16[4,512,1024]{2,1,0:T(8,128)(2,1)} %build_matrix.1.m_own), channel_id=1, source_target_pairs={{0,1},{1,0},{2,3},{3,2},{4,5},{5,4},{6,7},{7,6},{8,9},{9,8},{10,11... | collective-permute-start | bytes 12582920 | tf_op jit(solution)/shard_map/ppermute | solution.py:437
  43.3 5.4 %collective-permute-start.9 = (bf16[256,256]{1,0:T(8,128)(2,1)}, bf16[256,256]{1,0:T(8,128)(2,1)S(1)}, u32[]{:S(2)}, u32[]{:S(2)}) collective-permute-start(bf16[256,256]{1,0:T(8,128)(2,1)} %get-tuple-element.32), channel_id=1, source_target_pairs={{0,1},{1,0},{2,3},{3,2},{4,5},{5,4},{6,7},{7,6},{8,9},{9,8},{10,11... | collective-permute-start | bytes 393224 | tf_op jit(solution)/shard_map/ppermute | solution.py:437
  51.1 10.3 %collective-permute-start.12 = (bf16[512,256]{1,0:T(8,128)(2,1)}, bf16[512,256]{1,0:T(8,128)(2,1)S(1)}, u32[]{:S(2)}, u32[]{:S(2)}) collective-permute-start(bf16[512,256]{1,0:T(8,128)(2,1)} %merge.1.refs_0_), channel_id=1, source_target_pairs={{0,6},{1,7},{2,4},{3,5},{4,2},{5,3},{6,0},{7,1},{8,14},{9,15},{10,... | collective-permute-start | bytes 786440 | tf_op jit(solution)/shard_map/ppermute | solution.py:440
  53.5 12.7 %collective-permute-start.11 = (bf16[512,256]{1,0:T(8,128)(2,1)}, bf16[512,256]{1,0:T(8,128)(2,1)S(1)}, u32[]{:S(2)}, u32[]{:S(2)}) collective-permute-start(bf16[512,256]{1,0:T(8,128)(2,1)} %merge.1.refs_0_), channel_id=1, source_target_pairs={{0,4},{1,5},{2,6},{3,7},{4,0},{5,1},{6,2},{7,3},{8,12},{9,13},{10,... | collective-permute-start | bytes 786440 | tf_op jit(solution)/shard_map/ppermute | solution.py:440
  54.0 12.1 %collective-permute-start.10 = (bf16[512,256]{1,0:T(8,128)(2,1)}, bf16[512,256]{1,0:T(8,128)(2,1)S(1)}, u32[]{:S(2)}, u32[]{:S(2)}) collective-permute-start(bf16[512,256]{1,0:T(8,128)(2,1)} %merge.1.refs_0_), channel_id=1, source_target_pairs={{0,2},{1,3},{2,0},{3,1},{4,6},{5,7},{6,4},{7,5},{8,10},{9,11},{10,... | collective-permute-start | bytes 786440 | tf_op jit(solution)/shard_map/ppermute | solution.py:440
  57.8 54.2 %collective-permute-start = (f32[1,3,256,256]{3,2,1,0:T(8,128)}, f32[1,3,256,256]{3,2,1,0:T(8,128)S(1)}, u32[]{:S(2)}, u32[]{:S(2)}) collective-permute-start(f32[1,3,256,256]{3,2,1,0:T(8,128)} %get-tuple-element.27), channel_id=1, source_target_pairs={{0,1},{1,0},{2,3},{3,2},{4,5},{5,4},{6,7},{7,6},{8,9},{9,8},{10,11... | collective-permute-start | bytes 2359304 | tf_op jit(solution)/shard_map/ppermute | solution.py:437
  76.7 8.7 %collective-permute-start.15 = (bf16[512,256]{1,0:T(8,128)(2,1)}, bf16[512,256]{1,0:T(8,128)(2,1)S(1)}, u32[]{:S(2)}, u32[]{:S(2)}) collective-permute-start(bf16[512,256]{1,0:T(8,128)(2,1)} %pick.2.refs_0_), channel_id=1, source_target_pairs={{0,24},{8,0},{16,8},{24,16},{1,25},{9,1},{17,9},{25,17},{2,26},{10... | collective-permute-start | bytes 786440 | tf_op jit(solution)/shard_map/ppermute | solution.py:443
  76.9 24.3 %collective-permute-start.14 = (bf16[512,256]{1,0:T(8,128)(2,1)}, bf16[512,256]{1,0:T(8,128)(2,1)S(1)}, u32[]{:S(2)}, u32[]{:S(2)}) collective-permute-start(bf16[512,256]{1,0:T(8,128)(2,1)} %pick.2.refs_0_), channel_id=1, source_target_pairs={{0,16},{8,24},{16,0},{24,8},{1,17},{9,25},{17,1},{25,9},{2,18},{10... | collective-permute-start | bytes 786440 | tf_op jit(solution)/shard_map/ppermute | solution.py:443
  78.0 23.2 %collective-permute-start.13 = (bf16[512,256]{1,0:T(8,128)(2,1)}, bf16[512,256]{1,0:T(8,128)(2,1)S(1)}, u32[]{:S(2)}, u32[]{:S(2)}) collective-permute-start(bf16[512,256]{1,0:T(8,128)(2,1)} %pick.2.refs_0_), channel_id=1, source_target_pairs={{0,8},{8,16},{16,24},{24,0},{1,9},{9,17},{17,25},{25,1},{2,10},{10... | collective-permute-start | bytes 786440 | tf_op jit(solution)/shard_map/ppermute | solution.py:443
  108.6 9.2 %collective-permute-start.16 = (bf16[512,256]{1,0:T(8,128)(2,1)S(1)}, bf16[512,256]{1,0:T(8,128)(2,1)S(1)}, u32[]{:S(2)}, u32[]{:S(2)}) collective-permute-start(bf16[512,256]{1,0:T(8,128)(2,1)S(1)} %get-tuple-element.34), channel_id=1, source_target_pairs={{0,2},{1,3},{2,0},{3,1},{4,6},{5,7},{6,4},{7,5},{8,10},{9,11},{10,... | collective-permute-start | bytes 786440 | tf_op jit(solution)/shard_map/ppermute | solution.py:440
  110.0 12.7 %collective-permute-start.17 = (bf16[512,256]{1,0:T(8,128)(2,1)S(1)}, bf16[512,256]{1,0:T(8,128)(2,1)S(1)}, u32[]{:S(2)}, u32[]{:S(2)}) collective-permute-start(bf16[512,256]{1,0:T(8,128)(2,1)S(1)} %get-tuple-element.35), channel_id=1, source_target_pairs={{0,4},{1,5},{2,6},{3,7},{4,0},{5,1},{6,2},{7,3},{8,12},{9,13},{10,... | collective-permute-start | bytes 786440 | tf_op jit(solution)/shard_map/ppermute | solution.py:440
  110.2 12.5 %collective-permute-start.18 = (bf16[512,256]{1,0:T(8,128)(2,1)S(1)}, bf16[512,256]{1,0:T(8,128)(2,1)S(1)}, u32[]{:S(2)}, u32[]{:S(2)}) collective-permute-start(bf16[512,256]{1,0:T(8,128)(2,1)S(1)} %get-tuple-element.36), channel_id=1, source_target_pairs={{0,6},{1,7},{2,4},{3,5},{4,2},{5,3},{6,0},{7,1},{8,14},{9,15},{10,... | collective-permute-start | bytes 786440 | tf_op jit(solution)/shard_map/ppermute | solution.py:440
  112.0 10.7 %copy-start.9 = (f32[1,3,256,256]{3,2,1,0:T(8,128)}, f32[1,3,256,256]{3,2,1,0:T(8,128)S(1)}, u32[]{:S(2)}) copy-start(f32[1,3,256,256]{3,2,1,0:T(8,128)S(1)} %collective-permute-done.recv) | copy-start | bytes 2359300
  126.7 10.3 %collective-permute-start.21 = (bf16[512,256]{1,0:T(8,128)(2,1)}, bf16[512,256]{1,0:T(8,128)(2,1)S(1)}, u32[]{:S(2)}, u32[]{:S(2)}) collective-permute-start(bf16[512,256]{1,0:T(8,128)(2,1)} %get-tuple-element.38.refs_0_), channel_id=1, source_target_pairs={{0,6},{1,7},{2,4},{3,5},{4,2},{5,3},{6,0},{7,1},{8,14},{9,15},{10,... | collective-permute-start | bytes 786440 | tf_op jit(solution)/shard_map/ppermute | solution.py:440
  128.3 11.4 %collective-permute-start.20 = (bf16[512,256]{1,0:T(8,128)(2,1)}, bf16[512,256]{1,0:T(8,128)(2,1)S(1)}, u32[]{:S(2)}, u32[]{:S(2)}) collective-permute-start(bf16[512,256]{1,0:T(8,128)(2,1)} %get-tuple-element.38.refs_0_), channel_id=1, source_target_pairs={{0,4},{1,5},{2,6},{3,7},{4,0},{5,1},{6,2},{7,3},{8,12},{9,13},{10,... | collective-permute-start | bytes 786440 | tf_op jit(solution)/shard_map/ppermute | solution.py:440
  128.6 11.1 %collective-permute-start.19 = (bf16[512,256]{1,0:T(8,128)(2,1)}, bf16[512,256]{1,0:T(8,128)(2,1)S(1)}, u32[]{:S(2)}, u32[]{:S(2)}) collective-permute-start(bf16[512,256]{1,0:T(8,128)(2,1)} %get-tuple-element.38.refs_0_), channel_id=1, source_target_pairs={{0,2},{1,3},{2,0},{3,1},{4,6},{5,7},{6,4},{7,5},{8,10},{9,11},{10,... | collective-permute-start | bytes 786440 | tf_op jit(solution)/shard_map/ppermute | solution.py:440
  141.1 48.0 %copy-start.32 = (f32[256,256]{1,0:T(8,128)S(1)}, f32[256,256]{1,0:T(8,128)}, u32[]{:S(2)}) copy-start(f32[256,256]{1,0:T(8,128)} %get-tuple-element.47) | copy-start | bytes 786436
  150.9 8.6 %collective-permute-start.24 = (bf16[512,256]{1,0:T(8,128)(2,1)}, bf16[512,256]{1,0:T(8,128)(2,1)S(1)}, u32[]{:S(2)}, u32[]{:S(2)}) collective-permute-start(bf16[512,256]{1,0:T(8,128)(2,1)} %pick.3.refs_0_), channel_id=1, source_target_pairs={{0,24},{8,0},{16,8},{24,16},{1,25},{9,1},{17,9},{25,17},{2,26},{10... | collective-permute-start | bytes 786440 | tf_op jit(solution)/shard_map/ppermute | solution.py:443
  151.0 27.2 %collective-permute-start.23 = (bf16[512,256]{1,0:T(8,128)(2,1)}, bf16[512,256]{1,0:T(8,128)(2,1)S(1)}, u32[]{:S(2)}, u32[]{:S(2)}) collective-permute-start(bf16[512,256]{1,0:T(8,128)(2,1)} %pick.3.refs_0_), channel_id=1, source_target_pairs={{0,16},{8,24},{16,0},{24,8},{1,17},{9,25},{17,1},{25,9},{2,18},{10... | collective-permute-start | bytes 786440 | tf_op jit(solution)/shard_map/ppermute | solution.py:443
  154.8 23.5 %collective-permute-start.22 = (bf16[512,256]{1,0:T(8,128)(2,1)}, bf16[512,256]{1,0:T(8,128)(2,1)S(1)}, u32[]{:S(2)}, u32[]{:S(2)}) collective-permute-start(bf16[512,256]{1,0:T(8,128)(2,1)} %pick.3.refs_0_), channel_id=1, source_target_pairs={{0,8},{8,16},{16,24},{24,0},{1,9},{9,17},{17,25},{25,1},{2,10},{10... | collective-permute-start | bytes 786440 | tf_op jit(solution)/shard_map/ppermute | solution.py:443
  185.6 9.2 %collective-permute-start.25 = (bf16[512,256]{1,0:T(8,128)(2,1)S(1)}, bf16[512,256]{1,0:T(8,128)(2,1)S(1)}, u32[]{:S(2)}, u32[]{:S(2)}) collective-permute-start(bf16[512,256]{1,0:T(8,128)(2,1)S(1)} %get-tuple-element.40), channel_id=1, source_target_pairs={{0,2},{1,3},{2,0},{3,1},{4,6},{5,7},{6,4},{7,5},{8,10},{9,11},{10,... | collective-permute-start | bytes 786440 | tf_op jit(solution)/shard_map/ppermute | solution.py:440
  185.9 12.4 %collective-permute-start.26 = (bf16[512,256]{1,0:T(8,128)(2,1)S(1)}, bf16[512,256]{1,0:T(8,128)(2,1)S(1)}, u32[]{:S(2)}, u32[]{:S(2)}) collective-permute-start(bf16[512,256]{1,0:T(8,128)(2,1)S(1)} %get-tuple-element.41), channel_id=1, source_target_pairs={{0,4},{1,5},{2,6},{3,7},{4,0},{5,1},{6,2},{7,3},{8,12},{9,13},{10,... | collective-permute-start | bytes 786440 | tf_op jit(solution)/shard_map/ppermute | solution.py:440
  187.7 11.3 %collective-permute-start.27 = (bf16[512,256]{1,0:T(8,128)(2,1)S(1)}, bf16[512,256]{1,0:T(8,128)(2,1)S(1)}, u32[]{:S(2)}, u32[]{:S(2)}) collective-permute-start(bf16[512,256]{1,0:T(8,128)(2,1)S(1)} %get-tuple-element.42), channel_id=1, source_target_pairs={{0,6},{1,7},{2,4},{3,5},{4,2},{5,3},{6,0},{7,1},{8,14},{9,15},{10,... | collective-permute-start | bytes 786440 | tf_op jit(solution)/shard_map/ppermute | solution.py:440
  189.1 12.9 %collective-permute-start.29 = (f32[256,256]{1,0:T(8,128)S(1)}, f32[256,256]{1,0:T(8,128)S(1)}, u32[]{:S(2)}, u32[]{:S(2)}) collective-permute-start(f32[256,256]{1,0:T(8,128)S(1)} %copy-done.32), channel_id=1, source_target_pairs={{0,1},{1,0},{2,3},{3,2},{4,5},{5,4},{6,7},{7,6},{8,9},{9,8},{10,11... | collective-permute-start | bytes 786440 | tf_op jit(solution)/shard_map/ppermute | solution.py:437
  202.0 3.0 %collective-permute-start.28 = (f32[256,256]{1,0:T(8,128)}, f32[256,256]{1,0:T(8,128)S(1)}, u32[]{:S(2)}, u32[]{:S(2)}) collective-permute-start(f32[256,256]{1,0:T(8,128)} %get-tuple-element.44), channel_id=1, source_target_pairs={{0,1},{1,0},{2,3},{3,2},{4,5},{5,4},{6,7},{7,6},{8,9},{9,8},{10,11... | collective-permute-start | bytes 786440 | tf_op jit(solution)/shard_map/ppermute | solution.py:437
  (31 other events, 49.6 us)

commit v2 on v1

--- a/solution.py
+++ b/solution.py
@@ -21,7 +21,7 @@
 VMEM = pl.BlockSpec(memory_space=pltpu.VMEM)
 SMEM = pl.BlockSpec(memory_space=pltpu.SMEM)
 ANY = pl.BlockSpec(memory_space=pl.ANY)
-LIMIT = 40 * 1024 * 1024
+LIMIT = 16 * 1024 * 1024
 
 
 def params(limit=LIMIT):
@@ -37,26 +37,27 @@
 
 
 def plan_kernel(n_pair, n_row, patch_count, width, *refs):
-    info = refs[0]
-    patches = refs[1 : 1 + n_pair]
-    perms = refs[1 + n_pair : 1 + n_pair + n_row]
-    sel, arr, rows, inv = refs[1 + n_pair + n_row :]
+    patches = refs[:n_pair]
+    perms = refs[n_pair : n_pair + n_row]
+    sel, arr, rows, inv = refs[n_pair + n_row :]
     pair_patches = 2 * patch_count
     rows_dev = perms[0].shape[0]
+    col = lax.axis_index("col")
+    side = lax.rem(col, 2)
+    groups = (col, col + 1 - 2 * side)
     for m in range(n_pair):
         for i in range(pair_patches):
-            q = patches[m][i]
+            q = patches[m][lax.rem(i + side * patch_count, pair_patches)]
             inv[q] = m * pair_patches + i
             rows[m * pair_patches + i] = q
-    for side in range(2):
-        group = info[1 + side]
-
-        def pick(q, count):
+    for n, group in enumerate(groups):
+
+        def pick(q, count, n=n, group=group):
             hit = lax.div(perms[0][q], width) == group
 
             @pl.when(hit)
             def _():
-                sel[side * patch_count + count] = inv[q]
+                sel[n * patch_count + count] = inv[q]
 
             return count + hit.astype(jnp.int32)
 
@@ -65,7 +66,7 @@
 
         def place(q, count):
             block = perms[s][q]
-            hit = lax.div(block, width) == info[1]
+            hit = lax.div(block, width) == groups[0]
 
             @pl.when(hit)
             def _():
@@ -76,7 +77,7 @@
         lax.fori_loop(0, rows_dev, place, jnp.int32(0))
 
 
-def make_plan(info, patches, perms, patch_count, width):
+def make_plan(patches, perms, patch_count, width):
     n_pair, n_row = len(patches), len(perms)
     rows_dev = perms[0].shape[0]
     return pl.pallas_call(
@@ -86,12 +87,13 @@
             struct((width,), jnp.int32),
             struct((rows_dev,), jnp.int32),
         ),
-        in_specs=[SMEM] * (1 + n_pair + n_row),
+        in_specs=[SMEM] * (n_pair + n_row),
         out_specs=(SMEM,) * 3,
         scratch_shapes=[pltpu.SMEM((rows_dev,), jnp.int32)],
+        compiler_params=params(),
         cost_estimate=cost(1000, 1000),
         name="plan",
-    )(info, *patches, *perms)
+    )(*patches, *perms)
 
 
 def build_kernel(rows, arr, near_cols, far_cols, far_ranks, near, left, right, out, spread, acc):
@@ -147,7 +149,7 @@
                 pltpu.VMEM((cell, depth), F32),
             ],
         ),
-        compiler_params=params(),
+        compiler_params=params(56 * 1024 * 1024),
         cost_estimate=cost(
             2 * rows_dev * cell * far_slots * rank * depth, 2 * (near.size + left.size + right.size) + 2 * rows_dev * cell * depth
         ),
@@ -156,23 +158,15 @@
 
 
 def pick_kernel(pair_patches, cell, sel, *refs):
-    n_pair = len(refs) - 2
-    sources, out, sems = refs[:n_pair], refs[n_pair], refs[n_pair + 1]
+    sources, out = refs[:-1], refs[-1]
     for t in range(pair_patches):
         which = lax.div(sel[t], pair_patches)
         block = pl.multiple_of(lax.rem(sel[t], pair_patches) * cell, cell)
-        for m in range(n_pair):
+        for m, source in enumerate(sources):
 
             @pl.when(which == m)
             def _():
-                pltpu.make_async_copy(
-                    sources[m].at[pl.ds(block, cell)], out.at[pl.ds(t * cell, cell)], sems.at[t]
-                ).start()
-
-    for t in range(pair_patches):
-        pltpu.make_async_copy(
-            sources[0].at[pl.ds(0, cell)], out.at[pl.ds(t * cell, cell)], sems.at[t]
-        ).wait()
+                out[pl.ds(t * cell, cell)] = source[pl.ds(block, cell)]
 
 
 def pick(sel, sources, cell):
@@ -180,9 +174,9 @@
     return pl.pallas_call(
         functools.partial(pick_kernel, pair_patches, cell),
         out_shape=struct(sources[0].shape, BF16),
-        in_specs=[SMEM] + [ANY] * len(sources),
-        out_specs=ANY,
-        scratch_shapes=[pltpu.SemaphoreType.DMA((pair_patches,))],
+        in_specs=[SMEM] + [VMEM] * len(sources),
+        out_specs=VMEM,
+        compiler_params=params(),
         cost_estimate=cost(0, 4 * sources[0].size),
         name="pick",
     )(sel, *sources)
@@ -228,11 +222,11 @@
     )(m_own, m_sib, *pieces)
 
 
-def start_kernel(chunks, info, stress, state, direct, *outs):
+def start_kernel(chunks, stress, state, direct, *outs):
     keep, give = outs[:chunks], outs[chunks:]
     half = stress.shape[1] // 2
     lanes = half // chunks
-    side = info[0]
+    side = lax.rem(lax.axis_index("col"), 2)
     for own, refs in ((False, give), (True, keep)):
         base = (side if own else 1 - side) * half
         for j in range(chunks):
@@ -243,7 +237,7 @@
             refs[j][...] = velocity.astype(BF16)
 
 
-def start(info, stress, state, direct, chunks):
+def start(stress, state, direct, chunks):
     high, members = stress.shape
     lanes = members // 2 // chunks
     tile = 128
@@ -251,17 +245,18 @@
         functools.partial(start_kernel, chunks),
         out_shape=(struct((high, lanes), BF16),) * (2 * chunks),
         grid=(high // tile,),
-        in_specs=[SMEM] + [pl.BlockSpec((tile, members), lambda i: (i, 0))] * 3,
+        in_specs=[pl.BlockSpec((tile, members), lambda i: (i, 0))] * 3,
         out_specs=(pl.BlockSpec((tile, lanes), lambda i: (i, 0)),) * (2 * chunks),
+        compiler_params=params(),
         cost_estimate=cost(10 * stress.size, 14 * stress.size, 3 * stress.size),
         name="start",
-    )(info, stress, state, direct)
-
-
-def mid_kernel(chunks, info, stress, state, direct, evolve, relax, load, keep, give, base, state_base):
+    )(stress, state, direct)
+
+
+def mid_kernel(chunks, stress, state, direct, evolve, relax, load, keep, give, base, state_base):
     half = stress.shape[1] // 2
     lanes = half // chunks
-    side = info[0]
+    side = lax.rem(lax.axis_index("col"), 2)
     for own, ref in ((True, keep), (False, give)):
         first = (side if own else 1 - side) * half
         for j in range(chunks):
@@ -280,7 +275,7 @@
             state_base[:, at] = state_now + W1 * state_rate + W2 * relax_now * jnp.exp(-state_mid * inverse_e)
 
 
-def mid(info, stress, state, direct, evolve, relax, load, chunks):
+def mid(stress, state, direct, evolve, relax, load, chunks):
     high, members = stress.shape
     lanes = members // 2 // chunks
     tile = 128
@@ -290,38 +285,40 @@
         functools.partial(mid_kernel, chunks),
         out_shape=(struct((chunks, 3, high, lanes), F32),) * 2 + (struct(stress.shape, F32),) * 2,
         grid=(high // tile,),
-        in_specs=[SMEM] + [wide] * 6,
+        in_specs=[wide] * 6,
         out_specs=(split, split, wide, wide),
+        compiler_params=params(),
         cost_estimate=cost(20 * stress.size, 44 * stress.size, 6 * stress.size),
         name="mid",
-    )(info, stress, state, direct, evolve, relax, load)
-
-
-def merge_kernel(info, keep, recv, out):
+    )(stress, state, direct, evolve, relax, load)
+
+
+def merge_kernel(keep, recv, out):
     high = keep.shape[0]
-    side = info[0]
+    side = lax.rem(lax.axis_index("col"), 2)
     out[pl.ds(pl.multiple_of(side * high, high), high)] = keep[...]
     out[pl.ds(pl.multiple_of((1 - side) * high, high), high)] = recv[...]
 
 
-def merge(info, keep, recv):
+def merge(keep, recv):
     high, lanes = keep.shape
     return pl.pallas_call(
         merge_kernel,
         out_shape=struct((2 * high, lanes), keep.dtype),
-        in_specs=[SMEM, VMEM, VMEM],
+        in_specs=[VMEM, VMEM],
         out_specs=VMEM,
+        compiler_params=params(),
         cost_estimate=cost(0, 8 * keep.size),
         name="merge",
-    )(info, keep, recv)
-
-
-def second_kernel(info, keep, recv, *refs):
+    )(keep, recv)
+
+
+def second_kernel(keep, recv, *refs):
     n_pair = len(refs) - 4
     parts = refs[:n_pair]
     total_out, vel_b, vel_keep, vel_give = refs[n_pair:]
     high = keep.shape[2]
-    side = info[0]
+    side = lax.rem(lax.axis_index("col"), 2)
     for own, held, vel_out in ((True, keep, vel_keep), (False, recv, vel_give)):
         at = pl.ds(pl.multiple_of((side if own else 1 - side) * high, high), high)
         total = parts[0][at]
@@ -334,7 +331,7 @@
         vel_out[...] = velocity
 
 
-def second(info, keep, recv, parts, chunk):
+def second(keep, recv, parts, chunk):
     high, lanes = parts[0].shape
     held = pl.BlockSpec((1, 3, high // 2, lanes), lambda i: (chunk, 0, 0, 0))
     whole = pl.BlockSpec((high, lanes), lambda i: (0, 0))
@@ -344,18 +341,19 @@
         out_shape=(struct((high, lanes), F32), struct((high, lanes), BF16))
         + (struct((high // 2, lanes), F32),) * 2,
         grid=(1,),
-        in_specs=[SMEM, held, held] + [whole] * len(parts),
+        in_specs=[held, held] + [whole] * len(parts),
         out_specs=(whole, whole, half, half),
+        compiler_params=params(),
         cost_estimate=cost(10 * high * lanes, 40 * high * lanes, 2 * high * lanes),
         name="second",
-    )(info, keep, recv, *parts)
-
-
-def weigh_kernel(info, first, *refs):
+    )(keep, recv, *parts)
+
+
+def weigh_kernel(first, *refs):
     parts = refs[:-2]
     keep, give = refs[-2:]
     high = keep.shape[0]
-    side = info[0]
+    side = lax.rem(lax.axis_index("col"), 2)
     for own, ref in ((False, give), (True, keep)):
         at = pl.ds(pl.multiple_of((side if own else 1 - side) * high, high), high)
         total = parts[0][at]
@@ -364,25 +362,26 @@
         ref[...] = first[at] + W2 * total
 
 
-def weigh(info, first, parts):
+def weigh(first, parts):
     high, lanes = first.shape
     return pl.pallas_call(
         weigh_kernel,
         out_shape=(struct((high // 2, lanes), F32),) * 2,
-        in_specs=[SMEM] + [VMEM] * (1 + len(parts)),
+        in_specs=[VMEM] * (1 + len(parts)),
         out_specs=(VMEM, VMEM),
+        compiler_params=params(),
         cost_estimate=cost(10 * high * lanes, 20 * high * lanes),
         name="weigh",
-    )(info, first, *parts)
-
-
-def finish_kernel(chunks, scaled, info, base, *refs):
+    )(first, *parts)
+
+
+def finish_kernel(chunks, scaled, base, *refs):
     out = refs[-1]
     factor = refs[0] if scaled else None
     pieces = refs[1:-1] if scaled else refs[:-1]
     half = base.shape[1] // 2
     lanes = half // chunks
-    side = info[0]
+    side = lax.rem(lax.axis_index("col"), 2)
     for j in range(chunks):
         for own, piece in ((True, pieces[j]), (False, pieces[chunks + j])):
             first = (side if own else 1 - side) * half + j * lanes
@@ -393,18 +392,19 @@
             out[:, at] = base[:, at] - change
 
 
-def finish(info, base, factor, keeps, recvs):
+def finish(base, factor, keeps, recvs):
     chunks = len(keeps)
     scaled = factor is not None
     extra = [factor] if scaled else []
     return pl.pallas_call(
         functools.partial(finish_kernel, chunks, scaled),
         out_shape=struct(base.shape, F32),
-        in_specs=[SMEM] + [VMEM] * (1 + len(extra) + 2 * chunks),
+        in_specs=[VMEM] * (1 + len(extra) + 2 * chunks),
         out_specs=VMEM,
+        compiler_params=params(),
         cost_estimate=cost(3 * base.size, 16 * base.size),
         name="finish",
-    )(info, base, *extra, *keeps, *recvs)
+    )(base, *extra, *keeps, *recvs)
 
 
 def shards(
@@ -429,9 +429,9 @@
     patch_count = patch_rows.shape[0]
     width = rows_dev * n_row // n_col
     cell = near_blocks.shape[-1]
-    col = lax.axis_index("col")
-    side = col % 2
-    info = jnp.stack([side, col, col + 1 - 2 * side]).astype(jnp.int32)
+
+    def after(values, dep):
+        return lax.optimization_barrier((values, dep))[0]
 
     def swap(x):
         return lax.ppermute(x, "col", [(i, i ^ 1) for i in range(n_col)])
@@ -442,51 +442,45 @@
     def along(x, s):
         return lax.ppermute(x, "row", [(i, (i + s) % n_row) for i in range(n_row)])
 
-    both = jnp.stack([patch_rows, swap(patch_rows)])
-    both = jnp.where(side == 0, both, both[::-1]).reshape(-1)
+    started = start(stress, friction_state, direct, CHUNKS)
+    keep_first, give_first = started[:CHUNKS], started[CHUNKS:]
+    recv_first = [swap(give) for give in give_first]
+    rows_mine, perm_mine = after((patch_rows, row_perm), give_first[0])
+    both = jnp.concatenate([rows_mine, swap(rows_mine)])
     patches = [both] + [across(both, m) for m in range(1, n_pair)]
-    perms = [row_perm] + [along(row_perm, s) for s in range(1, n_row)]
-    sel, arr, rows = make_plan(info, patches, perms, patch_count, width)
-
-    started = start(info, stress, friction_state, direct, CHUNKS)
-    keep_first, give_first = started[:CHUNKS], started[CHUNKS:]
-    keep_mid, give_mid, base, state_base = mid(
-        info, stress, friction_state, direct, evolve, relax_rate, load_rate, CHUNKS
-    )
-    recv_mid = swap(give_mid)
-    m_own = build_matrix(
-        rows,
-        arr,
-        near_cols.reshape(-1),
-        far_cols.reshape(-1),
-        far_ranks.reshape(-1),
-        near_blocks,
-        far_left,
-        far_right,
-        n_pair,
-    )
+    perms = [perm_mine] + [along(perm_mine, s) for s in range(1, n_row)]
+    sel, arr, rows = make_plan(patches, perms, patch_count, width)
+
+    vel_first = [merge(keep, recv) for keep, recv in zip(keep_first, recv_first)]
+    tables = after((near_cols, far_cols, far_ranks), vel_first[0])
+    m_own = build_matrix(rows, arr, *[t.reshape(-1) for t in tables], near_blocks, far_left, far_right, n_pair)
     m_sib = swap(m_own)
 
-    def traction_parts(vel_b):
+    def route(vel_b):
         sources = [vel_b] + [across(vel_b, m) for m in range(1, n_pair)]
-        chosen = pick(sel, sources, cell)
+        return pick(sel, sources, cell)
+
+    def traction_parts(chosen):
         pieces = [chosen] + [along(chosen, s) for s in range(1, n_row)]
         partial = apply_matrix(m_own, m_sib, pieces)
         return [partial[0]] + [across(partial[m], m) for m in range(1, n_pair)]
 
+    chosen_first = [route(vel_b) for vel_b in vel_first]
+    held = (stress, friction_state, direct, evolve, relax_rate, load_rate)
+    keep_mid, give_mid, base, state_base = mid(*after(held, chosen_first[0]), CHUNKS)
+    recv_mid = swap(give_mid)
     keeps, recvs, vel_keeps, vel_recvs = [], [], [], []
     for j in range(CHUNKS):
-        vel_b = merge(info, keep_first[j], swap(give_first[j]))
-        parts = traction_parts(vel_b)
-        first, vel_b, vel_keep, vel_give = second(info, keep_mid, recv_mid, parts, j)
+        parts = traction_parts(chosen_first[j])
+        first, vel_b, vel_keep, vel_give = second(keep_mid, recv_mid, parts, j)
         vel_keeps.append(vel_keep)
         vel_recvs.append(swap(vel_give))
-        parts = traction_parts(vel_b)
-        keep, give = weigh(info, first, parts)
+        parts = traction_parts(route(vel_b))
+        keep, give = weigh(first, parts)
         keeps.append(keep)
         recvs.append(swap(give))
-    state_next = finish(info, state_base, relax_rate, vel_keeps, vel_recvs)
-    stress_next = finish(info, base, None, keeps, recvs)
+    state_next = finish(state_base, relax_rate, vel_keeps, vel_recvs)
+    stress_next = finish(base, None, keeps, recvs)
     return (stress_next, state_next)
 
 

time: 209 us -> 168 us (0.80)
  Pallas kernels: 60.7 us -> 28.4 us
  local copies, waits for them, and re-layouts: 18.7 us -> 9.07 us
  waiting for transfers between devices: 90.7 us -> 96.4 us
    pallas_call x2, Pallas kernels: 19.6 us -> 1.3 us  [pick(): pl.pallas_call(functools.partial(pick_kernel, pair_patches, cell), out_sh...]
    unnamed x69 -> x26, local copies, waits for them, and re-layouts: 18.3 us -> 4.8 us
    ppermute x15, waiting for transfers between devices: 41.9 us -> 50.2 us  [across(): return lax.ppermute(x, 'col', [(i, i ^ 2 * m) for i in range(n_col)])]
    pallas_call x2, Pallas kernels: 11.2 us -> 6.19 us  [apply_matrix(): pl.pallas_call(functools.partial(apply_kernel, n_pair, len(pieces)), out_...]
    pallas_call x1, Pallas kernels: 10.7 us -> 15.2 us  [build_matrix(): pl.pallas_call(build_kernel, out_shape=struct((n_pair, per * cell, depth)...]
    ppermute x9, starting transfers between devices: 15.8 us -> 12.4 us  [along(): return lax.ppermute(x, 'row', [(i, (i + s) % n_row) for i in range(n_row)])]
    ppermute x6, waiting for transfers between devices: 4.94 us -> 1.87 us  [swap(): return lax.ppermute(x, 'col', [(i, i ^ 1) for i in range(n_col)])]
    pallas_call x1, Pallas kernels: 3.14 us -> 0.32 us  [second(): pl.pallas_call(second_kernel, out_shape=(struct((high, lanes), F32), stru...]
  transfers between devices with their start and end apart: 30 -> 30, of which waited for: 17 -> 18; matrix products, arithmetic and copies ran while one was open for 2% -> 0% of each run, Pallas kernels for 13% -> 5%
where the time goes in v2:
time: 168 us
  waiting for transfers between devices  96.4 us (57%)
  starting transfers between devices  32.8 us (20%)
  Pallas kernels  28.4 us (17%)
  local copies, waits for them, and re-layouts  9.07 us (5%)
    ppermute x15, waiting for transfers between devices, across(): return lax.ppermute(x, 'col', [(i, i ^ 2 * m) for i in range(n_col)])  50.2 us
    ppermute x9, waiting for transfers between devices, along(): return lax.ppermute(x, 'row', [(i, (i + s) % n_row) for i in range(n_row)])  44.3 us
    ppermute x15, starting transfers between devices, across(): return lax.ppermute(x, 'col', [(i, i ^ 2 * m) for i in range(n_col)])  19.7 us
    pallas_call x1, Pallas kernels, build_matrix(): pl.pallas_call(build_kernel, out_shape=struct((n_pair, per * cell, depth)...  15.2 us
    ppermute x9, starting transfers between devices, along(): return lax.ppermute(x, 'row', [(i, (i + s) % n_row) for i in range(n_row)])  12.4 us
    pallas_call x2, Pallas kernels, apply_matrix(): pl.pallas_call(functools.partial(apply_kernel, n_pair, len(pieces)), out_...  6.19 us
    unnamed x26, local copies, waits for them, and re-layouts  4.8 us
  transfers between devices with their start and end apart: 30, of which 18 were waited for; matrix products, arithmetic and copies ran while one was open for 0% of the time, Pallas kernels for 5%

profile of v2, /device:TPU:0, one launch (start us, length us, event | category | flops | bytes accessed | tf_op | source)
XLA Modules:
  0.0 168.3 jit_solution(5930937254978413719)
XLA Ops:
  4.6 4.7 %collective-permute-start.6 = (s32[16]{0:T(128)}, s32[16]{0:T(128)S(1)}, u32[]{:S(2)}, u32[]{:S(2)}) collective-permute-start(s32[16]{0:T(128)} %refs_4_), channel_id=1, source_target_pairs={{0,24},{8,0},{16,8},{24,16},{1,25},{9,1},{17,9},{25,17},{2,26},{10... | collective-permute-start | bytes 200 | tf_op jit(solution)/shard_map/ppermute | solution.py:443
  10.2 1.3 collective-permute-done
  12.2 2.4 %collective-permute-start.3 = (s32[4]{0:T(128)S(1)}, s32[4]{0:T(128)S(1)}, u32[]{:S(2)}, u32[]{:S(2)}) collective-permute-start(s32[4]{0:T(128)S(1)} %pad_add_fusion.refs_0_), channel_id=1, source_target_pairs={{0,6},{1,7},{2,4},{3,5},{4,2},{5,3},{6,0},{7,1},{8,14},{9,15},{10,... | collective-permute-start | bytes 56 | tf_op jit(solution)/shard_map/ppermute | solution.py:440
  14.7 2.0 %collective-permute-done.3.refs_3_ = s32[4]{0:T(128)S(1)} collective-permute-done((s32[4]{0:T(128)S(1)}, s32[4]{0:T(128)S(1)}, u32[]{:S(2)}, u32[]{:S(2)}) %collective-permute-start.3) | collective-permute-done | bytes 48 | tf_op jit(solution)/shard_map/ppermute | solution.py:440
  16.7 1.5 collective-permute-start.2
  18.2 2.0 %collective-permute-done.2.refs_2_ = s32[4]{0:T(128)S(1)} collective-permute-done((s32[4]{0:T(128)S(1)}, s32[4]{0:T(128)S(1)}, u32[]{:S(2)}, u32[]{:S(2)}) %collective-permute-start.2) | collective-permute-done | bytes 48 | tf_op jit(solution)/shard_map/ppermute | solution.py:440
  20.2 1.5 collective-permute-start.1
  21.7 2.0 %collective-permute-done.1.refs_1_ = s32[4]{0:T(128)S(1)} collective-permute-done((s32[4]{0:T(128)S(1)}, s32[4]{0:T(128)S(1)}, u32[]{:S(2)}, u32[]{:S(2)}) %collective-permute-start.1) | collective-permute-done | bytes 48 | tf_op jit(solution)/shard_map/ppermute | solution.py:440
  24.4 2.3 %plan.1 = (s32[4]{0:T(128)S(1)}, s32[8]{0:T(128)S(1)}, s32[16]{0:T(128)S(1)}) custom-call(s32[4]{0:T(128)S(1)} %pad_add_fusion.refs_0_, s32[4]{0:T(128)S(1)} %collective-permute-done.1.refs_1_, s32[4]{0:T(128)S(1)} %collective-permute-done.2.refs_2_, s32[4]{0:T(128)S(1)} %collective-permute-done.3.refs_3_, s32[16]{0:T(128)S(1)} %copy-done.12, ...), custom_call_target="tpu_custom_call" | custom-call | flops 1000 | bytes 1000 | tf_op jit(solution)/shard_map/plan/pallas_call | solution.py:83
  32.1 15.2 %build_matrix.1.m_own = bf16[4,512,1024]{2,1,0:T(8,128)(2,1)} custom-call(s32[16]{0:T(128)} %copy-done.11, s32[8]{0:T(128)} %copy-done.10, s32[112]{0:T(128)} %reshape.13.near_cols, s32[144]{0:T(256)} %reshape.14.far_cols, s32[144]{0:T(256)} %reshape.15.far_ranks, bf16[16,1,7,128,128]{4,3,2,1,0:T(8,128)(2,1)} %near.1, bf16[16,1,9,32,128]{4,3,2,1,0:T(8,128)(2,1)} %left.1, ...), custom_call_target="tpu_custom_call" | custom-call | flops 1207959552 | bytes 10223616 | tf_op jit(solution)/shard_map/build_matrix/pallas_call | solution.py:135
  47.3 2.6 %collective-permute-start.10 = (bf16[512,256]{1,0:T(8,128)(2,1)S(1)}, bf16[512,256]{1,0:T(8,128)(2,1)S(1)}, u32[]{:S(2)}, u32[]{:S(2)}) collective-permute-start(bf16[512,256]{1,0:T(8,128)(2,1)S(1)} %merge.1.refs_0_), channel_id=1, source_target_pairs={{0,6},{1,7},{2,4},{3,5},{4,2},{5,3},{6,0},{7,1},{8,14},{9,15},{10,... | collective-permute-start | bytes 786440 | tf_op jit(solution)/shard_map/ppermute | solution.py:440
  50.9 6.6 %collective-permute-done.10.refs_3_ = bf16[512,256]{1,0:T(8,128)(2,1)S(1)} collective-permute-done((bf16[512,256]{1,0:T(8,128)(2,1)S(1)}, bf16[512,256]{1,0:T(8,128)(2,1)S(1)}, u32[]{:S(2)}, u32[]{:S(2)}) %collective-permute-start.10) | collective-permute-done | bytes 262176 | tf_op jit(solution)/shard_map/ppermute | solution.py:440
  57.4 5.1 %collective-permute-done.9.refs_2_ = bf16[512,256]{1,0:T(8,128)(2,1)S(1)} collective-permute-done((bf16[512,256]{1,0:T(8,128)(2,1)S(1)}, bf16[512,256]{1,0:T(8,128)(2,1)S(1)}, u32[]{:S(2)}, u32[]{:S(2)}) %collective-permute-start.9) | collective-permute-done | bytes 262176 | tf_op jit(solution)/shard_map/ppermute | solution.py:440
  64.4 2.9 %collective-permute-start.15 = (bf16[512,256]{1,0:T(8,128)(2,1)S(1)}, bf16[512,256]{1,0:T(8,128)(2,1)S(1)}, u32[]{:S(2)}, u32[]{:S(2)}) collective-permute-start(bf16[512,256]{1,0:T(8,128)(2,1)S(1)} %pick.2.refs_0_), channel_id=1, source_target_pairs={{0,24},{8,0},{16,8},{24,16},{1,25},{9,1},{17,9},{25,17},{2,26},{10... | collective-permute-start | bytes 786440 | tf_op jit(solution)/shard_map/ppermute | solution.py:443
  68.6 5.4 %collective-permute-done.15.refs_3_ = bf16[512,256]{1,0:T(8,128)(2,1)S(1)} collective-permute-done((bf16[512,256]{1,0:T(8,128)(2,1)S(1)}, bf16[512,256]{1,0:T(8,128)(2,1)S(1)}, u32[]{:S(2)}, u32[]{:S(2)}) %collective-permute-start.15) | collective-permute-done | bytes 262176 | tf_op jit(solution)/shard_map/ppermute | solution.py:443
  74.0 17.9 %collective-permute-done.14.refs_2_ = bf16[512,256]{1,0:T(8,128)(2,1)S(1)} collective-permute-done((bf16[512,256]{1,0:T(8,128)(2,1)S(1)}, bf16[512,256]{1,0:T(8,128)(2,1)S(1)}, u32[]{:S(2)}, u32[]{:S(2)}) %collective-permute-start.14) | collective-permute-done | bytes 262176 | tf_op jit(solution)/shard_map/ppermute | solution.py:443
  91.9 3.1 %apply_matrix.2 = (f32[512,256]{1,0:T(8,128)S(1)}, bf16[512,256]{1,0:T(8,128)(2,1)S(1)}, bf16[512,256]{1,0:T(8,128)(2,1)S(1)}, bf16[512,256]{1,0:T(8,128)(2,1)S(1)}) custom-call(bf16[4,512,1024]{2,1,0:T(8,128)(2,1)S(1)} %copy-done, bf16[4,512,1024]{2,1,0:T(8,128)(2,1)S(1)} %collective-permute-done.12.m_sib, bf16[512,256]{1,0:T(8,128)(2,1)S(1)} %pick.2.refs_0_, ...), custom_call_target="tpu_custom_call" | custom-call | flops 2147483648 | bytes 8388608 | tf_op jit(solution)/shard_map/apply_matrix/pallas_call | solution.py:212
  95.0 1.7 collective-permute-start.16
  97.4 1.2 collective-permute-start.18
  98.6 5.7 %collective-permute-done.16.refs_1_ = bf16[512,256]{1,0:T(8,128)(2,1)S(1)} collective-permute-done((bf16[512,256]{1,0:T(8,128)(2,1)S(1)}, bf16[512,256]{1,0:T(8,128)(2,1)S(1)}, u32[]{:S(2)}, u32[]{:S(2)}) %collective-permute-start.16) | collective-permute-done | bytes 262176 | tf_op jit(solution)/shard_map/ppermute | solution.py:440
  104.3 5.6 %collective-permute-done.17.refs_2_ = bf16[512,256]{1,0:T(8,128)(2,1)S(1)} collective-permute-done((bf16[512,256]{1,0:T(8,128)(2,1)S(1)}, bf16[512,256]{1,0:T(8,128)(2,1)S(1)}, u32[]{:S(2)}, u32[]{:S(2)}) %collective-permute-start.17) | collective-permute-done | bytes 262176 | tf_op jit(solution)/shard_map/ppermute | solution.py:440
  110.2 1.3 collective-permute-start.21
  112.1 1.6 collective-permute-start.19
  113.8 6.7 %collective-permute-done.21.refs_3_ = bf16[512,256]{1,0:T(8,128)(2,1)S(1)} collective-permute-done((bf16[512,256]{1,0:T(8,128)(2,1)S(1)}, bf16[512,256]{1,0:T(8,128)(2,1)S(1)}, u32[]{:S(2)}, u32[]{:S(2)}) %collective-permute-start.21) | collective-permute-done | bytes 262176 | tf_op jit(solution)/shard_map/ppermute | solution.py:440
  120.4 2.8 %collective-permute-done.20.refs_2_ = bf16[512,256]{1,0:T(8,128)(2,1)S(1)} collective-permute-done((bf16[512,256]{1,0:T(8,128)(2,1)S(1)}, bf16[512,256]{1,0:T(8,128)(2,1)S(1)}, u32[]{:S(2)}, u32[]{:S(2)}) %collective-permute-start.20) | collective-permute-done | bytes 262176 | tf_op jit(solution)/shard_map/ppermute | solution.py:440
  124.6 1.9 %collective-permute-start.22 = (bf16[512,256]{1,0:T(8,128)(2,1)S(1)}, bf16[512,256]{1,0:T(8,128)(2,1)S(1)}, u32[]{:S(2)}, u32[]{:S(2)}) collective-permute-start(bf16[512,256]{1,0:T(8,128)(2,1)S(1)} %pick.3.refs_0_), channel_id=1, source_target_pairs={{0,8},{8,16},{16,24},{24,0},{1,9},{9,17},{17,25},{25,1},{2,10},{10... | collective-permute-start | bytes 786440 | tf_op jit(solution)/shard_map/ppermute | solution.py:443
  126.5 7.0 %collective-permute-done.24.refs_3_ = bf16[512,256]{1,0:T(8,128)(2,1)S(1)} collective-permute-done((bf16[512,256]{1,0:T(8,128)(2,1)S(1)}, bf16[512,256]{1,0:T(8,128)(2,1)S(1)}, u32[]{:S(2)}, u32[]{:S(2)}) %collective-permute-start.24) | collective-permute-done | bytes 262176 | tf_op jit(solution)/shard_map/ppermute | solution.py:443
  133.5 14.0 %collective-permute-done.23.refs_2_ = bf16[512,256]{1,0:T(8,128)(2,1)S(1)} collective-permute-done((bf16[512,256]{1,0:T(8,128)(2,1)S(1)}, bf16[512,256]{1,0:T(8,128)(2,1)S(1)}, u32[]{:S(2)}, u32[]{:S(2)}) %collective-permute-start.23) | collective-permute-done | bytes 262176 | tf_op jit(solution)/shard_map/ppermute | solution.py:443
  147.5 3.1 %apply_matrix.3 = (f32[512,256]{1,0:T(8,128)S(1)}, bf16[512,256]{1,0:T(8,128)(2,1)S(1)}, bf16[512,256]{1,0:T(8,128)(2,1)S(1)}, bf16[512,256]{1,0:T(8,128)(2,1)S(1)}) custom-call(bf16[4,512,1024]{2,1,0:T(8,128)(2,1)S(1)} %copy-done, bf16[4,512,1024]{2,1,0:T(8,128)(2,1)S(1)} %collective-permute-done.12.m_sib, bf16[512,256]{1,0:T(8,128)(2,1)S(1)} %pick.3.refs_0_, ...), custom_call_target="tpu_custom_call" | custom-call | flops 2147483648 | bytes 8388608 | tf_op jit(solution)/shard_map/apply_matrix/pallas_call | solution.py:212
  150.6 2.0 %collective-permute-start.25 = (bf16[512,256]{1,0:T(8,128)(2,1)S(1)}, bf16[512,256]{1,0:T(8,128)(2,1)S(1)}, u32[]{:S(2)}, u32[]{:S(2)}) collective-permute-start(bf16[512,256]{1,0:T(8,128)(2,1)S(1)} %get-tuple-element.62), channel_id=1, source_target_pairs={{0,2},{1,3},{2,0},{3,1},{4,6},{5,7},{6,4},{7,5},{8,10},{9,11},{10,... | collective-permute-start | bytes 786440 | tf_op jit(solution)/shard_map/ppermute | solution.py:440
  154.2 5.7 %collective-permute-done.25.refs_1_ = bf16[512,256]{1,0:T(8,128)(2,1)S(1)} collective-permute-done((bf16[512,256]{1,0:T(8,128)(2,1)S(1)}, bf16[512,256]{1,0:T(8,128)(2,1)S(1)}, u32[]{:S(2)}, u32[]{:S(2)}) %collective-permute-start.25) | collective-permute-done | bytes 262176 | tf_op jit(solution)/shard_map/ppermute | solution.py:440
  159.9 5.8 %collective-permute-done.26.refs_2_ = bf16[512,256]{1,0:T(8,128)(2,1)S(1)} collective-permute-done((bf16[512,256]{1,0:T(8,128)(2,1)S(1)}, bf16[512,256]{1,0:T(8,128)(2,1)S(1)}, u32[]{:S(2)}, u32[]{:S(2)}) %collective-permute-start.26) | collective-permute-done | bytes 262176 | tf_op jit(solution)/shard_map/ppermute | solution.py:440
  (74 shorter events, 22.8 us)
Async XLA Ops:
  4.0 23.7 %collective-permute-start.7 = (bf16[256,256]{1,0:T(8,128)(2,1)S(1)}, bf16[256,256]{1,0:T(8,128)(2,1)S(1)}, u32[]{:S(2)}, u32[]{:S(2)}) collective-permute-start(bf16[256,256]{1,0:T(8,128)(2,1)S(1)} %get-tuple-element.36), channel_id=1, source_target_pairs={{0,1},{1,0},{2,3},{3,2},{4,5},{5,4},{6,7},{7,6},{8,9},{9,8},{10,11... | collective-permute-start | bytes 393224 | tf_op jit(solution)/shard_map/ppermute | solution.py:437
  4.6 19.2 %collective-permute-start.6 = (s32[16]{0:T(128)}, s32[16]{0:T(128)S(1)}, u32[]{:S(2)}, u32[]{:S(2)}) collective-permute-start(s32[16]{0:T(128)} %refs_4_), channel_id=1, source_target_pairs={{0,24},{8,0},{16,8},{24,16},{1,25},{9,1},{17,9},{25,17},{2,26},{10... | collective-permute-start | bytes 200 | tf_op jit(solution)/shard_map/ppermute | solution.py:443
  9.2 14.5 %collective-permute-start.5 = (s32[16]{0:T(128)}, s32[16]{0:T(128)S(1)}, u32[]{:S(2)}, u32[]{:S(2)}) collective-permute-start(s32[16]{0:T(128)} %refs_4_), channel_id=1, source_target_pairs={{0,16},{8,24},{16,0},{24,8},{1,17},{9,25},{17,1},{25,9},{2,18},{10... | collective-permute-start | bytes 200 | tf_op jit(solution)/shard_map/ppermute | solution.py:443
  9.2 14.5 %collective-permute-start.4 = (s32[16]{0:T(128)}, s32[16]{0:T(128)S(1)}, u32[]{:S(2)}, u32[]{:S(2)}) collective-permute-start(s32[16]{0:T(128)} %refs_4_), channel_id=1, source_target_pairs={{0,8},{8,16},{16,24},{24,0},{1,9},{9,17},{17,25},{25,1},{2,10},{10... | collective-permute-start | bytes 200 | tf_op jit(solution)/shard_map/ppermute | solution.py:443
  10.2 1.3 collective-permute-start
  12.2 4.4 %collective-permute-start.3 = (s32[4]{0:T(128)S(1)}, s32[4]{0:T(128)S(1)}, u32[]{:S(2)}, u32[]{:S(2)}) collective-permute-start(s32[4]{0:T(128)S(1)} %pad_add_fusion.refs_0_), channel_id=1, source_target_pairs={{0,6},{1,7},{2,4},{3,5},{4,2},{5,3},{6,0},{7,1},{8,14},{9,15},{10,... | collective-permute-start | bytes 56 | tf_op jit(solution)/shard_map/ppermute | solution.py:440
  16.7 3.5 %collective-permute-start.2 = (s32[4]{0:T(128)S(1)}, s32[4]{0:T(128)S(1)}, u32[]{:S(2)}, u32[]{:S(2)}) collective-permute-start(s32[4]{0:T(128)S(1)} %pad_add_fusion.refs_0_), channel_id=1, source_target_pairs={{0,4},{1,5},{2,6},{3,7},{4,0},{5,1},{6,2},{7,3},{8,12},{9,13},{10,... | collective-permute-start | bytes 56 | tf_op jit(solution)/shard_map/ppermute | solution.py:440
  20.2 3.5 %collective-permute-start.1 = (s32[4]{0:T(128)S(1)}, s32[4]{0:T(128)S(1)}, u32[]{:S(2)}, u32[]{:S(2)}) collective-permute-start(s32[4]{0:T(128)S(1)} %pad_add_fusion.refs_0_), channel_id=1, source_target_pairs={{0,2},{1,3},{2,0},{3,1},{4,6},{5,7},{6,4},{7,5},{8,10},{9,11},{10,... | collective-permute-start | bytes 56 | tf_op jit(solution)/shard_map/ppermute | solution.py:440
  32.1 31.3 %copy-start.8 = (f32[256,512]{1,0:T(8,128)S(1)}, f32[256,512]{1,0:T(8,128)}, u32[]{:S(2)}) copy-start(f32[256,512]{1,0:T(8,128)} %evolve) | copy-start | bytes 1572868
  47.3 44.6 %copy-start = (bf16[4,512,1024]{2,1,0:T(8,128)(2,1)S(1)}, bf16[4,512,1024]{2,1,0:T(8,128)(2,1)}, u32[]{:S(2)}) copy-start(bf16[4,512,1024]{2,1,0:T(8,128)(2,1)} %build_matrix.1.m_own) | copy-start | bytes 12582916
  47.3 44.6 %collective-permute-start.12 = (bf16[4,512,1024]{2,1,0:T(8,128)(2,1)}, bf16[4,512,1024]{2,1,0:T(8,128)(2,1)S(1)}, u32[]{:S(2)}, u32[]{:S(2)}) collective-permute-start(bf16[4,512,1024]{2,1,0:T(8,128)(2,1)} %build_matrix.1.m_own), channel_id=1, source_target_pairs={{0,1},{1,0},{2,3},{3,2},{4,5},{5,4},{6,7},{7,6},{8,9},{9,8},{10,11... | collective-permute-start | bytes 12582920 | tf_op jit(solution)/shard_map/ppermute | solution.py:437
  47.3 10.1 %collective-permute-start.10 = (bf16[512,256]{1,0:T(8,128)(2,1)S(1)}, bf16[512,256]{1,0:T(8,128)(2,1)S(1)}, u32[]{:S(2)}, u32[]{:S(2)}) collective-permute-start(bf16[512,256]{1,0:T(8,128)(2,1)S(1)} %merge.1.refs_0_), channel_id=1, source_target_pairs={{0,6},{1,7},{2,4},{3,5},{4,2},{5,3},{6,0},{7,1},{8,14},{9,15},{10,... | collective-permute-start | bytes 786440 | tf_op jit(solution)/shard_map/ppermute | solution.py:440
  49.9 12.7 %collective-permute-start.9 = (bf16[512,256]{1,0:T(8,128)(2,1)S(1)}, bf16[512,256]{1,0:T(8,128)(2,1)S(1)}, u32[]{:S(2)}, u32[]{:S(2)}) collective-permute-start(bf16[512,256]{1,0:T(8,128)(2,1)S(1)} %merge.1.refs_0_), channel_id=1, source_target_pairs={{0,4},{1,5},{2,6},{3,7},{4,0},{5,1},{6,2},{7,3},{8,12},{9,13},{10,... | collective-permute-start | bytes 786440 | tf_op jit(solution)/shard_map/ppermute | solution.py:440
  50.7 12.0 %collective-permute-start.8 = (bf16[512,256]{1,0:T(8,128)(2,1)S(1)}, bf16[512,256]{1,0:T(8,128)(2,1)S(1)}, u32[]{:S(2)}, u32[]{:S(2)}) collective-permute-start(bf16[512,256]{1,0:T(8,128)(2,1)S(1)} %merge.1.refs_0_), channel_id=1, source_target_pairs={{0,2},{1,3},{2,0},{3,1},{4,6},{5,7},{6,4},{7,5},{8,10},{9,11},{10,... | collective-permute-start | bytes 786440 | tf_op jit(solution)/shard_map/ppermute | solution.py:440
  64.3 34.2 %collective-permute-start.11 = (f32[1,3,256,256]{3,2,1,0:T(8,128)S(1)}, f32[1,3,256,256]{3,2,1,0:T(8,128)S(1)}, u32[]{:S(2)}, u32[]{:S(2)}) collective-permute-start(f32[1,3,256,256]{3,2,1,0:T(8,128)S(1)} %get-tuple-element.49), channel_id=1, source_target_pairs={{0,1},{1,0},{2,3},{3,2},{4,5},{5,4},{6,7},{7,6},{8,9},{9,8},{10,11... | collective-permute-start | bytes 2359304 | tf_op jit(solution)/shard_map/ppermute | solution.py:437
  64.4 9.6 %collective-permute-start.15 = (bf16[512,256]{1,0:T(8,128)(2,1)S(1)}, bf16[512,256]{1,0:T(8,128)(2,1)S(1)}, u32[]{:S(2)}, u32[]{:S(2)}) collective-permute-start(bf16[512,256]{1,0:T(8,128)(2,1)S(1)} %pick.2.refs_0_), channel_id=1, source_target_pairs={{0,24},{8,0},{16,8},{24,16},{1,25},{9,1},{17,9},{25,17},{2,26},{10... | collective-permute-start | bytes 786440 | tf_op jit(solution)/shard_map/ppermute | solution.py:443
  67.3 24.6 %collective-permute-start.14 = (bf16[512,256]{1,0:T(8,128)(2,1)S(1)}, bf16[512,256]{1,0:T(8,128)(2,1)S(1)}, u32[]{:S(2)}, u32[]{:S(2)}) collective-permute-start(bf16[512,256]{1,0:T(8,128)(2,1)S(1)} %pick.2.refs_0_), channel_id=1, source_target_pairs={{0,16},{8,24},{16,0},{24,8},{1,17},{9,25},{17,1},{25,9},{2,18},{10... | collective-permute-start | bytes 786440 | tf_op jit(solution)/shard_map/ppermute | solution.py:443
  68.4 23.5 %collective-permute-start.13 = (bf16[512,256]{1,0:T(8,128)(2,1)S(1)}, bf16[512,256]{1,0:T(8,128)(2,1)S(1)}, u32[]{:S(2)}, u32[]{:S(2)}) collective-permute-start(bf16[512,256]{1,0:T(8,128)(2,1)S(1)} %pick.2.refs_0_), channel_id=1, source_target_pairs={{0,8},{8,16},{16,24},{24,0},{1,9},{9,17},{17,25},{25,1},{2,10},{10... | collective-permute-start | bytes 786440 | tf_op jit(solution)/shard_map/ppermute | solution.py:443
  95.0 9.3 %collective-permute-start.16 = (bf16[512,256]{1,0:T(8,128)(2,1)S(1)}, bf16[512,256]{1,0:T(8,128)(2,1)S(1)}, u32[]{:S(2)}, u32[]{:S(2)}) collective-permute-start(bf16[512,256]{1,0:T(8,128)(2,1)S(1)} %get-tuple-element.56), channel_id=1, source_target_pairs={{0,2},{1,3},{2,0},{3,1},{4,6},{5,7},{6,4},{7,5},{8,10},{9,11},{10,... | collective-permute-start | bytes 786440 | tf_op jit(solution)/shard_map/ppermute | solution.py:440
  96.7 13.2 %collective-permute-start.17 = (bf16[512,256]{1,0:T(8,128)(2,1)S(1)}, bf16[512,256]{1,0:T(8,128)(2,1)S(1)}, u32[]{:S(2)}, u32[]{:S(2)}) collective-permute-start(bf16[512,256]{1,0:T(8,128)(2,1)S(1)} %get-tuple-element.57), channel_id=1, source_target_pairs={{0,4},{1,5},{2,6},{3,7},{4,0},{5,1},{6,2},{7,3},{8,12},{9,13},{10,... | collective-permute-start | bytes 786440 | tf_op jit(solution)/shard_map/ppermute | solution.py:440
  97.4 12.5 %collective-permute-start.18 = (bf16[512,256]{1,0:T(8,128)(2,1)S(1)}, bf16[512,256]{1,0:T(8,128)(2,1)S(1)}, u32[]{:S(2)}, u32[]{:S(2)}) collective-permute-start(bf16[512,256]{1,0:T(8,128)(2,1)S(1)} %get-tuple-element.58), channel_id=1, source_target_pairs={{0,6},{1,7},{2,4},{3,5},{4,2},{5,3},{6,0},{7,1},{8,14},{9,15},{10,... | collective-permute-start | bytes 786440 | tf_op jit(solution)/shard_map/ppermute | solution.py:440
  110.2 10.2 %collective-permute-start.21 = (bf16[512,256]{1,0:T(8,128)(2,1)S(1)}, bf16[512,256]{1,0:T(8,128)(2,1)S(1)}, u32[]{:S(2)}, u32[]{:S(2)}) collective-permute-start(bf16[512,256]{1,0:T(8,128)(2,1)S(1)} %get-tuple-element.60.refs_0_), channel_id=1, source_target_pairs={{0,6},{1,7},{2,4},{3,5},{4,2},{5,3},{6,0},{7,1},{8,14},{9,15},{10,... | collective-permute-start | bytes 786440 | tf_op jit(solution)/shard_map/ppermute | solution.py:440
  111.5 11.8 %collective-permute-start.20 = (bf16[512,256]{1,0:T(8,128)(2,1)S(1)}, bf16[512,256]{1,0:T(8,128)(2,1)S(1)}, u32[]{:S(2)}, u32[]{:S(2)}) collective-permute-start(bf16[512,256]{1,0:T(8,128)(2,1)S(1)} %get-tuple-element.60.refs_0_), channel_id=1, source_target_pairs={{0,4},{1,5},{2,6},{3,7},{4,0},{5,1},{6,2},{7,3},{8,12},{9,13},{10,... | collective-permute-start | bytes 786440 | tf_op jit(solution)/shard_map/ppermute | solution.py:440
  112.1 11.1 %collective-permute-start.19 = (bf16[512,256]{1,0:T(8,128)(2,1)S(1)}, bf16[512,256]{1,0:T(8,128)(2,1)S(1)}, u32[]{:S(2)}, u32[]{:S(2)}) collective-permute-start(bf16[512,256]{1,0:T(8,128)(2,1)S(1)} %get-tuple-element.60.refs_0_), channel_id=1, source_target_pairs={{0,2},{1,3},{2,0},{3,1},{4,6},{5,7},{6,4},{7,5},{8,10},{9,11},{10,... | collective-permute-start | bytes 786440 | tf_op jit(solution)/shard_map/ppermute | solution.py:440
  123.9 9.6 %collective-permute-start.24 = (bf16[512,256]{1,0:T(8,128)(2,1)S(1)}, bf16[512,256]{1,0:T(8,128)(2,1)S(1)}, u32[]{:S(2)}, u32[]{:S(2)}) collective-permute-start(bf16[512,256]{1,0:T(8,128)(2,1)S(1)} %pick.3.refs_0_), channel_id=1, source_target_pairs={{0,24},{8,0},{16,8},{24,16},{1,25},{9,1},{17,9},{25,17},{2,26},{10... | collective-permute-start | bytes 786440 | tf_op jit(solution)/shard_map/ppermute | solution.py:443
  124.0 23.5 %collective-permute-start.23 = (bf16[512,256]{1,0:T(8,128)(2,1)S(1)}, bf16[512,256]{1,0:T(8,128)(2,1)S(1)}, u32[]{:S(2)}, u32[]{:S(2)}) collective-permute-start(bf16[512,256]{1,0:T(8,128)(2,1)S(1)} %pick.3.refs_0_), channel_id=1, source_target_pairs={{0,16},{8,24},{16,0},{24,8},{1,17},{9,25},{17,1},{25,9},{2,18},{10... | collective-permute-start | bytes 786440 | tf_op jit(solution)/shard_map/ppermute | solution.py:443
  124.6 22.9 %collective-permute-start.22 = (bf16[512,256]{1,0:T(8,128)(2,1)S(1)}, bf16[512,256]{1,0:T(8,128)(2,1)S(1)}, u32[]{:S(2)}, u32[]{:S(2)}) collective-permute-start(bf16[512,256]{1,0:T(8,128)(2,1)S(1)} %pick.3.refs_0_), channel_id=1, source_target_pairs={{0,8},{8,16},{16,24},{24,0},{1,9},{9,17},{17,25},{25,1},{2,10},{10... | collective-permute-start | bytes 786440 | tf_op jit(solution)/shard_map/ppermute | solution.py:443
  150.6 9.3 %collective-permute-start.25 = (bf16[512,256]{1,0:T(8,128)(2,1)S(1)}, bf16[512,256]{1,0:T(8,128)(2,1)S(1)}, u32[]{:S(2)}, u32[]{:S(2)}) collective-permute-start(bf16[512,256]{1,0:T(8,128)(2,1)S(1)} %get-tuple-element.62), channel_id=1, source_target_pairs={{0,2},{1,3},{2,0},{3,1},{4,6},{5,7},{6,4},{7,5},{8,10},{9,11},{10,... | collective-permute-start | bytes 786440 | tf_op jit(solution)/shard_map/ppermute | solution.py:440
  152.6 13.0 %collective-permute-start.26 = (bf16[512,256]{1,0:T(8,128)(2,1)S(1)}, bf16[512,256]{1,0:T(8,128)(2,1)S(1)}, u32[]{:S(2)}, u32[]{:S(2)}) collective-permute-start(bf16[512,256]{1,0:T(8,128)(2,1)S(1)} %get-tuple-element.63), channel_id=1, source_target_pairs={{0,4},{1,5},{2,6},{3,7},{4,0},{5,1},{6,2},{7,3},{8,12},{9,13},{10,... | collective-permute-start | bytes 786440 | tf_op jit(solution)/shard_map/ppermute | solution.py:440
  153.0 12.7 %collective-permute-start.27 = (bf16[512,256]{1,0:T(8,128)(2,1)S(1)}, bf16[512,256]{1,0:T(8,128)(2,1)S(1)}, u32[]{:S(2)}, u32[]{:S(2)}) collective-permute-start(bf16[512,256]{1,0:T(8,128)(2,1)S(1)} %get-tuple-element.64), channel_id=1, source_target_pairs={{0,6},{1,7},{2,4},{3,5},{4,2},{5,3},{6,0},{7,1},{8,14},{9,15},{10,... | collective-permute-start | bytes 786440 | tf_op jit(solution)/shard_map/ppermute | solution.py:440
  154.2 11.7 %collective-permute-start.29 = (f32[256,256]{1,0:T(8,128)S(1)}, f32[256,256]{1,0:T(8,128)S(1)}, u32[]{:S(2)}, u32[]{:S(2)}) collective-permute-start(f32[256,256]{1,0:T(8,128)S(1)} %get-tuple-element.69), channel_id=1, source_target_pairs={{0,1},{1,0},{2,3},{3,2},{4,5},{5,4},{6,7},{7,6},{8,9},{9,8},{10,11... | collective-permute-start | bytes 786440 | tf_op jit(solution)/shard_map/ppermute | solution.py:437
  165.8 1.6 collective-permute-start.28
  (11 other events, 161.4 us)

commit v3 on v2

v3 whole, which is shorter than its diff:
```python
import functools

import jax
import jax.numpy as jnp
from jax import lax
from jax.experimental import pallas as pl
from jax.experimental.pallas import tpu as pltpu
from jax.sharding import PartitionSpec as P

TIME_STEP = 0.1
SECTION_SHIFT = 2.0 / 3.0
FIRST_WEIGHT = 0.25
SECOND_WEIGHT = 0.75
MID = TIME_STEP * SECTION_SHIFT
W1 = TIME_STEP * FIRST_WEIGHT
W2 = TIME_STEP * SECOND_WEIGHT
CHUNKS = 2
SHARES = (1,)
COST_SHARE = 0.01
GROUP = 4
WIDE = 56 * 1024 * 1024

F32 = jnp.float32
BF16 = jnp.bfloat16
VMEM = pl.BlockSpec(memory_space=pltpu.VMEM)
SMEM = pl.BlockSpec(memory_space=pltpu.SMEM)
HBM = pl.BlockSpec(memory_space=pltpu.HBM)
EXTRA = 16
LIMIT = 16 * 1024 * 1024


def params(limit=LIMIT):
    return pltpu.CompilerParams(vmem_limit_bytes=limit)


def cost(flops, nbytes, trans=0):
    return pl.CostEstimate(
        flops=int(flops * COST_SHARE), bytes_accessed=int(nbytes * COST_SHARE), transcendentals=int(trans * COST_SHARE)
    )


def struct(shape, dtype):
    return jax.ShapeDtypeStruct(shape, dtype)


def build_kernel(first, count, near_cols, far_cols, far_ranks, near_in, left_in, right_in, out, *scratch):
    near, left, right, spread, dense, held, sems, out_sems = scratch
    slots, cell = near.shape[2], near.shape[3]
    far_slots, rank = left.shape[2], left.shape[3]
    pairs = ((near_in, near), (left_in, left), (right_in, right))
    copies, stores = [], []
    for i in range(0, count, GROUP):
        copies.append(
            [
                pltpu.make_async_copy(src.at[pl.ds(first + i, GROUP)], dst.at[pl.ds(i, GROUP)], sems.at[n, i // GROUP])
                for n, (src, dst) in enumerate(pairs)
            ]
        )
        at = pl.ds(i * cell, GROUP * cell)
        stores.append(pltpu.make_async_copy(held.at[at], out.at[at], out_sems.at[i // GROUP]))
    for group in copies:
        for copy in group:
            copy.start()
    ranks = lax.broadcasted_iota(jnp.int32, (rank, cell), 0)
    spread[...] = jnp.zeros_like(spread)
    dense[...] = jnp.zeros_like(dense)

    def far_place(q, k):
        return pl.ds(pl.multiple_of(far_cols[k, 0, q] * cell, cell), cell)

    def near_place(q, k):
        return pl.ds(pl.multiple_of(jnp.maximum(near_cols[k, 0, q], 0) * cell, cell), cell)

    for i in range(count):
        q = first + i
        turn = i % 2
        if i % GROUP == 0:
            for copy in copies[i // GROUP]:
                copy.wait()
        if i >= 2:
            for k in range(far_slots):
                spread[turn, pl.ds(k * rank, rank), far_place(q - 2, k)] = jnp.zeros((rank, cell), BF16)
            for k in range(slots):
                dense[turn, :, near_place(q - 2, k)] = jnp.zeros((cell, cell), BF16)
        for k in range(far_slots):
            kept = jnp.where(ranks < far_ranks[k, 0, q], right[i, 0, k], jnp.zeros((), BF16))
            spread[turn, pl.ds(k * rank, rank), far_place(q, k)] = kept
        for k in range(slots):

            @pl.when(near_cols[k, 0, q] >= 0)
            def _():
                dense[turn, :, near_place(q, k)] = near[i, 0, k]

        product = lax.dot_general(
            left[i, 0].reshape(far_slots * rank, cell),
            spread[turn],
            (((0,), (0,)), ((), ())),
            preferred_element_type=F32,
        )
        held[pl.ds(i * cell, cell)] = (product + dense[turn].astype(F32)).astype(BF16)
        if i % GROUP == GROUP - 1:
            stores[i // GROUP].start()
    for store in stores:
        store.wait()


def build_matrix(tables, factors, width, first, count):
    near, left, right = factors
    cell = near.shape[3]
    far_slots, rank = left.shape[2:4]
    depth = width * cell
    held = [pltpu.VMEM((count,) + array.shape[1:], BF16) for array in factors]
    return pl.pallas_call(
        functools.partial(build_kernel, first, count),
        out_shape=struct((count * cell, depth), BF16),
        in_specs=[SMEM] * 3 + [HBM] * 3,
        out_specs=HBM,
        scratch_shapes=held
        + [
            pltpu.VMEM((2, far_slots * rank, depth), BF16),
            pltpu.VMEM((2, cell, depth), BF16),
            pltpu.VMEM((count * cell, depth), BF16),
            pltpu.SemaphoreType.DMA((3, count // GROUP)),
            pltpu.SemaphoreType.DMA((count // GROUP,)),
        ],
        compiler_params=params(WIDE),
        cost_estimate=cost(2 * count * cell * far_slots * rank * depth, 2 * (near.size + left.size + right.size)),
        name="build_matrix",
    )(*tables, *factors)


def copy_picked(sel, sources, out, cell):
    pair_patches = sel.shape[0]
    for t in range(pair_patches):
        which = lax.div(sel[t], pair_patches)
        block = pl.multiple_of(lax.rem(sel[t], pair_patches) * cell, cell)
        for m, source in enumerate(sources):

            @pl.when(which == m)
            def _():
                out[pl.ds(t * cell, cell)] = source[pl.ds(block, cell)]


def pick_kernel(cell, sel, *refs):
    copy_picked(sel, refs[:-1], refs[-1], cell)


def pick(sel, sources, cell):
    return pl.pallas_call(
        functools.partial(pick_kernel, cell),
        out_shape=struct(sources[0].shape, BF16),
        in_specs=[SMEM] + [VMEM] * len(sources),
        out_specs=VMEM,
        compiler_params=params(),
        cost_estimate=cost(0, 4 * sources[0].size),
        name="pick",
    )(sel, *sources)


def read_extra(ref, count):
    high = ref.shape[0] - EXTRA
    tile = ref[pl.ds(high, EXTRA), pl.ds(0, 128)].astype(F32)
    return [jnp.max(tile[i : i + 1]).astype(jnp.int32) for i in range(count)]


def write_extra(ref, values):
    high, lanes = ref.shape[0] - EXTRA, ref.shape[1]
    at = lax.broadcasted_iota(jnp.int32, (EXTRA, lanes), 0)
    tile = jnp.zeros((EXTRA, lanes), F32)
    for i, value in values:
        tile = jnp.where(at == i, value.astype(F32), tile)
    ref[pl.ds(high, EXTRA)] = tile.astype(BF16)


def first_pick_kernel(cell, width, patch_count, perm, *refs):
    sources, (out, sel, rows, inv, ids) = refs[:-5], refs[-5:]
    pair_patches = 2 * patch_count
    for m, source in enumerate(sources):
        for i, q in enumerate(read_extra(source, pair_patches)):
            inv[q] = m * pair_patches + i
            rows[m * pair_patches + i] = q
    col = lax.axis_index("col")
    for n, group in enumerate((col, col + 1 - 2 * lax.rem(col, 2))):

        def choose(q, count, n=n, group=group):
            hit = lax.div(perm[q], width) == group

            @pl.when(hit)
            def _():
                sel[n * patch_count + count] = inv[q]
                ids[n * patch_count + count] = lax.rem(perm[q], width)

            return count + hit.astype(jnp.int32)

        lax.fori_loop(0, perm.shape[0], choose, jnp.int32(0))
    copy_picked(sel, sources, out, cell)
    write_extra(out, [(t, ids[t]) for t in range(pair_patches)])


def first_pick(perm, sources, cell, width, patch_count):
    rows_dev = perm.shape[0]
    return pl.pallas_call(
        functools.partial(first_pick_kernel, cell, width, patch_count),
        out_shape=(
            struct(sources[0].shape, BF16),
            struct((2 * patch_count,), jnp.int32),
            struct((rows_dev,), jnp.int32),
        ),
        in_specs=[SMEM] + [VMEM] * len(sources),
        out_specs=(VMEM, SMEM, SMEM),
        scratch_shapes=[pltpu.SMEM((rows_dev,), jnp.int32), pltpu.SMEM((2 * patch_count,), jnp.int32)],
        compiler_params=params(),
        cost_estimate=cost(1000, 4 * sources[0].size),
        name="first_pick",
    )(perm, *sources)


def apply_kernel(n_part, n_pair, n_row, cell, patch_count, first, *refs):
    m_own, m_sib = refs[:n_part], refs[n_part : 2 * n_part]
    pieces = refs[2 * n_part : 2 * n_part + n_row]
    rows, refs = refs[2 * n_part + n_row], refs[2 * n_part + n_row + 1 :]
    pair_patches = 2 * patch_count
    if not first:
        ids, refs = refs[0], refs[1:]
    outs, refs = refs[:n_pair], refs[n_pair:]
    if first:
        ids, refs = refs[0], refs[1:]
        for s in range(n_row):
            for t, block in enumerate(read_extra(pieces[s], pair_patches)):
                ids[s * pair_patches + t] = block
    x_own, x_sib, total = refs
    for s in range(n_row):
        for t in range(pair_patches):
            at = pl.ds(pl.multiple_of(ids[s * pair_patches + t] * cell, cell), cell)
            (x_own if t < patch_count else x_sib)[at] = pieces[s][pl.ds(t * cell, cell)]
    high, base = pair_patches * cell, 0
    for own, sib in zip(m_own, m_sib):
        for at in range(0, own.shape[0], high):
            part = jnp.dot(own[pl.ds(at, high)], x_own[...], preferred_element_type=F32)
            part = part + jnp.dot(sib[pl.ds(at, high)], x_sib[...], preferred_element_type=F32)
            total[pl.ds(base + at, high)] = part
        base += own.shape[0]
    for m in range(n_pair):
        for i in range(pair_patches):
            at = pl.ds(pl.multiple_of(rows[m * pair_patches + i] * cell, cell), cell)
            outs[m][pl.ds(i * cell, cell)] = total[at].astype(outs[m].dtype)


def apply_matrix(m_own, m_sib, pieces, rows, ids, cell, patch_count):
    n_row, n_part = len(pieces), len(m_own)
    high, depth = 2 * patch_count * cell, m_own[0].shape[1]
    rows_dev = rows.shape[0]
    n_pair = rows_dev * cell // high
    lanes = pieces[0].shape[1]
    first = ids is None
    extra = [] if first else [ids]
    ids_shape = struct((n_row * 2 * patch_count,), jnp.int32)
    return pl.pallas_call(
        functools.partial(apply_kernel, n_part, n_pair, n_row, cell, patch_count, first),
        out_shape=tuple(struct((high, lanes), F32 if m == 0 else BF16) for m in range(n_pair))
        + ((ids_shape,) if first else ()),
        in_specs=[VMEM] * (2 * n_part + n_row) + [SMEM] * (1 + len(extra)),
        out_specs=(VMEM,) * n_pair + ((SMEM,) if first else ()),
        scratch_shapes=[pltpu.VMEM((depth, lanes), BF16)] * 2 + [pltpu.VMEM((rows_dev * cell, lanes), F32)],
        compiler_params=params(48 * 1024 * 1024 if n_pair > 4 else LIMIT),
        cost_estimate=cost(4 * n_pair * high * depth * lanes, 4 * n_pair * high * depth),
        name="apply_matrix",
    )(*m_own, *m_sib, *pieces, rows, *extra)


def start_kernel(chunks, patch_rows, stress_in, state_in, direct_in, *refs):
    keep, give = refs[:chunks], refs[chunks : 2 * chunks]
    stress, state, direct, sems = refs[2 * chunks :]
    pairs = ((stress_in, stress), (state_in, state), (direct_in, direct))
    tile = stress.shape[0] // GROUP
    copies = [
        [
            pltpu.make_async_copy(src.at[pl.ds(g * tile, tile)], dst.at[pl.ds(g * tile, tile)], sems.at[n, g])
            for n, (src, dst) in enumerate(pairs)
        ]
        for g in range(GROUP)
    ]
    for group in copies:
        for copy in group:
            copy.start()
    half = stress.shape[1] // 2
    lanes = half // chunks
    patch_count = patch_rows.shape[0]
    side = lax.rem(lax.axis_index("col"), 2)
    for ref in (keep[0], give[0]):
        write_extra(ref, [(side * patch_count + i, patch_rows[i]) for i in range(patch_count)])
    for g, group in enumerate(copies):
        for copy in group:
            copy.wait()
        down = pl.ds(g * tile, tile)
        for own, outs in ((False, give), (True, keep)):
            base = (side if own else 1 - side) * half
            for j in range(chunks):
                at = pl.ds(pl.multiple_of(base + j * lanes, lanes), lanes)
                inverse = 1.0 / direct[down, at]
                stress_now, state_now = stress[down, at], state[down, at]
                velocity = jnp.exp((stress_now - state_now) * inverse) - jnp.exp((-stress_now - state_now) * inverse)
                outs[j][down] = velocity.astype(BF16)


def start(patch_rows, stress, state, direct, chunks):
    high, members = stress.shape
    lanes = members // 2 // chunks
    shapes = tuple(struct((high + (EXTRA if j == 0 else 0), lanes), BF16) for j in range(chunks))
    return pl.pallas_call(
        functools.partial(start_kernel, chunks),
        out_shape=shapes * 2,
        in_specs=[SMEM] + [HBM] * 3,
        out_specs=(VMEM,) * (2 * chunks),
        scratch_shapes=[pltpu.VMEM(stress.shape, F32)] * 3 + [pltpu.SemaphoreType.DMA((3, GROUP))],
        compiler_params=params(WIDE),
        cost_estimate=cost(10 * stress.size, 14 * stress.size, 3 * stress.size),
        name="start",
    )(patch_rows, stress, state, direct)


def mid_kernel(chunks, stress, state, direct, evolve, relax, load, keep, give, base, state_base):
    half = stress.shape[1] // 2
    lanes = half // chunks
    side = lax.rem(lax.axis_index("col"), 2)
    for own, ref in ((True, keep), (False, give)):
        first = (side if own else 1 - side) * half
        for j in range(chunks):
            at = pl.ds(pl.multiple_of(first + j * lanes, lanes), lanes)
            inverse = 1.0 / direct[:, at]
            inverse_e = 1.0 / evolve[:, at]
            stress_now, state_now = stress[:, at], state[:, at]
            relax_now, load_now = relax[:, at], load[:, at]
            velocity = jnp.exp((stress_now - state_now) * inverse) - jnp.exp((-stress_now - state_now) * inverse)
            state_rate = relax_now * (jnp.exp(-state_now * inverse_e) - velocity)
            state_mid = state_now + MID * state_rate
            ref[j, 0] = stress_now + MID * load_now
            ref[j, 1] = inverse
            ref[j, 2] = jnp.exp(-state_mid * inverse)
            base[:, at] = stress_now + TIME_STEP * load_now
            state_base[:, at] = state_now + W1 * state_rate + W2 * relax_now * jnp.exp(-state_mid * inverse_e)


def mid(stress, state, direct, evolve, relax, load, chunks):
    high, members = stress.shape
    lanes = members // 2 // chunks
    tile = 128
    wide = pl.BlockSpec((tile, members), lambda i: (i, 0))
    split = pl.BlockSpec((chunks, 3, tile, lanes), lambda i: (0, 0, i, 0))
    return pl.pallas_call(
        functools.partial(mid_kernel, chunks),
        out_shape=(struct((chunks, 3, high, lanes), F32),) * 2 + (struct(stress.shape, F32),) * 2,
        grid=(high // tile,),
        in_specs=[wide] * 6,
        out_specs=(split, split, wide, wide),
        compiler_params=params(),
        cost_estimate=cost(20 * stress.size, 44 * stress.size, 6 * stress.size),
        name="mid",
    )(stress, state, direct, evolve, relax, load)


def merge_kernel(high, keep, recv, out):
    side = lax.rem(lax.axis_index("col"), 2)
    out[pl.ds(pl.multiple_of(side * high, high), high)] = keep[pl.ds(0, high)]
    out[pl.ds(pl.multiple_of((1 - side) * high, high), high)] = recv[pl.ds(0, high)]
    if keep.shape[0] > high:
        out[pl.ds(2 * high, EXTRA)] = keep[pl.ds(high, EXTRA)] + recv[pl.ds(high, EXTRA)]


def merge(keep, recv, high):
    return pl.pallas_call(
        functools.partial(merge_kernel, high),
        out_shape=struct((keep.shape[0] + high, keep.shape[1]), keep.dtype),
        in_specs=[VMEM, VMEM],
        out_specs=VMEM,
        compiler_params=params(),
        cost_estimate=cost(0, 8 * keep.size),
        name="merge",
    )(keep, recv)


def second_kernel(keep, recv, *refs):
    n_pair = len(refs) - 4
    parts = refs[:n_pair]
    total_out, vel_b, vel_keep, vel_give = refs[n_pair:]
    high = keep.shape[2]
    side = lax.rem(lax.axis_index("col"), 2)
    for own, held, vel_out in ((True, keep, vel_keep), (False, recv, vel_give)):
        at = pl.ds(pl.multiple_of((side if own else 1 - side) * high, high), high)
        total = parts[0][at]
        for m in range(1, n_pair):
            total = total + parts[m][at].astype(F32)
        total_out[at] = W1 * total
        scaled = (held[0, 0] - MID * total) * held[0, 1]
        velocity = held[0, 2] * (jnp.exp(scaled) - jnp.exp(-scaled))
        vel_b[at] = velocity.astype(BF16)
        vel_out[...] = velocity


def second(keep, recv, parts, chunk):
    high, lanes = parts[0].shape
    held = pl.BlockSpec((1, 3, high // 2, lanes), lambda i: (chunk, 0, 0, 0))
    whole = pl.BlockSpec((high, lanes), lambda i: (0, 0))
    half = pl.BlockSpec((high // 2, lanes), lambda i: (0, 0))
    return pl.pallas_call(
        second_kernel,
        out_shape=(struct((high, lanes), F32), struct((high, lanes), BF16))
        + (struct((high // 2, lanes), F32),) * 2,
        grid=(1,),
        in_specs=[held, held] + [whole] * len(parts),
        out_specs=(whole, whole, half, half),
        compiler_params=params(),
        cost_estimate=cost(10 * high * lanes, 40 * high * lanes, 2 * high * lanes),
        name="second",
    )(keep, recv, *parts)


def weigh_kernel(first, *refs):
    parts = refs[:-2]
    keep, give = refs[-2:]
    high = keep.shape[0]
    side = lax.rem(lax.axis_index("col"), 2)
    for own, ref in ((False, give), (True, keep)):
        at = pl.ds(pl.multiple_of((side if own else 1 - side) * high, high), high)
        total = parts[0][at]
        for part in parts[1:]:
            total = total + part[at].astype(F32)
        ref[...] = first[at] + W2 * total


def weigh(first, parts):
    high, lanes = first.shape
    return pl.pallas_call(
        weigh_kernel,
        out_shape=(struct((high // 2, lanes), F32),) * 2,
        in_specs=[VMEM] * (1 + len(parts)),
        out_specs=(VMEM, VMEM),
        compiler_params=params(),
        cost_estimate=cost(10 * high * lanes, 20 * high * lanes),
        name="weigh",
    )(first, *parts)


def finish_kernel(chunks, scaled, base, *refs):
    out = refs[-1]
    factor = refs[0] if scaled else None
    pieces = refs[1:-1] if scaled else refs[:-1]
    half = base.shape[1] // 2
    lanes = half // chunks
    side = lax.rem(lax.axis_index("col"), 2)
    for j in range(chunks):
        for own, piece in ((True, pieces[j]), (False, pieces[chunks + j])):
            first = (side if own else 1 - side) * half + j * lanes
            at = pl.ds(pl.multiple_of(first, lanes), lanes)
            change = piece[...]
            if scaled:
                change = W2 * factor[:, at] * change
            out[:, at] = base[:, at] - change


def finish(base, factor, keeps, recvs):
    chunks = len(keeps)
    scaled = factor is not None
    extra = [factor] if scaled else []
    return pl.pallas_call(
        functools.partial(finish_kernel, chunks, scaled),
        out_shape=struct(base.shape, F32),
        in_specs=[VMEM] * (1 + len(extra) + 2 * chunks),
        out_specs=VMEM,
        compiler_params=params(),
        cost_estimate=cost(3 * base.size, 16 * base.size),
        name="finish",
    )(base, *extra, *keeps, *recvs)


def shards(
    stress,
    friction_state,
    direct,
    evolve,
    relax_rate,
    load_rate,
    row_perm,
    patch_rows,
    near_cols,
    near_blocks,
    far_cols,
    far_ranks,
    far_left,
    far_right,
):
    n_col, n_row = lax.axis_size("col"), lax.axis_size("row")
    n_pair = n_col // 2
    rows_dev = row_perm.shape[0]
    patch_count = patch_rows.shape[0]
    width = rows_dev * n_row // n_col
    cell = near_blocks.shape[-1]

    def after(values, dep):
        return lax.optimization_barrier((values, dep))[0]

    def swap(x):
        return lax.ppermute(x, "col", [(i, i ^ 1) for i in range(n_col)])

    def across(x, m):
        return lax.ppermute(x, "col", [(i, i ^ (2 * m)) for i in range(n_col)])

    def along(x, s):
        return lax.ppermute(x, "row", [(i, i ^ s) for i in range(n_row)])

    def after(values, dep):
        return lax.optimization_barrier((values, dep))[0]

    high = stress.shape[0]
    started = start(patch_rows, stress, friction_state, direct, CHUNKS)
    keep_first, give_first = started[:CHUNKS], started[CHUNKS:]
    tables = after([t.transpose(2, 1, 0) for t in (near_cols, far_cols, far_ranks)], give_first[0])
    factors = (near_blocks, far_left, far_right)
    unit = rows_dev // sum(SHARES)
    m_own, first_row = [], 0
    for share in SHARES:
        m_own.append(build_matrix(tables, factors, width, first_row, share * unit))
        first_row += share * unit
    recv_first = [swap(give) for give in give_first]
    held = (stress, friction_state, direct, evolve, relax_rate, load_rate)
    keep_mid, give_mid, base, state_base = mid(*after(held, m_own), CHUNKS)
    recv_first, m_own, give_mid = lax.optimization_barrier((recv_first, m_own, give_mid))
    m_sib = [swap(m) for m in m_own]
    recv_mid = swap(give_mid)

    def spread(vel_b):
        return [vel_b] + [across(vel_b, m) for m in range(1, n_pair)]

    def gather(chosen, dep=None):
        pieces, step = [chosen], n_row // 2
        while step:
            sent = [along(piece, step) for piece in pieces]
            if dep is not None:
                sent, dep = after(sent, dep), None
            pieces = pieces + sent
            step //= 2
        return pieces

    def reduce(partial):
        return [partial[0]] + [across(partial[m], m) for m in range(1, n_pair)]

    n = CHUNKS
    sources = spread(merge(keep_first[0], recv_first[0], high))
    perm = after(row_perm, (m_sib, recv_mid))
    chosen, sel, rows = first_pick(perm, sources, cell, width, patch_count)
    picked, arrived, partials, ids, dep = [chosen], [], [], None, chosen
    for j in range(1, n):
        sources = spread(merge(keep_first[j], after(recv_first[j], dep), high))
        arrived.append(gather(picked[-1], sources[1:]))
        partials.append(apply_matrix(m_own, m_sib, arrived[-1], rows, ids, cell, patch_count))
        ids = partials[-1][-1] if ids is None else ids
        picked.append(pick(after(sel, partials[-1][0]), sources, cell))
        dep = picked[-1]
    arrived.append(gather(picked[-1]))
    firsts, vel_keeps, vel_recvs, keeps, recvs = [], [], [], [], []
    dep, held_vel, last = None, [], []
    for j in range(n):
        if j == n - 1:
            rows_j = rows if dep is None else after(rows, dep)
            partials.append(apply_matrix(m_own, m_sib, arrived[j], rows_j, ids, cell, patch_count))
            ids = partials[-1][-1] if ids is None else ids
        parts = reduce(partials[j])
        if held_vel:
            parts[0] = after(parts[0], held_vel[-1])
        first, vel_b, vel_keep, vel_give = second(keep_mid, recv_mid, parts, j)
        dep = vel_b
        firsts.append(first)
        vel_keeps.append(vel_keep)
        vel_recvs.append(swap(vel_give))
        sel_j = sel if j == 0 else after(sel, last[-1][0])
        held_vel.append(pick(sel_j, spread(vel_b), cell))
        arrived.append(gather(held_vel[-1]))
        if j < n - 1:
            last.append(apply_matrix(m_own, m_sib, arrived[-1], rows, ids, cell, patch_count))
    for j in range(n):
        if j == n - 1:
            rows_j = rows if j == 0 else after(rows, keeps[-1])
            last.append(apply_matrix(m_own, m_sib, arrived[-1], rows_j, ids, cell, patch_count))
        keep, give = weigh(firsts[j], reduce(last[j]))
        keeps.append(keep)
        recvs.append(swap(give))
    state_next = finish(state_base, relax_rate, vel_keeps, vel_recvs)
    stress_next = finish(base, None, keeps, recvs)
    return (stress_next, state_next)


def solution(mesh):
    cells = P(("row", "col"), None)
    placed = (
        cells,
        cells,
        cells,
        cells,
        cells,
        cells,
        P("row"),
        P(("row", "col")),
        P("row", "col", None),
        P("row", "col", None, None, None),
        P("row", "col", None),
        P("row", "col", None),
        P("row", "col", None, None, None),
        P("row", "col", None, None, None),
    )
    return jax.shard_map(
        shards,
        mesh=mesh,
        in_specs=placed,
        out_specs=(cells, cells),
        check_vma=False,
    )
```

time: 168 us -> 118 us (0.70)
  waiting for transfers between devices: 96.4 us -> 41.3 us
  starting transfers between devices: 32.8 us -> 43.3 us
  local copies, waits for them, and re-layouts: 9.07 us -> 0.05 us
  Pallas kernels: 28.4 us -> 32.6 us
    ppermute x9 -> x12, waiting for transfers between devices: 44.3 us -> 10.4 us  [along(): return lax.ppermute(x, 'row', [(i, i ^ s) for i in range(n_row)])]
    ppermute x15 -> x24, waiting for transfers between devices: 50.2 us -> 27 us  [across(): return lax.ppermute(x, 'col', [(i, i ^ 2 * m) for i in range(n_col)])]
    ppermute x15 -> x24, starting transfers between devices: 19.7 us -> 29.4 us  [across(): return lax.ppermute(x, 'col', [(i, i ^ 2 * m) for i in range(n_col)])]
    unnamed x26 -> x20, local copies, waits for them, and re-layouts: 4.8 us -> 0.05 us
    pallas_call x8 -> x12, Pallas kernels: 25.3 us -> 29.1 us  [the longest x4 12 us: apply_matrix(): pl.pallas_call(functools.partial(apply_kernel, n_part, n_pair, n_row, cel...]
    optimization_barrier x3 -> x0, local copies, waits for them, and re-layouts: 2.29 us -> none  [after(): return lax.optimization_barrier((values, dep))[0]]
    ppermute x6 -> x8, waiting for transfers between devices: 1.87 us -> 3.86 us  [swap(): return lax.ppermute(x, 'col', [(i, i ^ 1) for i in range(n_col)])]
    reshape x3 -> x0, local copies, waits for them, and re-layouts: 1.99 us -> none  [shards(): t.reshape(-1)]
  transfers between devices with their start and end apart: 30 -> 44, of which waited for: 18 -> 25; matrix products, arithmetic and copies ran while one was open for 0% -> 0% of each run, Pallas kernels for 5% -> 17%
where the time goes in v3:
time: 118 us
  starting transfers between devices  43.3 us (37%)
  waiting for transfers between devices  41.3 us (35%)
  Pallas kernels  32.6 us (28%)
    ppermute x24, starting transfers between devices, across(): return lax.ppermute(x, 'col', [(i, i ^ 2 * m) for i in range(n_col)])  29.4 us
    ppermute x24, waiting for transfers between devices, across(): return lax.ppermute(x, 'col', [(i, i ^ 2 * m) for i in range(n_col)])  27 us
    ppermute x12, starting transfers between devices, along(): return lax.ppermute(x, 'row', [(i, i ^ s) for i in range(n_row)])  12 us
    pallas_call x4, Pallas kernels, apply_matrix(): pl.pallas_call(functools.partial(apply_kernel, n_part, n_pair, n_row, cel...  12 us
    ppermute x12, waiting for transfers between devices, along(): return lax.ppermute(x, 'row', [(i, i ^ s) for i in range(n_row)])  10.4 us
    pallas_call x1, Pallas kernels, build_matrix(): pl.pallas_call(functools.partial(build_kernel, first, count), out_shape=s...  10.2 us
    ppermute x8, waiting for transfers between devices, swap(): return lax.ppermute(x, 'col', [(i, i ^ 1) for i in range(n_col)])  3.86 us
    pallas_call x1, Pallas kernels, start(): pl.pallas_call(functools.partial(start_kernel, chunks), out_shape=shapes...  2.94 us
  transfers between devices with their start and end apart: 44, of which 25 were waited for; matrix products, arithmetic and copies ran while one was open for 0% of the time, Pallas kernels for 17%

profile of v3, /device:TPU:0, one launch (start us, length us, event | category | flops | bytes accessed | tf_op | source)
XLA Modules:
  0.0 118.1 jit_solution(15600332903264776799)
XLA Ops:
  0.6 2.9 %start.1 = (bf16[272,128]{1,0:T(8,128)(2,1)}, bf16[256,128]{1,0:T(8,128)(2,1)}, bf16[272,128]{1,0:T(8,128)(2,1)}, bf16[256,128]{1,0:T(8,128)(2,1)}) custom-call(s32[2]{0:T(128)} %patch_rows.1, f32[256,512]{1,0:T(8,128)} %stress, f32[256,512]{1,0:T(8,128)} %state, f32[256,512]{1,0:T(8,128)} %direct), custom_call_target="tpu_custom_call" | custom-call | flops 13107 | bytes 18350 | tf_op jit(solution)/shard_map/start/pallas_call | solution.py:310
  4.2 10.2 %build_matrix.1.refs_0_ = bf16[2048,1024]{1,0:T(8,128)(2,1)} custom-call(s32[7,1,16]{2,1,0:T(1,128)} %bitcast.5, s32[9,1,16]{2,1,0:T(1,128)} %bitcast.3, s32[9,1,16]{2,1,0:T(1,128)} %bitcast.4, bf16[16,1,7,128,128]{4,3,2,1,0:T(8,128)(2,1)} %near_in.1, bf16[16,1,9,32,128]{4,3,2,1,0:T(8,128)(2,1)} %left_in.1, bf16[16,1,9,32,128]{4,3,2,1,0:T(8,128)(2,1)} %right_in.1), custom_call_target="tpu_custom_call" | custom-call | flops 12079595 | bytes 60293 | tf_op jit(solution)/shard_map/build_matrix/pallas_call | solution.py:113
  16.4 3.9 %collective-permute-start.6 = (bf16[528,128]{1,0:T(8,128)(2,1)S(1)}, bf16[528,128]{1,0:T(8,128)(2,1)S(1)}, u32[]{:S(2)}, u32[]{:S(2)}) collective-permute-start(bf16[528,128]{1,0:T(8,128)(2,1)S(1)} %merge.2.refs_0_), channel_id=1, source_target_pairs={{0,6},{1,7},{2,4},{3,5},{4,2},{5,3},{6,0},{7,1},{8,14},{9,15},{10,... | collective-permute-start | bytes 405512 | tf_op jit(solution)/shard_map/ppermute | solution.py:506
  20.9 3.2 %collective-permute-done.2.recv = f32[2,3,256,128]{3,2,1,0:T(8,128)S(1)} collective-permute-done((f32[2,3,256,128]{3,2,1,0:T(8,128)S(1)}, f32[2,3,256,128]{3,2,1,0:T(8,128)S(1)}, u32[]{:S(2)}, u32[]{:S(2)}) %collective-permute-start.2) | collective-permute-done | bytes 786464 | tf_op jit(solution)/shard_map/ppermute | solution.py:503
  24.4 2.6 %collective-permute-done.5.refs_2_ = bf16[528,128]{1,0:T(8,128)(2,1)S(1)} collective-permute-done((bf16[528,128]{1,0:T(8,128)(2,1)S(1)}, bf16[528,128]{1,0:T(8,128)(2,1)S(1)}, u32[]{:S(2)}, u32[]{:S(2)}) %collective-permute-start.5) | collective-permute-done | bytes 135200 | tf_op jit(solution)/shard_map/ppermute | solution.py:506
  27.3 1.9 %first_pick.1 = (bf16[528,128]{1,0:T(8,128)(2,1)S(1)}, s32[4]{0:T(128)S(1)}, s32[16]{0:T(128)S(1)}) custom-call(s32[16]{0:T(128)S(1)} %copy-done.9, bf16[528,128]{1,0:T(8,128)(2,1)S(1)} %merge.2.refs_0_, bf16[528,128]{1,0:T(8,128)(2,1)S(1)} %collective-permute-done.4.refs_1_, bf16[528,128]{1,0:T(8,128)(2,1)S(1)} %collective-permute-done.5.refs_2_, ...), custom_call_target="tpu_custom_call" | custom-call | flops 10 | bytes 2703 | tf_op jit(solution)/shard_map/first_pick/pallas_call | solution.py:202
  29.2 2.6 %collective-permute-start.7 = (bf16[528,128]{1,0:T(8,128)(2,1)S(1)}, bf16[528,128]{1,0:T(8,128)(2,1)S(1)}, u32[]{:S(2)}, u32[]{:S(2)}) collective-permute-start(bf16[528,128]{1,0:T(8,128)(2,1)S(1)} %get-tuple-element.82.refs_2_), channel_id=1, source_target_pairs={{0,16},{8,24},{16,0},{24,8},{1,17},{9,25},{17,1},{25,9},{2,18},{10... | collective-permute-start | bytes 405512 | tf_op jit(solution)/shard_map/ppermute | solution.py:509
  31.9 1.8 %collective-permute-start.10 = (bf16[512,128]{1,0:T(8,128)(2,1)S(1)}, bf16[512,128]{1,0:T(8,128)(2,1)S(1)}, u32[]{:S(2)}, u32[]{:S(2)}) collective-permute-start(bf16[512,128]{1,0:T(8,128)(2,1)S(1)} %merge.3.refs_0_), channel_id=1, source_target_pairs={{0,6},{1,7},{2,4},{3,5},{4,2},{5,3},{6,0},{7,1},{8,14},{9,15},{10,... | collective-permute-start | bytes 393224 | tf_op jit(solution)/shard_map/ppermute | solution.py:506
  35.4 1.6 %collective-permute-start.11 = (bf16[528,128]{1,0:T(8,128)(2,1)S(1)}, bf16[528,128]{1,0:T(8,128)(2,1)S(1)}, u32[]{:S(2)}, u32[]{:S(2)}) collective-permute-start(bf16[528,128]{1,0:T(8,128)(2,1)S(1)} %get-tuple-element.82.refs_2_), channel_id=1, source_target_pairs={{0,8},{8,0},{16,24},{24,16},{1,9},{9,1},{17,25},{25,17},{2,10},{10... | collective-permute-start | bytes 405512 | tf_op jit(solution)/shard_map/ppermute | solution.py:509
  37.1 2.2 %collective-permute-done.10.refs_3_ = bf16[512,128]{1,0:T(8,128)(2,1)S(1)} collective-permute-done((bf16[512,128]{1,0:T(8,128)(2,1)S(1)}, bf16[512,128]{1,0:T(8,128)(2,1)S(1)}, u32[]{:S(2)}, u32[]{:S(2)}) %collective-permute-start.10) | collective-permute-done | bytes 131104 | tf_op jit(solution)/shard_map/ppermute | solution.py:506
  40.8 1.6 %collective-permute-start.12 = (bf16[528,128]{1,0:T(8,128)(2,1)S(1)}, bf16[528,128]{1,0:T(8,128)(2,1)S(1)}, u32[]{:S(2)}, u32[]{:S(2)}) collective-permute-start(bf16[528,128]{1,0:T(8,128)(2,1)S(1)} %collective-permute-done.7.refs_3_), channel_id=1, source_target_pairs={{0,8},{8,0},{16,24},{24,16},{1,9},{9,1},{17,25},{25,17},{2,10},{10... | collective-permute-start | bytes 405512 | tf_op jit(solution)/shard_map/ppermute | solution.py:509
  42.4 3.4 %collective-permute-done.12.refs_5_ = bf16[528,128]{1,0:T(8,128)(2,1)S(1)} collective-permute-done((bf16[528,128]{1,0:T(8,128)(2,1)S(1)}, bf16[528,128]{1,0:T(8,128)(2,1)S(1)}, u32[]{:S(2)}, u32[]{:S(2)}) %collective-permute-start.12) | collective-permute-done | bytes 135200 | tf_op jit(solution)/shard_map/ppermute | solution.py:509
  45.8 3.1 %apply_matrix.4 = (f32[512,128]{1,0:T(8,128)S(1)}, bf16[512,128]{1,0:T(8,128)(2,1)S(1)}, bf16[512,128]{1,0:T(8,128)(2,1)S(1)}, bf16[512,128]{1,0:T(8,128)(2,1)S(1)}, s32[16]{0:T(128)S(1)}) custom-call(bf16[2048,1024]{1,0:T(8,128)(2,1)S(1)} %copy-done, bf16[2048,1024]{1,0:T(8,128)(2,1)S(1)} %collective-permute-done.3.refs_1_, ...), custom_call_target="tpu_custom_call" | custom-call | flops 10737418 | bytes 83886 | tf_op jit(solution)/shard_map/apply_matrix/pallas_call | solution.py:258
  49.0 1.9 %collective-permute-start.13 = (bf16[512,128]{1,0:T(8,128)(2,1)S(1)}, bf16[512,128]{1,0:T(8,128)(2,1)S(1)}, u32[]{:S(2)}, u32[]{:S(2)}) collective-permute-start(bf16[512,128]{1,0:T(8,128)(2,1)S(1)} %get-tuple-element.89), channel_id=1, source_target_pairs={{0,2},{1,3},{2,0},{3,1},{4,6},{5,7},{6,4},{7,5},{8,10},{9,11},{10,... | collective-permute-start | bytes 393224 | tf_op jit(solution)/shard_map/ppermute | solution.py:506
  50.9 1.6 %collective-permute-start.15 = (bf16[512,128]{1,0:T(8,128)(2,1)S(1)}, bf16[512,128]{1,0:T(8,128)(2,1)S(1)}, u32[]{:S(2)}, u32[]{:S(2)}) collective-permute-start(bf16[512,128]{1,0:T(8,128)(2,1)S(1)} %get-tuple-element.91), channel_id=1, source_target_pairs={{0,6},{1,7},{2,4},{3,5},{4,2},{5,3},{6,0},{7,1},{8,14},{9,15},{10,... | collective-permute-start | bytes 393224 | tf_op jit(solution)/shard_map/ppermute | solution.py:506
  54.5 3.4 %collective-permute-done.14.refs_2_ = bf16[512,128]{1,0:T(8,128)(2,1)S(1)} collective-permute-done((bf16[512,128]{1,0:T(8,128)(2,1)S(1)}, bf16[512,128]{1,0:T(8,128)(2,1)S(1)}, u32[]{:S(2)}, u32[]{:S(2)}) %collective-permute-start.14) | collective-permute-done | bytes 131104 | tf_op jit(solution)/shard_map/ppermute | solution.py:506
  58.1 1.5 %collective-permute-start.18 = (bf16[512,128]{1,0:T(8,128)(2,1)S(1)}, bf16[512,128]{1,0:T(8,128)(2,1)S(1)}, u32[]{:S(2)}, u32[]{:S(2)}) collective-permute-start(bf16[512,128]{1,0:T(8,128)(2,1)S(1)} %get-tuple-element.94.refs_0_), channel_id=1, source_target_pairs={{0,6},{1,7},{2,4},{3,5},{4,2},{5,3},{6,0},{7,1},{8,14},{9,15},{10,... | collective-permute-start | bytes 393224 | tf_op jit(solution)/shard_map/ppermute | solution.py:506
  61.7 1.7 %collective-permute-start.26 = (bf16[512,128]{1,0:T(8,128)(2,1)S(1)}, bf16[512,128]{1,0:T(8,128)(2,1)S(1)}, u32[]{:S(2)}, u32[]{:S(2)}) collective-permute-start(bf16[512,128]{1,0:T(8,128)(2,1)S(1)} %pick.4.refs_2_), channel_id=1, source_target_pairs={{0,8},{8,0},{16,24},{24,16},{1,9},{9,1},{17,25},{25,17},{2,10},{10... | collective-permute-start | bytes 393224 | tf_op jit(solution)/shard_map/ppermute | solution.py:509
  68.0 1.5 %collective-permute-done.27.refs_5_ = bf16[512,128]{1,0:T(8,128)(2,1)S(1)} collective-permute-done((bf16[512,128]{1,0:T(8,128)(2,1)S(1)}, bf16[512,128]{1,0:T(8,128)(2,1)S(1)}, u32[]{:S(2)}, u32[]{:S(2)}) %collective-permute-start.27) | collective-permute-done | bytes 131104 | tf_op jit(solution)/shard_map/ppermute | solution.py:509
  69.4 2.9 %apply_matrix.6 = (f32[512,128]{1,0:T(8,128)S(1)}, bf16[512,128]{1,0:T(8,128)(2,1)S(1)}, bf16[512,128]{1,0:T(8,128)(2,1)S(1)}, bf16[512,128]{1,0:T(8,128)(2,1)S(1)}) custom-call(bf16[2048,1024]{1,0:T(8,128)(2,1)S(1)} %copy-done, bf16[2048,1024]{1,0:T(8,128)(2,1)S(1)} %collective-permute-done.3.refs_1_, bf16[512,128]{1,0:T(8,128)(2,1)S(1)} %pick.4.refs_2_, ...), custom_call_target="tpu_custom_call" | custom-call | flops 10737418 | bytes 83886 | tf_op jit(solution)/shard_map/apply_matrix/pallas_call | solution.py:258
  74.5 1.5 %collective-permute-start.30 = (bf16[512,128]{1,0:T(8,128)(2,1)S(1)}, bf16[512,128]{1,0:T(8,128)(2,1)S(1)}, u32[]{:S(2)}, u32[]{:S(2)}) collective-permute-start(bf16[512,128]{1,0:T(8,128)(2,1)S(1)} %get-tuple-element.107), channel_id=1, source_target_pairs={{0,6},{1,7},{2,4},{3,5},{4,2},{5,3},{6,0},{7,1},{8,14},{9,15},{10,... | collective-permute-start | bytes 393224 | tf_op jit(solution)/shard_map/ppermute | solution.py:506
  76.5 1.5 %collective-permute-start.21 = (bf16[512,128]{1,0:T(8,128)(2,1)S(1)}, bf16[512,128]{1,0:T(8,128)(2,1)S(1)}, u32[]{:S(2)}, u32[]{:S(2)}) collective-permute-start(bf16[512,128]{1,0:T(8,128)(2,1)S(1)} %collective-permute-done.19.refs_3_), channel_id=1, source_target_pairs={{0,8},{8,0},{16,24},{24,16},{1,9},{9,1},{17,25},{25,17},{2,10},{10... | collective-permute-start | bytes 393224 | tf_op jit(solution)/shard_map/ppermute | solution.py:509
  78.0 4.1 %collective-permute-done.29.refs_2_ = bf16[512,128]{1,0:T(8,128)(2,1)S(1)} collective-permute-done((bf16[512,128]{1,0:T(8,128)(2,1)S(1)}, bf16[512,128]{1,0:T(8,128)(2,1)S(1)}, u32[]{:S(2)}, u32[]{:S(2)}) %collective-permute-start.29) | collective-permute-done | bytes 131104 | tf_op jit(solution)/shard_map/ppermute | solution.py:506
  82.2 1.5 %collective-permute-start.33 = (bf16[512,128]{1,0:T(8,128)(2,1)S(1)}, bf16[512,128]{1,0:T(8,128)(2,1)S(1)}, u32[]{:S(2)}, u32[]{:S(2)}) collective-permute-start(bf16[512,128]{1,0:T(8,128)(2,1)S(1)} %get-tuple-element.110.refs_0_), channel_id=1, source_target_pairs={{0,6},{1,7},{2,4},{3,5},{4,2},{5,3},{6,0},{7,1},{8,14},{9,15},{10,... | collective-permute-start | bytes 393224 | tf_op jit(solution)/shard_map/ppermute | solution.py:506
  85.8 2.9 %apply_matrix.5 = (f32[512,128]{1,0:T(8,128)S(1)}, bf16[512,128]{1,0:T(8,128)(2,1)S(1)}, bf16[512,128]{1,0:T(8,128)(2,1)S(1)}, bf16[512,128]{1,0:T(8,128)(2,1)S(1)}) custom-call(bf16[2048,1024]{1,0:T(8,128)(2,1)S(1)} %copy-done, bf16[2048,1024]{1,0:T(8,128)(2,1)S(1)} %collective-permute-done.3.refs_1_, bf16[512,128]{1,0:T(8,128)(2,1)S(1)} %pick.3.refs_2_, ...), custom_call_target="tpu_custom_call" | custom-call | flops 10737418 | bytes 83886 | tf_op jit(solution)/shard_map/apply_matrix/pallas_call | solution.py:258
  89.5 2.8 %collective-permute-done.32.refs_2_ = bf16[512,128]{1,0:T(8,128)(2,1)S(1)} collective-permute-done((bf16[512,128]{1,0:T(8,128)(2,1)S(1)}, bf16[512,128]{1,0:T(8,128)(2,1)S(1)}, u32[]{:S(2)}, u32[]{:S(2)}) %collective-permute-start.32) | collective-permute-done | bytes 131104 | tf_op jit(solution)/shard_map/ppermute | solution.py:506
  95.0 1.6 %collective-permute-start.24 = (bf16[512,128]{1,0:T(8,128)(2,1)S(1)}, bf16[512,128]{1,0:T(8,128)(2,1)S(1)}, u32[]{:S(2)}, u32[]{:S(2)}) collective-permute-start(bf16[512,128]{1,0:T(8,128)(2,1)S(1)} %get-tuple-element.99), channel_id=1, source_target_pairs={{0,6},{1,7},{2,4},{3,5},{4,2},{5,3},{6,0},{7,1},{8,14},{9,15},{10,... | collective-permute-start | bytes 393224 | tf_op jit(solution)/shard_map/ppermute | solution.py:506
  97.3 2.3 %collective-permute-done.34.refs_3_ = bf16[512,128]{1,0:T(8,128)(2,1)S(1)} collective-permute-done((bf16[512,128]{1,0:T(8,128)(2,1)S(1)}, bf16[512,128]{1,0:T(8,128)(2,1)S(1)}, u32[]{:S(2)}, u32[]{:S(2)}) %collective-permute-start.34) | collective-permute-done | bytes 131104 | tf_op jit(solution)/shard_map/ppermute | solution.py:509
  99.7 2.7 %collective-permute-done.24.refs_3_ = bf16[512,128]{1,0:T(8,128)(2,1)S(1)} collective-permute-done((bf16[512,128]{1,0:T(8,128)(2,1)S(1)}, bf16[512,128]{1,0:T(8,128)(2,1)S(1)}, u32[]{:S(2)}, u32[]{:S(2)}) %collective-permute-start.24) | collective-permute-done | bytes 131104 | tf_op jit(solution)/shard_map/ppermute | solution.py:506
  102.5 2.1 %collective-permute-done.36.refs_5_ = bf16[512,128]{1,0:T(8,128)(2,1)S(1)} collective-permute-done((bf16[512,128]{1,0:T(8,128)(2,1)S(1)}, bf16[512,128]{1,0:T(8,128)(2,1)S(1)}, u32[]{:S(2)}, u32[]{:S(2)}) %collective-permute-start.36) | collective-permute-done | bytes 131104 | tf_op jit(solution)/shard_map/ppermute | solution.py:509
  104.6 2.9 %apply_matrix.7 = (f32[512,128]{1,0:T(8,128)S(1)}, bf16[512,128]{1,0:T(8,128)(2,1)S(1)}, bf16[512,128]{1,0:T(8,128)(2,1)S(1)}, bf16[512,128]{1,0:T(8,128)(2,1)S(1)}) custom-call(bf16[2048,1024]{1,0:T(8,128)(2,1)S(1)} %copy-done, bf16[2048,1024]{1,0:T(8,128)(2,1)S(1)} %collective-permute-done.3.refs_1_, bf16[512,128]{1,0:T(8,128)(2,1)S(1)} %pick.5.refs_2_, ...), custom_call_target="tpu_custom_call" | custom-call | flops 10737418 | bytes 83886 | tf_op jit(solution)/shard_map/apply_matrix/pallas_call | solution.py:258
  113.5 2.2 %collective-permute-done.39.refs_3_ = bf16[512,128]{1,0:T(8,128)(2,1)S(1)} collective-permute-done((bf16[512,128]{1,0:T(8,128)(2,1)S(1)}, bf16[512,128]{1,0:T(8,128)(2,1)S(1)}, u32[]{:S(2)}, u32[]{:S(2)}) %collective-permute-start.39) | collective-permute-done | bytes 131104 | tf_op jit(solution)/shard_map/ppermute | solution.py:506
  (95 shorter events, 33.4 us)
Async XLA Ops:
  3.6 12.1 %collective-permute-start = (bf16[272,128]{1,0:T(8,128)(2,1)}, bf16[272,128]{1,0:T(8,128)(2,1)S(1)}, u32[]{:S(2)}, u32[]{:S(2)}) collective-permute-start(bf16[272,128]{1,0:T(8,128)(2,1)} %get-tuple-element.63), channel_id=1, source_target_pairs={{0,1},{1,0},{2,3},{3,2},{4,5},{5,4},{6,7},{7,6},{8,9},{9,8},{10,11... | collective-permute-start | bytes 208904 | tf_op jit(solution)/shard_map/ppermute | solution.py:503
  4.1 11.5 %collective-permute-start.1 = (bf16[256,128]{1,0:T(8,128)(2,1)}, bf16[256,128]{1,0:T(8,128)(2,1)S(1)}, u32[]{:S(2)}, u32[]{:S(2)}) collective-permute-start(bf16[256,128]{1,0:T(8,128)(2,1)} %get-tuple-element.75), channel_id=1, source_target_pairs={{0,1},{1,0},{2,3},{3,2},{4,5},{5,4},{6,7},{7,6},{8,9},{9,8},{10,11... | collective-permute-start | bytes 196616 | tf_op jit(solution)/shard_map/ppermute | solution.py:503
  15.6 8.8 %collective-permute-start.3 = (bf16[2048,1024]{1,0:T(8,128)(2,1)}, bf16[2048,1024]{1,0:T(8,128)(2,1)S(1)}, u32[]{:S(2)}, u32[]{:S(2)}) collective-permute-start(bf16[2048,1024]{1,0:T(8,128)(2,1)} %build_matrix.1.refs_0_), channel_id=1, source_target_pairs={{0,1},{1,0},{2,3},{3,2},{4,5},{5,4},{6,7},{7,6},{8,9},{9,8},{10,11... | collective-permute-start | bytes 12582920 | tf_op jit(solution)/shard_map/ppermute | solution.py:503
  16.3 7.8 %collective-permute-start.2 = (f32[2,3,256,128]{3,2,1,0:T(8,128)S(1)}, f32[2,3,256,128]{3,2,1,0:T(8,128)S(1)}, u32[]{:S(2)}, u32[]{:S(2)}) collective-permute-start(f32[2,3,256,128]{3,2,1,0:T(8,128)S(1)} %get-tuple-element.77), channel_id=1, source_target_pairs={{0,1},{1,0},{2,3},{3,2},{4,5},{5,4},{6,7},{7,6},{8,9},{9,8},{10,11... | collective-permute-start | bytes 2359304 | tf_op jit(solution)/shard_map/ppermute | solution.py:503
  16.4 8.0 %collective-permute-start.6 = (bf16[528,128]{1,0:T(8,128)(2,1)S(1)}, bf16[528,128]{1,0:T(8,128)(2,1)S(1)}, u32[]{:S(2)}, u32[]{:S(2)}) collective-permute-start(bf16[528,128]{1,0:T(8,128)(2,1)S(1)} %merge.2.refs_0_), channel_id=1, source_target_pairs={{0,6},{1,7},{2,4},{3,5},{4,2},{5,3},{6,0},{7,1},{8,14},{9,15},{10,... | collective-permute-start | bytes 405512 | tf_op jit(solution)/shard_map/ppermute | solution.py:506
  20.3 6.8 %collective-permute-start.5 = (bf16[528,128]{1,0:T(8,128)(2,1)S(1)}, bf16[528,128]{1,0:T(8,128)(2,1)S(1)}, u32[]{:S(2)}, u32[]{:S(2)}) collective-permute-start(bf16[528,128]{1,0:T(8,128)(2,1)S(1)} %merge.2.refs_0_), channel_id=1, source_target_pairs={{0,4},{1,5},{2,6},{3,7},{4,0},{5,1},{6,2},{7,3},{8,12},{9,13},{10,... | collective-permute-start | bytes 405512 | tf_op jit(solution)/shard_map/ppermute | solution.py:506
  20.7 6.6 %collective-permute-start.4 = (bf16[528,128]{1,0:T(8,128)(2,1)S(1)}, bf16[528,128]{1,0:T(8,128)(2,1)S(1)}, u32[]{:S(2)}, u32[]{:S(2)}) collective-permute-start(bf16[528,128]{1,0:T(8,128)(2,1)S(1)} %merge.2.refs_0_), channel_id=1, source_target_pairs={{0,2},{1,3},{2,0},{3,1},{4,6},{5,7},{6,4},{7,5},{8,10},{9,11},{10,... | collective-permute-start | bytes 405512 | tf_op jit(solution)/shard_map/ppermute | solution.py:506
  29.2 11.5 %collective-permute-start.7 = (bf16[528,128]{1,0:T(8,128)(2,1)S(1)}, bf16[528,128]{1,0:T(8,128)(2,1)S(1)}, u32[]{:S(2)}, u32[]{:S(2)}) collective-permute-start(bf16[528,128]{1,0:T(8,128)(2,1)S(1)} %get-tuple-element.82.refs_2_), channel_id=1, source_target_pairs={{0,16},{8,24},{16,0},{24,8},{1,17},{9,25},{17,1},{25,9},{2,18},{10... | collective-permute-start | bytes 405512 | tf_op jit(solution)/shard_map/ppermute | solution.py:509
  31.9 7.4 %collective-permute-start.10 = (bf16[512,128]{1,0:T(8,128)(2,1)S(1)}, bf16[512,128]{1,0:T(8,128)(2,1)S(1)}, u32[]{:S(2)}, u32[]{:S(2)}) collective-permute-start(bf16[512,128]{1,0:T(8,128)(2,1)S(1)} %merge.3.refs_0_), channel_id=1, source_target_pairs={{0,6},{1,7},{2,4},{3,5},{4,2},{5,3},{6,0},{7,1},{8,14},{9,15},{10,... | collective-permute-start | bytes 393224 | tf_op jit(solution)/shard_map/ppermute | solution.py:506
  33.6 7.0 %collective-permute-start.9 = (bf16[512,128]{1,0:T(8,128)(2,1)S(1)}, bf16[512,128]{1,0:T(8,128)(2,1)S(1)}, u32[]{:S(2)}, u32[]{:S(2)}) collective-permute-start(bf16[512,128]{1,0:T(8,128)(2,1)S(1)} %merge.3.refs_0_), channel_id=1, source_target_pairs={{0,4},{1,5},{2,6},{3,7},{4,0},{5,1},{6,2},{7,3},{8,12},{9,13},{10,... | collective-permute-start | bytes 393224 | tf_op jit(solution)/shard_map/ppermute | solution.py:506
  34.9 5.9 %collective-permute-start.8 = (bf16[512,128]{1,0:T(8,128)(2,1)S(1)}, bf16[512,128]{1,0:T(8,128)(2,1)S(1)}, u32[]{:S(2)}, u32[]{:S(2)}) collective-permute-start(bf16[512,128]{1,0:T(8,128)(2,1)S(1)} %merge.3.refs_0_), channel_id=1, source_target_pairs={{0,2},{1,3},{2,0},{3,1},{4,6},{5,7},{6,4},{7,5},{8,10},{9,11},{10,... | collective-permute-start | bytes 393224 | tf_op jit(solution)/shard_map/ppermute | solution.py:506
  35.4 7.0 %collective-permute-start.11 = (bf16[528,128]{1,0:T(8,128)(2,1)S(1)}, bf16[528,128]{1,0:T(8,128)(2,1)S(1)}, u32[]{:S(2)}, u32[]{:S(2)}) collective-permute-start(bf16[528,128]{1,0:T(8,128)(2,1)S(1)} %get-tuple-element.82.refs_2_), channel_id=1, source_target_pairs={{0,8},{8,0},{16,24},{24,16},{1,9},{9,1},{17,25},{25,17},{2,10},{10... | collective-permute-start | bytes 405512 | tf_op jit(solution)/shard_map/ppermute | solution.py:509
  50.8 7.1 %collective-permute-start.14 = (bf16[512,128]{1,0:T(8,128)(2,1)S(1)}, bf16[512,128]{1,0:T(8,128)(2,1)S(1)}, u32[]{:S(2)}, u32[]{:S(2)}) collective-permute-start(bf16[512,128]{1,0:T(8,128)(2,1)S(1)} %get-tuple-element.90), channel_id=1, source_target_pairs={{0,4},{1,5},{2,6},{3,7},{4,0},{5,1},{6,2},{7,3},{8,12},{9,13},{10,... | collective-permute-start | bytes 393224 | tf_op jit(solution)/shard_map/ppermute | solution.py:506
  50.9 7.0 %collective-permute-start.15 = (bf16[512,128]{1,0:T(8,128)(2,1)S(1)}, bf16[512,128]{1,0:T(8,128)(2,1)S(1)}, u32[]{:S(2)}, u32[]{:S(2)}) collective-permute-start(bf16[512,128]{1,0:T(8,128)(2,1)S(1)} %get-tuple-element.91), channel_id=1, source_target_pairs={{0,6},{1,7},{2,4},{3,5},{4,2},{5,3},{6,0},{7,1},{8,14},{9,15},{10,... | collective-permute-start | bytes 393224 | tf_op jit(solution)/shard_map/ppermute | solution.py:506
  53.2 10.2 %collective-permute-start.25 = (bf16[512,128]{1,0:T(8,128)(2,1)S(1)}, bf16[512,128]{1,0:T(8,128)(2,1)S(1)}, u32[]{:S(2)}, u32[]{:S(2)}) collective-permute-start(bf16[512,128]{1,0:T(8,128)(2,1)S(1)} %pick.4.refs_2_), channel_id=1, source_target_pairs={{0,16},{8,24},{16,0},{24,8},{1,17},{9,25},{17,1},{25,9},{2,18},{10... | collective-permute-start | bytes 393224 | tf_op jit(solution)/shard_map/ppermute | solution.py:509
  58.1 6.0 %collective-permute-start.18 = (bf16[512,128]{1,0:T(8,128)(2,1)S(1)}, bf16[512,128]{1,0:T(8,128)(2,1)S(1)}, u32[]{:S(2)}, u32[]{:S(2)}) collective-permute-start(bf16[512,128]{1,0:T(8,128)(2,1)S(1)} %get-tuple-element.94.refs_0_), channel_id=1, source_target_pairs={{0,6},{1,7},{2,4},{3,5},{4,2},{5,3},{6,0},{7,1},{8,14},{9,15},{10,... | collective-permute-start | bytes 393224 | tf_op jit(solution)/shard_map/ppermute | solution.py:506
  59.6 5.8 %collective-permute-start.17 = (bf16[512,128]{1,0:T(8,128)(2,1)S(1)}, bf16[512,128]{1,0:T(8,128)(2,1)S(1)}, u32[]{:S(2)}, u32[]{:S(2)}) collective-permute-start(bf16[512,128]{1,0:T(8,128)(2,1)S(1)} %get-tuple-element.94.refs_0_), channel_id=1, source_target_pairs={{0,4},{1,5},{2,6},{3,7},{4,0},{5,1},{6,2},{7,3},{8,12},{9,13},{10,... | collective-permute-start | bytes 393224 | tf_op jit(solution)/shard_map/ppermute | solution.py:506
  61.7 6.3 %collective-permute-start.26 = (bf16[512,128]{1,0:T(8,128)(2,1)S(1)}, bf16[512,128]{1,0:T(8,128)(2,1)S(1)}, u32[]{:S(2)}, u32[]{:S(2)}) collective-permute-start(bf16[512,128]{1,0:T(8,128)(2,1)S(1)} %pick.4.refs_2_), channel_id=1, source_target_pairs={{0,8},{8,0},{16,24},{24,16},{1,9},{9,1},{17,25},{25,17},{2,10},{10... | collective-permute-start | bytes 393224 | tf_op jit(solution)/shard_map/ppermute | solution.py:509
  63.4 6.1 %collective-permute-start.27 = (bf16[512,128]{1,0:T(8,128)(2,1)S(1)}, bf16[512,128]{1,0:T(8,128)(2,1)S(1)}, u32[]{:S(2)}, u32[]{:S(2)}) collective-permute-start(bf16[512,128]{1,0:T(8,128)(2,1)S(1)} %collective-permute-done.25.refs_3_), channel_id=1, source_target_pairs={{0,8},{8,0},{16,24},{24,16},{1,9},{9,1},{17,25},{25,17},{2,10},{10... | collective-permute-start | bytes 393224 | tf_op jit(solution)/shard_map/ppermute | solution.py:509
  66.3 10.1 %collective-permute-start.19 = (bf16[512,128]{1,0:T(8,128)(2,1)S(1)}, bf16[512,128]{1,0:T(8,128)(2,1)S(1)}, u32[]{:S(2)}, u32[]{:S(2)}) collective-permute-start(bf16[512,128]{1,0:T(8,128)(2,1)S(1)} %pick.3.refs_2_), channel_id=1, source_target_pairs={{0,16},{8,24},{16,0},{24,8},{1,17},{9,25},{17,1},{25,9},{2,18},{10... | collective-permute-start | bytes 393224 | tf_op jit(solution)/shard_map/ppermute | solution.py:509
  73.4 8.7 %collective-permute-start.29 = (bf16[512,128]{1,0:T(8,128)(2,1)S(1)}, bf16[512,128]{1,0:T(8,128)(2,1)S(1)}, u32[]{:S(2)}, u32[]{:S(2)}) collective-permute-start(bf16[512,128]{1,0:T(8,128)(2,1)S(1)} %get-tuple-element.106), channel_id=1, source_target_pairs={{0,4},{1,5},{2,6},{3,7},{4,0},{5,1},{6,2},{7,3},{8,12},{9,13},{10,... | collective-permute-start | bytes 393224 | tf_op jit(solution)/shard_map/ppermute | solution.py:506
  74.5 7.6 %collective-permute-start.30 = (bf16[512,128]{1,0:T(8,128)(2,1)S(1)}, bf16[512,128]{1,0:T(8,128)(2,1)S(1)}, u32[]{:S(2)}, u32[]{:S(2)}) collective-permute-start(bf16[512,128]{1,0:T(8,128)(2,1)S(1)} %get-tuple-element.107), channel_id=1, source_target_pairs={{0,6},{1,7},{2,4},{3,5},{4,2},{5,3},{6,0},{7,1},{8,14},{9,15},{10,... | collective-permute-start | bytes 393224 | tf_op jit(solution)/shard_map/ppermute | solution.py:506
  75.9 9.8 %collective-permute-start.20 = (bf16[512,128]{1,0:T(8,128)(2,1)S(1)}, bf16[512,128]{1,0:T(8,128)(2,1)S(1)}, u32[]{:S(2)}, u32[]{:S(2)}) collective-permute-start(bf16[512,128]{1,0:T(8,128)(2,1)S(1)} %pick.3.refs_2_), channel_id=1, source_target_pairs={{0,8},{8,0},{16,24},{24,16},{1,9},{9,1},{17,25},{25,17},{2,10},{10... | collective-permute-start | bytes 393224 | tf_op jit(solution)/shard_map/ppermute | solution.py:509
  76.5 9.3 %collective-permute-start.21 = (bf16[512,128]{1,0:T(8,128)(2,1)S(1)}, bf16[512,128]{1,0:T(8,128)(2,1)S(1)}, u32[]{:S(2)}, u32[]{:S(2)}) collective-permute-start(bf16[512,128]{1,0:T(8,128)(2,1)S(1)} %collective-permute-done.19.refs_3_), channel_id=1, source_target_pairs={{0,8},{8,0},{16,24},{24,16},{1,9},{9,1},{17,25},{25,17},{2,10},{10... | collective-permute-start | bytes 393224 | tf_op jit(solution)/shard_map/ppermute | solution.py:509
  82.2 7.3 %collective-permute-start.33 = (bf16[512,128]{1,0:T(8,128)(2,1)S(1)}, bf16[512,128]{1,0:T(8,128)(2,1)S(1)}, u32[]{:S(2)}, u32[]{:S(2)}) collective-permute-start(bf16[512,128]{1,0:T(8,128)(2,1)S(1)} %get-tuple-element.110.refs_0_), channel_id=1, source_target_pairs={{0,6},{1,7},{2,4},{3,5},{4,2},{5,3},{6,0},{7,1},{8,14},{9,15},{10,... | collective-permute-start | bytes 393224 | tf_op jit(solution)/shard_map/ppermute | solution.py:506
  83.7 8.6 %collective-permute-start.32 = (bf16[512,128]{1,0:T(8,128)(2,1)S(1)}, bf16[512,128]{1,0:T(8,128)(2,1)S(1)}, u32[]{:S(2)}, u32[]{:S(2)}) collective-permute-start(bf16[512,128]{1,0:T(8,128)(2,1)S(1)} %get-tuple-element.110.refs_0_), channel_id=1, source_target_pairs={{0,4},{1,5},{2,6},{3,7},{4,0},{5,1},{6,2},{7,3},{8,12},{9,13},{10,... | collective-permute-start | bytes 393224 | tf_op jit(solution)/shard_map/ppermute | solution.py:506
  84.8 7.5 %collective-permute-start.31 = (bf16[512,128]{1,0:T(8,128)(2,1)S(1)}, bf16[512,128]{1,0:T(8,128)(2,1)S(1)}, u32[]{:S(2)}, u32[]{:S(2)}) collective-permute-start(bf16[512,128]{1,0:T(8,128)(2,1)S(1)} %get-tuple-element.110.refs_0_), channel_id=1, source_target_pairs={{0,2},{1,3},{2,0},{3,1},{4,6},{5,7},{6,4},{7,5},{8,10},{9,11},{10,... | collective-permute-start | bytes 393224 | tf_op jit(solution)/shard_map/ppermute | solution.py:506
  93.0 6.7 %collective-permute-start.34 = (bf16[512,128]{1,0:T(8,128)(2,1)S(1)}, bf16[512,128]{1,0:T(8,128)(2,1)S(1)}, u32[]{:S(2)}, u32[]{:S(2)}) collective-permute-start(bf16[512,128]{1,0:T(8,128)(2,1)S(1)} %pick.5.refs_2_), channel_id=1, source_target_pairs={{0,16},{8,24},{16,0},{24,8},{1,17},{9,25},{17,1},{25,9},{2,18},{10... | collective-permute-start | bytes 393224 | tf_op jit(solution)/shard_map/ppermute | solution.py:509
  93.0 6.6 %collective-permute-start.22 = (bf16[512,128]{1,0:T(8,128)(2,1)S(1)}, bf16[512,128]{1,0:T(8,128)(2,1)S(1)}, u32[]{:S(2)}, u32[]{:S(2)}) collective-permute-start(bf16[512,128]{1,0:T(8,128)(2,1)S(1)} %get-tuple-element.97), channel_id=1, source_target_pairs={{0,2},{1,3},{2,0},{3,1},{4,6},{5,7},{6,4},{7,5},{8,10},{9,11},{10,... | collective-permute-start | bytes 393224 | tf_op jit(solution)/shard_map/ppermute | solution.py:506
  95.0 7.4 %collective-permute-start.24 = (bf16[512,128]{1,0:T(8,128)(2,1)S(1)}, bf16[512,128]{1,0:T(8,128)(2,1)S(1)}, u32[]{:S(2)}, u32[]{:S(2)}) collective-permute-start(bf16[512,128]{1,0:T(8,128)(2,1)S(1)} %get-tuple-element.99), channel_id=1, source_target_pairs={{0,6},{1,7},{2,4},{3,5},{4,2},{5,3},{6,0},{7,1},{8,14},{9,15},{10,... | collective-permute-start | bytes 393224 | tf_op jit(solution)/shard_map/ppermute | solution.py:506
  96.6 5.9 %collective-permute-start.35 = (bf16[512,128]{1,0:T(8,128)(2,1)S(1)}, bf16[512,128]{1,0:T(8,128)(2,1)S(1)}, u32[]{:S(2)}, u32[]{:S(2)}) collective-permute-start(bf16[512,128]{1,0:T(8,128)(2,1)S(1)} %pick.5.refs_2_), channel_id=1, source_target_pairs={{0,8},{8,0},{16,24},{24,16},{1,9},{9,1},{17,25},{25,17},{2,10},{10... | collective-permute-start | bytes 393224 | tf_op jit(solution)/shard_map/ppermute | solution.py:509
  109.9 5.9 %collective-permute-start.39 = (bf16[512,128]{1,0:T(8,128)(2,1)S(1)}, bf16[512,128]{1,0:T(8,128)(2,1)S(1)}, u32[]{:S(2)}, u32[]{:S(2)}) collective-permute-start(bf16[512,128]{1,0:T(8,128)(2,1)S(1)} %get-tuple-element.115), channel_id=1, source_target_pairs={{0,6},{1,7},{2,4},{3,5},{4,2},{5,3},{6,0},{7,1},{8,14},{9,15},{10,... | collective-permute-start | bytes 393224 | tf_op jit(solution)/shard_map/ppermute | solution.py:506
  (22 other events, 212.7 us)

commit v4 on v3

--- a/solution.py
+++ b/solution.py
@@ -514,19 +514,15 @@
     high = stress.shape[0]
     started = start(patch_rows, stress, friction_state, direct, CHUNKS)
     keep_first, give_first = started[:CHUNKS], started[CHUNKS:]
-    tables = after([t.transpose(2, 1, 0) for t in (near_cols, far_cols, far_ranks)], give_first[0])
+    recv_first = lax.optimization_barrier([swap(give) for give in give_first])
+    vel_first = merge(keep_first[0], recv_first[0], high)
+    tables = after([t.transpose(2, 1, 0) for t in (near_cols, far_cols, far_ranks)], vel_first)
     factors = (near_blocks, far_left, far_right)
     unit = rows_dev // sum(SHARES)
     m_own, first_row = [], 0
     for share in SHARES:
         m_own.append(build_matrix(tables, factors, width, first_row, share * unit))
         first_row += share * unit
-    recv_first = [swap(give) for give in give_first]
-    held = (stress, friction_state, direct, evolve, relax_rate, load_rate)
-    keep_mid, give_mid, base, state_base = mid(*after(held, m_own), CHUNKS)
-    recv_first, m_own, give_mid = lax.optimization_barrier((recv_first, m_own, give_mid))
-    m_sib = [swap(m) for m in m_own]
-    recv_mid = swap(give_mid)
 
     def spread(vel_b):
         return [vel_b] + [across(vel_b, m) for m in range(1, n_pair)]
@@ -534,27 +530,38 @@
     def gather(chosen, dep=None):
         pieces, step = [chosen], n_row // 2
         while step:
-            sent = [along(piece, step) for piece in pieces]
+            sent = [along(pieces[0], step)]
             if dep is not None:
                 sent, dep = after(sent, dep), None
+            sent += [along(after(piece, sent[0]), step) for piece in pieces[1:]]
             pieces = pieces + sent
             step //= 2
         return pieces
 
+    def gather_flat(chosen):
+        order, step = [0], n_row // 2
+        while step:
+            order, step = order + [way ^ step for way in order], step // 2
+        return [chosen] + [along(chosen, way) for way in order[1:]]
+
     def reduce(partial):
         return [partial[0]] + [across(partial[m], m) for m in range(1, n_pair)]
 
     n = CHUNKS
-    sources = spread(merge(keep_first[0], recv_first[0], high))
-    perm = after(row_perm, (m_sib, recv_mid))
+    sources = spread(vel_first)
+    perm = after(row_perm, m_own)
     chosen, sel, rows = first_pick(perm, sources, cell, width, patch_count)
+    m_sib = [swap(after(m, chosen)) for m in m_own]
+    held = (stress, friction_state, direct, evolve, relax_rate, load_rate)
+    keep_mid, give_mid, base, state_base = mid(*after(held, chosen), CHUNKS)
+    recv_mid = swap(give_mid)
     picked, arrived, partials, ids, dep = [chosen], [], [], None, chosen
     for j in range(1, n):
-        sources = spread(merge(keep_first[j], after(recv_first[j], dep), high))
-        arrived.append(gather(picked[-1], sources[1:]))
+        arrived.append(gather(picked[-1]))
+        sources = spread(merge(keep_first[j], after(recv_first[j], arrived[-1][1]), high))
         partials.append(apply_matrix(m_own, m_sib, arrived[-1], rows, ids, cell, patch_count))
         ids = partials[-1][-1] if ids is None else ids
-        picked.append(pick(after(sel, partials[-1][0]), sources, cell))
+        picked.append(pick(after(sel, (partials[-1][0], recv_mid)), sources, cell))
         dep = picked[-1]
     arrived.append(gather(picked[-1]))
     firsts, vel_keeps, vel_recvs, keeps, recvs = [], [], [], [], []
@@ -572,14 +579,14 @@
         firsts.append(first)
         vel_keeps.append(vel_keep)
         vel_recvs.append(swap(vel_give))
-        sel_j = sel if j == 0 else after(sel, last[-1][0])
+        sel_j = sel
         held_vel.append(pick(sel_j, spread(vel_b), cell))
-        arrived.append(gather(held_vel[-1]))
+        arrived.append((gather_flat if j == n - 1 else gather)(held_vel[-1]))
         if j < n - 1:
             last.append(apply_matrix(m_own, m_sib, arrived[-1], rows, ids, cell, patch_count))
     for j in range(n):
         if j == n - 1:
-            rows_j = rows if j == 0 else after(rows, keeps[-1])
+            rows_j = rows
             last.append(apply_matrix(m_own, m_sib, arrived[-1], rows_j, ids, cell, patch_count))
         keep, give = weigh(firsts[j], reduce(last[j]))
         keeps.append(keep)

time: 118 us -> 110 us (0.932)
  waiting for transfers between devices: 41.3 us -> 21.6 us
  starting transfers between devices: 43.3 us -> 51 us
  local copies, waits for them, and re-layouts: 0.05 us -> 3.11 us
    ppermute x24, waiting for transfers between devices: 27 us -> 14 us  [across(): return lax.ppermute(x, 'col', [(i, i ^ 2 * m) for i in range(n_col)])]
    ppermute x12, starting transfers between devices: 12 us -> 17.6 us  [along(): return lax.ppermute(x, 'row', [(i, i ^ s) for i in range(n_row)])]
    ppermute x12, waiting for transfers between devices: 10.4 us -> 5.83 us  [along(): return lax.ppermute(x, 'row', [(i, i ^ s) for i in range(n_row)])]
    unnamed x20 -> x22, local copies, waits for them, and re-layouts: 0.05 us -> 3.11 us
    ppermute x24, starting transfers between devices: 29.4 us -> 31.6 us  [across(): return lax.ppermute(x, 'col', [(i, i ^ 2 * m) for i in range(n_col)])]
    ppermute x8, waiting for transfers between devices: 3.86 us -> 1.74 us  [swap(): return lax.ppermute(x, 'col', [(i, i ^ 1) for i in range(n_col)])]
  transfers between devices with their start and end apart: 44 -> 44, of which waited for: 25 -> 14; matrix products, arithmetic and copies ran while one was open for 0% -> 0% of each run, Pallas kernels for 17% -> 24%
where the time goes in v4:
time: 110 us; the launch traced here: 109 us
  starting transfers between devices  51 us (46%)
  Pallas kernels  32.6 us (30%)
  waiting for transfers between devices  21.6 us (20%)
  local copies, waits for them, and re-layouts  3.11 us (3%)
    ppermute x24, starting transfers between devices, across(): return lax.ppermute(x, 'col', [(i, i ^ 2 * m) for i in range(n_col)])  31.6 us
    ppermute x12, starting transfers between devices, along(): return lax.ppermute(x, 'row', [(i, i ^ s) for i in range(n_row)])  17.6 us
    ppermute x24, waiting for transfers between devices, across(): return lax.ppermute(x, 'col', [(i, i ^ 2 * m) for i in range(n_col)])  14 us
    pallas_call x4, Pallas kernels, apply_matrix(): pl.pallas_call(functools.partial(apply_kernel, n_part, n_pair, n_row, cel...  12 us
    pallas_call x1, Pallas kernels, build_matrix(): pl.pallas_call(functools.partial(build_kernel, first, count), out_shape=s...  10.2 us
    ppermute x12, waiting for transfers between devices, along(): return lax.ppermute(x, 'row', [(i, i ^ s) for i in range(n_row)])  5.83 us
    unnamed x22, local copies, waits for them, and re-layouts  3.11 us
    pallas_call x1, Pallas kernels, start(): pl.pallas_call(functools.partial(start_kernel, chunks), out_shape=shapes...  2.94 us
  transfers between devices with their start and end apart: 44, of which 14 were waited for; matrix products, arithmetic and copies ran while one was open for 0% of the time, Pallas kernels for 24%

profile of v4, /device:TPU:0, one launch (start us, length us, event | category | flops | bytes accessed | tf_op | source)
XLA Modules:
  0.0 109.3 jit_solution(6222166642707508829)
XLA Ops:
  0.6 2.9 %start.1 = (bf16[272,128]{1,0:T(8,128)(2,1)}, bf16[256,128]{1,0:T(8,128)(2,1)}, bf16[272,128]{1,0:T(8,128)(2,1)}, bf16[256,128]{1,0:T(8,128)(2,1)}) custom-call(s32[2]{0:T(128)} %patch_rows.1, f32[256,512]{1,0:T(8,128)} %stress, f32[256,512]{1,0:T(8,128)} %state, f32[256,512]{1,0:T(8,128)} %direct), custom_call_target="tpu_custom_call" | custom-call | flops 13107 | bytes 18350 | tf_op jit(solution)/shard_map/start/pallas_call | solution.py:310
  6.5 3.7 %collective-permute-start.4 = (bf16[528,128]{1,0:T(8,128)(2,1)S(1)}, bf16[528,128]{1,0:T(8,128)(2,1)S(1)}, u32[]{:S(2)}, u32[]{:S(2)}) collective-permute-start(bf16[528,128]{1,0:T(8,128)(2,1)S(1)} %merge.2.refs_0_), channel_id=1, source_target_pairs={{0,6},{1,7},{2,4},{3,5},{4,2},{5,3},{6,0},{7,1},{8,14},{9,15},{10,... | collective-permute-start | bytes 405512 | tf_op jit(solution)/shard_map/ppermute | solution.py:506
  10.8 10.2 %build_matrix.1.refs_0_ = bf16[2048,1024]{1,0:T(8,128)(2,1)} custom-call(s32[7,1,16]{2,1,0:T(1,128)} %bitcast.5, s32[9,1,16]{2,1,0:T(1,128)} %bitcast.3, s32[9,1,16]{2,1,0:T(1,128)} %bitcast.4, bf16[16,1,7,128,128]{4,3,2,1,0:T(8,128)(2,1)} %near_in.1, bf16[16,1,9,32,128]{4,3,2,1,0:T(8,128)(2,1)} %left_in.1, bf16[16,1,9,32,128]{4,3,2,1,0:T(8,128)(2,1)} %right_in.1), custom_call_target="tpu_custom_call" | custom-call | flops 12079595 | bytes 60293 | tf_op jit(solution)/shard_map/build_matrix/pallas_call | solution.py:113
  21.1 1.9 %first_pick.1 = (bf16[528,128]{1,0:T(8,128)(2,1)S(1)}, s32[4]{0:T(128)S(1)}, s32[16]{0:T(128)S(1)}) custom-call(s32[16]{0:T(128)S(1)} %copy-done.10, bf16[528,128]{1,0:T(8,128)(2,1)S(1)} %merge.2.refs_0_, bf16[528,128]{1,0:T(8,128)(2,1)S(1)} %collective-permute-done.2.refs_1_, bf16[528,128]{1,0:T(8,128)(2,1)S(1)} %collective-permute-done.3.refs_2_, ...), custom_call_target="tpu_custom_call" | custom-call | flops 10 | bytes 2703 | tf_op jit(solution)/shard_map/first_pick/pallas_call | solution.py:202
  24.8 2.0 %collective-permute-start.8 = (bf16[528,128]{1,0:T(8,128)(2,1)S(1)}, bf16[528,128]{1,0:T(8,128)(2,1)S(1)}, u32[]{:S(2)}, u32[]{:S(2)}) collective-permute-start(bf16[528,128]{1,0:T(8,128)(2,1)S(1)} %get-tuple-element.70.refs_2_), channel_id=1, source_target_pairs={{0,8},{8,0},{16,24},{24,16},{1,9},{9,1},{17,25},{25,17},{2,10},{10... | collective-permute-start | bytes 405512 | tf_op jit(solution)/shard_map/ppermute | solution.py:509
  26.7 2.7 %collective-permute-start.7 = (bf16[528,128]{1,0:T(8,128)(2,1)S(1)}, bf16[528,128]{1,0:T(8,128)(2,1)S(1)}, u32[]{:S(2)}, u32[]{:S(2)}) collective-permute-start(bf16[528,128]{1,0:T(8,128)(2,1)S(1)} %get-tuple-element.70.refs_2_), channel_id=1, source_target_pairs={{0,16},{8,24},{16,0},{24,8},{1,17},{9,25},{17,1},{25,9},{2,18},{10... | collective-permute-start | bytes 405512 | tf_op jit(solution)/shard_map/ppermute | solution.py:509
  29.4 3.6 %collective-permute-done.8.refs_4_ = bf16[528,128]{1,0:T(8,128)(2,1)S(1)} collective-permute-done((bf16[528,128]{1,0:T(8,128)(2,1)S(1)}, bf16[528,128]{1,0:T(8,128)(2,1)S(1)}, u32[]{:S(2)}, u32[]{:S(2)}) %collective-permute-start.8) | collective-permute-done | bytes 135200 | tf_op jit(solution)/shard_map/ppermute | solution.py:509
  33.9 2.6 %collective-permute-start.9 = (bf16[528,128]{1,0:T(8,128)(2,1)S(1)}, bf16[528,128]{1,0:T(8,128)(2,1)S(1)}, u32[]{:S(2)}, u32[]{:S(2)}) collective-permute-start(bf16[528,128]{1,0:T(8,128)(2,1)S(1)} %collective-permute-done.7.refs_3_), channel_id=1, source_target_pairs={{0,8},{8,0},{16,24},{24,16},{1,9},{9,1},{17,25},{25,17},{2,10},{10... | collective-permute-start | bytes 405512 | tf_op jit(solution)/shard_map/ppermute | solution.py:509
  36.5 2.4 %collective-permute-start.24 = (bf16[512,128]{1,0:T(8,128)(2,1)S(1)}, bf16[512,128]{1,0:T(8,128)(2,1)S(1)}, u32[]{:S(2)}, u32[]{:S(2)}) collective-permute-start(bf16[512,128]{1,0:T(8,128)(2,1)S(1)} %merge.3.refs_0_), channel_id=1, source_target_pairs={{0,6},{1,7},{2,4},{3,5},{4,2},{5,3},{6,0},{7,1},{8,14},{9,15},{10,... | collective-permute-start | bytes 393224 | tf_op jit(solution)/shard_map/ppermute | solution.py:506
  39.5 3.0 %collective-permute-start.22 = (bf16[512,128]{1,0:T(8,128)(2,1)S(1)}, bf16[512,128]{1,0:T(8,128)(2,1)S(1)}, u32[]{:S(2)}, u32[]{:S(2)}) collective-permute-start(bf16[512,128]{1,0:T(8,128)(2,1)S(1)} %merge.3.refs_0_), channel_id=1, source_target_pairs={{0,2},{1,3},{2,0},{3,1},{4,6},{5,7},{6,4},{7,5},{8,10},{9,11},{10,... | collective-permute-start | bytes 393224 | tf_op jit(solution)/shard_map/ppermute | solution.py:506
  42.5 2.2 %copy-done = bf16[2048,1024]{1,0:T(8,128)(2,1)S(1)} copy-done((bf16[2048,1024]{1,0:T(8,128)(2,1)S(1)}, bf16[2048,1024]{1,0:T(8,128)(2,1)}, u32[]{:S(2)}) %copy-start) | copy-done | bytes 4194328
  44.7 3.1 %apply_matrix.4 = (f32[512,128]{1,0:T(8,128)S(1)}, bf16[512,128]{1,0:T(8,128)(2,1)S(1)}, bf16[512,128]{1,0:T(8,128)(2,1)S(1)}, bf16[512,128]{1,0:T(8,128)(2,1)S(1)}, s32[16]{0:T(128)S(1)}) custom-call(bf16[2048,1024]{1,0:T(8,128)(2,1)S(1)} %copy-done, bf16[2048,1024]{1,0:T(8,128)(2,1)S(1)} %collective-permute-done.6.refs_1_, ...), custom_call_target="tpu_custom_call" | custom-call | flops 10737418 | bytes 83886 | tf_op jit(solution)/shard_map/apply_matrix/pallas_call | solution.py:258
  49.0 2.6 %collective-permute-start.25 = (bf16[512,128]{1,0:T(8,128)(2,1)S(1)}, bf16[512,128]{1,0:T(8,128)(2,1)S(1)}, u32[]{:S(2)}, u32[]{:S(2)}) collective-permute-start(bf16[512,128]{1,0:T(8,128)(2,1)S(1)} %pick.4.refs_2_), channel_id=1, source_target_pairs={{0,16},{8,24},{16,0},{24,8},{1,17},{9,25},{17,1},{25,9},{2,18},{10... | collective-permute-start | bytes 393224 | tf_op jit(solution)/shard_map/ppermute | solution.py:509
  52.2 1.4 %collective-permute-start.11 = (bf16[512,128]{1,0:T(8,128)(2,1)S(1)}, bf16[512,128]{1,0:T(8,128)(2,1)S(1)}, u32[]{:S(2)}, u32[]{:S(2)}) collective-permute-start(bf16[512,128]{1,0:T(8,128)(2,1)S(1)} %get-tuple-element.85), channel_id=1, source_target_pairs={{0,4},{1,5},{2,6},{3,7},{4,0},{5,1},{6,2},{7,3},{8,12},{9,13},{10,... | collective-permute-start | bytes 393224 | tf_op jit(solution)/shard_map/ppermute | solution.py:506
  53.6 1.5 %collective-permute-start.12 = (bf16[512,128]{1,0:T(8,128)(2,1)S(1)}, bf16[512,128]{1,0:T(8,128)(2,1)S(1)}, u32[]{:S(2)}, u32[]{:S(2)}) collective-permute-start(bf16[512,128]{1,0:T(8,128)(2,1)S(1)} %get-tuple-element.86), channel_id=1, source_target_pairs={{0,6},{1,7},{2,4},{3,5},{4,2},{5,3},{6,0},{7,1},{8,14},{9,15},{10,... | collective-permute-start | bytes 393224 | tf_op jit(solution)/shard_map/ppermute | solution.py:506
  57.2 3.1 %collective-permute-done.12.refs_3_ = bf16[512,128]{1,0:T(8,128)(2,1)S(1)} collective-permute-done((bf16[512,128]{1,0:T(8,128)(2,1)S(1)}, bf16[512,128]{1,0:T(8,128)(2,1)S(1)}, u32[]{:S(2)}, u32[]{:S(2)}) %collective-permute-start.12) | collective-permute-done | bytes 131104 | tf_op jit(solution)/shard_map/ppermute | solution.py:506
  61.7 1.7 %collective-permute-start.14 = (bf16[512,128]{1,0:T(8,128)(2,1)S(1)}, bf16[512,128]{1,0:T(8,128)(2,1)S(1)}, u32[]{:S(2)}, u32[]{:S(2)}) collective-permute-start(bf16[512,128]{1,0:T(8,128)(2,1)S(1)} %get-tuple-element.89.refs_0_), channel_id=1, source_target_pairs={{0,4},{1,5},{2,6},{3,7},{4,0},{5,1},{6,2},{7,3},{8,12},{9,13},{10,... | collective-permute-start | bytes 393224 | tf_op jit(solution)/shard_map/ppermute | solution.py:506
  63.9 3.0 %apply_matrix.6 = (f32[512,128]{1,0:T(8,128)S(1)}, bf16[512,128]{1,0:T(8,128)(2,1)S(1)}, bf16[512,128]{1,0:T(8,128)(2,1)S(1)}, bf16[512,128]{1,0:T(8,128)(2,1)S(1)}) custom-call(bf16[2048,1024]{1,0:T(8,128)(2,1)S(1)} %copy-done.1, bf16[2048,1024]{1,0:T(8,128)(2,1)S(1)} %collective-permute-done.6.refs_1_, bf16[512,128]{1,0:T(8,128)(2,1)S(1)} %pick.4.refs_2_, ...), custom_call_target="tpu_custom_call" | custom-call | flops 10737418 | bytes 83886 | tf_op jit(solution)/shard_map/apply_matrix/pallas_call | solution.py:258
  66.9 1.5 %collective-permute-start.28 = (bf16[512,128]{1,0:T(8,128)(2,1)S(1)}, bf16[512,128]{1,0:T(8,128)(2,1)S(1)}, u32[]{:S(2)}, u32[]{:S(2)}) collective-permute-start(bf16[512,128]{1,0:T(8,128)(2,1)S(1)} %get-tuple-element.105), channel_id=1, source_target_pairs={{0,2},{1,3},{2,0},{3,1},{4,6},{5,7},{6,4},{7,5},{8,10},{9,11},{10,... | collective-permute-start | bytes 393224 | tf_op jit(solution)/shard_map/ppermute | solution.py:506
  68.8 1.7 %collective-permute-start.30 = (bf16[512,128]{1,0:T(8,128)(2,1)S(1)}, bf16[512,128]{1,0:T(8,128)(2,1)S(1)}, u32[]{:S(2)}, u32[]{:S(2)}) collective-permute-start(bf16[512,128]{1,0:T(8,128)(2,1)S(1)} %get-tuple-element.107), channel_id=1, source_target_pairs={{0,6},{1,7},{2,4},{3,5},{4,2},{5,3},{6,0},{7,1},{8,14},{9,15},{10,... | collective-permute-start | bytes 393224 | tf_op jit(solution)/shard_map/ppermute | solution.py:506
  71.4 2.5 %collective-permute-start.16 = (bf16[512,128]{1,0:T(8,128)(2,1)S(1)}, bf16[512,128]{1,0:T(8,128)(2,1)S(1)}, u32[]{:S(2)}, u32[]{:S(2)}) collective-permute-start(bf16[512,128]{1,0:T(8,128)(2,1)S(1)} %pick.3.refs_2_), channel_id=1, source_target_pairs={{0,16},{8,24},{16,0},{24,8},{1,17},{9,25},{17,1},{25,9},{2,18},{10... | collective-permute-start | bytes 393224 | tf_op jit(solution)/shard_map/ppermute | solution.py:509
  73.9 2.2 %collective-permute-done.29.refs_2_ = bf16[512,128]{1,0:T(8,128)(2,1)S(1)} collective-permute-done((bf16[512,128]{1,0:T(8,128)(2,1)S(1)}, bf16[512,128]{1,0:T(8,128)(2,1)S(1)}, u32[]{:S(2)}, u32[]{:S(2)}) %collective-permute-start.29) | collective-permute-done | bytes 131104 | tf_op jit(solution)/shard_map/ppermute | solution.py:506
  76.4 1.5 %collective-permute-start.33 = (bf16[512,128]{1,0:T(8,128)(2,1)S(1)}, bf16[512,128]{1,0:T(8,128)(2,1)S(1)}, u32[]{:S(2)}, u32[]{:S(2)}) collective-permute-start(bf16[512,128]{1,0:T(8,128)(2,1)S(1)} %get-tuple-element.109.refs_0_), channel_id=1, source_target_pairs={{0,6},{1,7},{2,4},{3,5},{4,2},{5,3},{6,0},{7,1},{8,14},{9,15},{10,... | collective-permute-start | bytes 393224 | tf_op jit(solution)/shard_map/ppermute | solution.py:506
  78.5 1.4 %collective-permute-start.31 = (bf16[512,128]{1,0:T(8,128)(2,1)S(1)}, bf16[512,128]{1,0:T(8,128)(2,1)S(1)}, u32[]{:S(2)}, u32[]{:S(2)}) collective-permute-start(bf16[512,128]{1,0:T(8,128)(2,1)S(1)} %get-tuple-element.109.refs_0_), channel_id=1, source_target_pairs={{0,2},{1,3},{2,0},{3,1},{4,6},{5,7},{6,4},{7,5},{8,10},{9,11},{10,... | collective-permute-start | bytes 393224 | tf_op jit(solution)/shard_map/ppermute | solution.py:506
  80.0 2.4 %collective-permute-done.33.refs_3_ = bf16[512,128]{1,0:T(8,128)(2,1)S(1)} collective-permute-done((bf16[512,128]{1,0:T(8,128)(2,1)S(1)}, bf16[512,128]{1,0:T(8,128)(2,1)S(1)}, u32[]{:S(2)}, u32[]{:S(2)}) %collective-permute-start.33) | collective-permute-done | bytes 131104 | tf_op jit(solution)/shard_map/ppermute | solution.py:506
  84.4 2.9 %collective-permute-start.36 = (bf16[512,128]{1,0:T(8,128)(2,1)S(1)}, bf16[512,128]{1,0:T(8,128)(2,1)S(1)}, u32[]{:S(2)}, u32[]{:S(2)}) collective-permute-start(bf16[512,128]{1,0:T(8,128)(2,1)S(1)} %pick.5.refs_2_), channel_id=1, source_target_pairs={{0,24},{8,16},{16,8},{24,0},{1,25},{9,17},{17,9},{25,1},{2,26},{10... | collective-permute-start | bytes 393224 | tf_op jit(solution)/shard_map/ppermute | solution.py:509
  87.4 1.5 %collective-permute-start.34 = (bf16[512,128]{1,0:T(8,128)(2,1)S(1)}, bf16[512,128]{1,0:T(8,128)(2,1)S(1)}, u32[]{:S(2)}, u32[]{:S(2)}) collective-permute-start(bf16[512,128]{1,0:T(8,128)(2,1)S(1)} %pick.5.refs_2_), channel_id=1, source_target_pairs={{0,16},{8,24},{16,0},{24,8},{1,17},{9,25},{17,1},{25,9},{2,18},{10... | collective-permute-start | bytes 393224 | tf_op jit(solution)/shard_map/ppermute | solution.py:509
  88.9 2.9 %apply_matrix.5 = (f32[512,128]{1,0:T(8,128)S(1)}, bf16[512,128]{1,0:T(8,128)(2,1)S(1)}, bf16[512,128]{1,0:T(8,128)(2,1)S(1)}, bf16[512,128]{1,0:T(8,128)(2,1)S(1)}) custom-call(bf16[2048,1024]{1,0:T(8,128)(2,1)S(1)} %copy-done.1, bf16[2048,1024]{1,0:T(8,128)(2,1)S(1)} %collective-permute-done.6.refs_1_, bf16[512,128]{1,0:T(8,128)(2,1)S(1)} %pick.3.refs_2_, ...), custom_call_target="tpu_custom_call" | custom-call | flops 10737418 | bytes 83886 | tf_op jit(solution)/shard_map/apply_matrix/pallas_call | solution.py:258
  93.0 1.5 %collective-permute-start.20 = (bf16[512,128]{1,0:T(8,128)(2,1)S(1)}, bf16[512,128]{1,0:T(8,128)(2,1)S(1)}, u32[]{:S(2)}, u32[]{:S(2)}) collective-permute-start(bf16[512,128]{1,0:T(8,128)(2,1)S(1)} %get-tuple-element.94), channel_id=1, source_target_pairs={{0,4},{1,5},{2,6},{3,7},{4,0},{5,1},{6,2},{7,3},{8,12},{9,13},{10,... | collective-permute-start | bytes 393224 | tf_op jit(solution)/shard_map/ppermute | solution.py:506
  95.4 3.0 %apply_matrix.7 = (f32[512,128]{1,0:T(8,128)S(1)}, bf16[512,128]{1,0:T(8,128)(2,1)S(1)}, bf16[512,128]{1,0:T(8,128)(2,1)S(1)}, bf16[512,128]{1,0:T(8,128)(2,1)S(1)}) custom-call(bf16[2048,1024]{1,0:T(8,128)(2,1)S(1)} %copy-done.1, bf16[2048,1024]{1,0:T(8,128)(2,1)S(1)} %collective-permute-done.6.refs_1_, bf16[512,128]{1,0:T(8,128)(2,1)S(1)} %pick.5.refs_2_, ...), custom_call_target="tpu_custom_call" | custom-call | flops 10737418 | bytes 83886 | tf_op jit(solution)/shard_map/apply_matrix/pallas_call | solution.py:258
  99.5 1.5 %collective-permute-start.38 = (bf16[512,128]{1,0:T(8,128)(2,1)S(1)}, bf16[512,128]{1,0:T(8,128)(2,1)S(1)}, u32[]{:S(2)}, u32[]{:S(2)}) collective-permute-start(bf16[512,128]{1,0:T(8,128)(2,1)S(1)} %get-tuple-element.112), channel_id=1, source_target_pairs={{0,4},{1,5},{2,6},{3,7},{4,0},{5,1},{6,2},{7,3},{8,12},{9,13},{10,... | collective-permute-start | bytes 393224 | tf_op jit(solution)/shard_map/ppermute | solution.py:506
  104.5 2.4 %collective-permute-done.39.refs_3_ = bf16[512,128]{1,0:T(8,128)(2,1)S(1)} collective-permute-done((bf16[512,128]{1,0:T(8,128)(2,1)S(1)}, bf16[512,128]{1,0:T(8,128)(2,1)S(1)}, u32[]{:S(2)}, u32[]{:S(2)}) %collective-permute-start.39) | collective-permute-done | bytes 131104 | tf_op jit(solution)/shard_map/ppermute | solution.py:506
  (97 shorter events, 26.0 us)
Async XLA Ops:
  6.5 14.6 %collective-permute-start.4 = (bf16[528,128]{1,0:T(8,128)(2,1)S(1)}, bf16[528,128]{1,0:T(8,128)(2,1)S(1)}, u32[]{:S(2)}, u32[]{:S(2)}) collective-permute-start(bf16[528,128]{1,0:T(8,128)(2,1)S(1)} %merge.2.refs_0_), channel_id=1, source_target_pairs={{0,6},{1,7},{2,4},{3,5},{4,2},{5,3},{6,0},{7,1},{8,14},{9,15},{10,... | collective-permute-start | bytes 405512 | tf_op jit(solution)/shard_map/ppermute | solution.py:506
  10.1 10.9 %collective-permute-start.3 = (bf16[528,128]{1,0:T(8,128)(2,1)S(1)}, bf16[528,128]{1,0:T(8,128)(2,1)S(1)}, u32[]{:S(2)}, u32[]{:S(2)}) collective-permute-start(bf16[528,128]{1,0:T(8,128)(2,1)S(1)} %merge.2.refs_0_), channel_id=1, source_target_pairs={{0,4},{1,5},{2,6},{3,7},{4,0},{5,1},{6,2},{7,3},{8,12},{9,13},{10,... | collective-permute-start | bytes 405512 | tf_op jit(solution)/shard_map/ppermute | solution.py:506
  10.6 10.4 %collective-permute-start.2 = (bf16[528,128]{1,0:T(8,128)(2,1)S(1)}, bf16[528,128]{1,0:T(8,128)(2,1)S(1)}, u32[]{:S(2)}, u32[]{:S(2)}) collective-permute-start(bf16[528,128]{1,0:T(8,128)(2,1)S(1)} %merge.2.refs_0_), channel_id=1, source_target_pairs={{0,2},{1,3},{2,0},{3,1},{4,6},{5,7},{6,4},{7,5},{8,10},{9,11},{10,... | collective-permute-start | bytes 405512 | tf_op jit(solution)/shard_map/ppermute | solution.py:506
  23.0 19.6 %collective-permute-start.6 = (bf16[2048,1024]{1,0:T(8,128)(2,1)}, bf16[2048,1024]{1,0:T(8,128)(2,1)S(1)}, u32[]{:S(2)}, u32[]{:S(2)}) collective-permute-start(bf16[2048,1024]{1,0:T(8,128)(2,1)} %build_matrix.1.refs_0_), channel_id=1, source_target_pairs={{0,1},{1,0},{2,3},{3,2},{4,5},{5,4},{6,7},{7,6},{8,9},{9,8},{10,11... | collective-permute-start | bytes 12582920 | tf_op jit(solution)/shard_map/ppermute | solution.py:503
  24.2 23.6 %collective-permute-start.5 = (f32[2,3,256,128]{3,2,1,0:T(8,128)S(1)}, f32[2,3,256,128]{3,2,1,0:T(8,128)S(1)}, u32[]{:S(2)}, u32[]{:S(2)}) collective-permute-start(f32[2,3,256,128]{3,2,1,0:T(8,128)S(1)} %get-tuple-element.79), channel_id=1, source_target_pairs={{0,1},{1,0},{2,3},{3,2},{4,5},{5,4},{6,7},{7,6},{8,9},{9,8},{10,11... | collective-permute-start | bytes 2359304 | tf_op jit(solution)/shard_map/ppermute | solution.py:503
  24.8 8.3 %collective-permute-start.8 = (bf16[528,128]{1,0:T(8,128)(2,1)S(1)}, bf16[528,128]{1,0:T(8,128)(2,1)S(1)}, u32[]{:S(2)}, u32[]{:S(2)}) collective-permute-start(bf16[528,128]{1,0:T(8,128)(2,1)S(1)} %get-tuple-element.70.refs_2_), channel_id=1, source_target_pairs={{0,8},{8,0},{16,24},{24,16},{1,9},{9,1},{17,25},{25,17},{2,10},{10... | collective-permute-start | bytes 405512 | tf_op jit(solution)/shard_map/ppermute | solution.py:509
  26.7 7.1 %collective-permute-start.7 = (bf16[528,128]{1,0:T(8,128)(2,1)S(1)}, bf16[528,128]{1,0:T(8,128)(2,1)S(1)}, u32[]{:S(2)}, u32[]{:S(2)}) collective-permute-start(bf16[528,128]{1,0:T(8,128)(2,1)S(1)} %get-tuple-element.70.refs_2_), channel_id=1, source_target_pairs={{0,16},{8,24},{16,0},{24,8},{1,17},{9,25},{17,1},{25,9},{2,18},{10... | collective-permute-start | bytes 405512 | tf_op jit(solution)/shard_map/ppermute | solution.py:509
  36.5 11.4 %collective-permute-start.24 = (bf16[512,128]{1,0:T(8,128)(2,1)S(1)}, bf16[512,128]{1,0:T(8,128)(2,1)S(1)}, u32[]{:S(2)}, u32[]{:S(2)}) collective-permute-start(bf16[512,128]{1,0:T(8,128)(2,1)S(1)} %merge.3.refs_0_), channel_id=1, source_target_pairs={{0,6},{1,7},{2,4},{3,5},{4,2},{5,3},{6,0},{7,1},{8,14},{9,15},{10,... | collective-permute-start | bytes 393224 | tf_op jit(solution)/shard_map/ppermute | solution.py:506
  38.8 9.0 %collective-permute-start.23 = (bf16[512,128]{1,0:T(8,128)(2,1)S(1)}, bf16[512,128]{1,0:T(8,128)(2,1)S(1)}, u32[]{:S(2)}, u32[]{:S(2)}) collective-permute-start(bf16[512,128]{1,0:T(8,128)(2,1)S(1)} %merge.3.refs_0_), channel_id=1, source_target_pairs={{0,4},{1,5},{2,6},{3,7},{4,0},{5,1},{6,2},{7,3},{8,12},{9,13},{10,... | collective-permute-start | bytes 393224 | tf_op jit(solution)/shard_map/ppermute | solution.py:506
  39.5 8.4 %collective-permute-start.22 = (bf16[512,128]{1,0:T(8,128)(2,1)S(1)}, bf16[512,128]{1,0:T(8,128)(2,1)S(1)}, u32[]{:S(2)}, u32[]{:S(2)}) collective-permute-start(bf16[512,128]{1,0:T(8,128)(2,1)S(1)} %merge.3.refs_0_), channel_id=1, source_target_pairs={{0,2},{1,3},{2,0},{3,1},{4,6},{5,7},{6,4},{7,5},{8,10},{9,11},{10,... | collective-permute-start | bytes 393224 | tf_op jit(solution)/shard_map/ppermute | solution.py:506
  48.5 6.6 %collective-permute-start.26 = (bf16[512,128]{1,0:T(8,128)(2,1)S(1)}, bf16[512,128]{1,0:T(8,128)(2,1)S(1)}, u32[]{:S(2)}, u32[]{:S(2)}) collective-permute-start(bf16[512,128]{1,0:T(8,128)(2,1)S(1)} %pick.4.refs_2_), channel_id=1, source_target_pairs={{0,8},{8,0},{16,24},{24,16},{1,9},{9,1},{17,25},{25,17},{2,10},{10... | collective-permute-start | bytes 393224 | tf_op jit(solution)/shard_map/ppermute | solution.py:509
  49.0 7.4 %collective-permute-start.25 = (bf16[512,128]{1,0:T(8,128)(2,1)S(1)}, bf16[512,128]{1,0:T(8,128)(2,1)S(1)}, u32[]{:S(2)}, u32[]{:S(2)}) collective-permute-start(bf16[512,128]{1,0:T(8,128)(2,1)S(1)} %pick.4.refs_2_), channel_id=1, source_target_pairs={{0,16},{8,24},{16,0},{24,8},{1,17},{9,25},{17,1},{25,9},{2,18},{10... | collective-permute-start | bytes 393224 | tf_op jit(solution)/shard_map/ppermute | solution.py:509
  53.6 6.6 %collective-permute-start.12 = (bf16[512,128]{1,0:T(8,128)(2,1)S(1)}, bf16[512,128]{1,0:T(8,128)(2,1)S(1)}, u32[]{:S(2)}, u32[]{:S(2)}) collective-permute-start(bf16[512,128]{1,0:T(8,128)(2,1)S(1)} %get-tuple-element.86), channel_id=1, source_target_pairs={{0,6},{1,7},{2,4},{3,5},{4,2},{5,3},{6,0},{7,1},{8,14},{9,15},{10,... | collective-permute-start | bytes 393224 | tf_op jit(solution)/shard_map/ppermute | solution.py:506
  56.5 7.5 %collective-permute-start.27 = (bf16[512,128]{1,0:T(8,128)(2,1)S(1)}, bf16[512,128]{1,0:T(8,128)(2,1)S(1)}, u32[]{:S(2)}, u32[]{:S(2)}) collective-permute-start(bf16[512,128]{1,0:T(8,128)(2,1)S(1)} %collective-permute-done.25.refs_3_), channel_id=1, source_target_pairs={{0,8},{8,0},{16,24},{24,16},{1,9},{9,1},{17,25},{25,17},{2,10},{10... | collective-permute-start | bytes 393224 | tf_op jit(solution)/shard_map/ppermute | solution.py:509
  60.4 8.4 %collective-permute-start.15 = (bf16[512,128]{1,0:T(8,128)(2,1)S(1)}, bf16[512,128]{1,0:T(8,128)(2,1)S(1)}, u32[]{:S(2)}, u32[]{:S(2)}) collective-permute-start(bf16[512,128]{1,0:T(8,128)(2,1)S(1)} %get-tuple-element.89.refs_0_), channel_id=1, source_target_pairs={{0,6},{1,7},{2,4},{3,5},{4,2},{5,3},{6,0},{7,1},{8,14},{9,15},{10,... | collective-permute-start | bytes 393224 | tf_op jit(solution)/shard_map/ppermute | solution.py:506
  61.7 8.8 %collective-permute-start.14 = (bf16[512,128]{1,0:T(8,128)(2,1)S(1)}, bf16[512,128]{1,0:T(8,128)(2,1)S(1)}, u32[]{:S(2)}, u32[]{:S(2)}) collective-permute-start(bf16[512,128]{1,0:T(8,128)(2,1)S(1)} %get-tuple-element.89.refs_0_), channel_id=1, source_target_pairs={{0,4},{1,5},{2,6},{3,7},{4,0},{5,1},{6,2},{7,3},{8,12},{9,13},{10,... | collective-permute-start | bytes 393224 | tf_op jit(solution)/shard_map/ppermute | solution.py:506
  63.4 7.1 %collective-permute-start.13 = (bf16[512,128]{1,0:T(8,128)(2,1)S(1)}, bf16[512,128]{1,0:T(8,128)(2,1)S(1)}, u32[]{:S(2)}, u32[]{:S(2)}) collective-permute-start(bf16[512,128]{1,0:T(8,128)(2,1)S(1)} %get-tuple-element.89.refs_0_), channel_id=1, source_target_pairs={{0,2},{1,3},{2,0},{3,1},{4,6},{5,7},{6,4},{7,5},{8,10},{9,11},{10,... | collective-permute-start | bytes 393224 | tf_op jit(solution)/shard_map/ppermute | solution.py:506
  66.9 7.0 %collective-permute-start.28 = (bf16[512,128]{1,0:T(8,128)(2,1)S(1)}, bf16[512,128]{1,0:T(8,128)(2,1)S(1)}, u32[]{:S(2)}, u32[]{:S(2)}) collective-permute-start(bf16[512,128]{1,0:T(8,128)(2,1)S(1)} %get-tuple-element.105), channel_id=1, source_target_pairs={{0,2},{1,3},{2,0},{3,1},{4,6},{5,7},{6,4},{7,5},{8,10},{9,11},{10,... | collective-permute-start | bytes 393224 | tf_op jit(solution)/shard_map/ppermute | solution.py:506
  68.4 7.8 %collective-permute-start.29 = (bf16[512,128]{1,0:T(8,128)(2,1)S(1)}, bf16[512,128]{1,0:T(8,128)(2,1)S(1)}, u32[]{:S(2)}, u32[]{:S(2)}) collective-permute-start(bf16[512,128]{1,0:T(8,128)(2,1)S(1)} %get-tuple-element.106), channel_id=1, source_target_pairs={{0,4},{1,5},{2,6},{3,7},{4,0},{5,1},{6,2},{7,3},{8,12},{9,13},{10,... | collective-permute-start | bytes 393224 | tf_op jit(solution)/shard_map/ppermute | solution.py:506
  68.8 7.4 %collective-permute-start.30 = (bf16[512,128]{1,0:T(8,128)(2,1)S(1)}, bf16[512,128]{1,0:T(8,128)(2,1)S(1)}, u32[]{:S(2)}, u32[]{:S(2)}) collective-permute-start(bf16[512,128]{1,0:T(8,128)(2,1)S(1)} %get-tuple-element.107), channel_id=1, source_target_pairs={{0,6},{1,7},{2,4},{3,5},{4,2},{5,3},{6,0},{7,1},{8,14},{9,15},{10,... | collective-permute-start | bytes 393224 | tf_op jit(solution)/shard_map/ppermute | solution.py:506
  71.3 8.6 %collective-permute-start.17 = (bf16[512,128]{1,0:T(8,128)(2,1)S(1)}, bf16[512,128]{1,0:T(8,128)(2,1)S(1)}, u32[]{:S(2)}, u32[]{:S(2)}) collective-permute-start(bf16[512,128]{1,0:T(8,128)(2,1)S(1)} %pick.3.refs_2_), channel_id=1, source_target_pairs={{0,8},{8,0},{16,24},{24,16},{1,9},{9,1},{17,25},{25,17},{2,10},{10... | collective-permute-start | bytes 393224 | tf_op jit(solution)/shard_map/ppermute | solution.py:509
  71.4 8.5 %collective-permute-start.16 = (bf16[512,128]{1,0:T(8,128)(2,1)S(1)}, bf16[512,128]{1,0:T(8,128)(2,1)S(1)}, u32[]{:S(2)}, u32[]{:S(2)}) collective-permute-start(bf16[512,128]{1,0:T(8,128)(2,1)S(1)} %pick.3.refs_2_), channel_id=1, source_target_pairs={{0,16},{8,24},{16,0},{24,8},{1,17},{9,25},{17,1},{25,9},{2,18},{10... | collective-permute-start | bytes 393224 | tf_op jit(solution)/shard_map/ppermute | solution.py:509
  76.4 6.0 %collective-permute-start.33 = (bf16[512,128]{1,0:T(8,128)(2,1)S(1)}, bf16[512,128]{1,0:T(8,128)(2,1)S(1)}, u32[]{:S(2)}, u32[]{:S(2)}) collective-permute-start(bf16[512,128]{1,0:T(8,128)(2,1)S(1)} %get-tuple-element.109.refs_0_), channel_id=1, source_target_pairs={{0,6},{1,7},{2,4},{3,5},{4,2},{5,3},{6,0},{7,1},{8,14},{9,15},{10,... | collective-permute-start | bytes 393224 | tf_op jit(solution)/shard_map/ppermute | solution.py:506
  77.8 5.8 %collective-permute-start.32 = (bf16[512,128]{1,0:T(8,128)(2,1)S(1)}, bf16[512,128]{1,0:T(8,128)(2,1)S(1)}, u32[]{:S(2)}, u32[]{:S(2)}) collective-permute-start(bf16[512,128]{1,0:T(8,128)(2,1)S(1)} %get-tuple-element.109.refs_0_), channel_id=1, source_target_pairs={{0,4},{1,5},{2,6},{3,7},{4,0},{5,1},{6,2},{7,3},{8,12},{9,13},{10,... | collective-permute-start | bytes 393224 | tf_op jit(solution)/shard_map/ppermute | solution.py:506
  79.9 9.0 %collective-permute-start.18 = (bf16[512,128]{1,0:T(8,128)(2,1)S(1)}, bf16[512,128]{1,0:T(8,128)(2,1)S(1)}, u32[]{:S(2)}, u32[]{:S(2)}) collective-permute-start(bf16[512,128]{1,0:T(8,128)(2,1)S(1)} %collective-permute-done.16.refs_3_), channel_id=1, source_target_pairs={{0,8},{8,0},{16,24},{24,16},{1,9},{9,1},{17,25},{25,17},{2,10},{10... | collective-permute-start | bytes 393224 | tf_op jit(solution)/shard_map/ppermute | solution.py:509
  84.4 10.1 %collective-permute-start.36 = (bf16[512,128]{1,0:T(8,128)(2,1)S(1)}, bf16[512,128]{1,0:T(8,128)(2,1)S(1)}, u32[]{:S(2)}, u32[]{:S(2)}) collective-permute-start(bf16[512,128]{1,0:T(8,128)(2,1)S(1)} %pick.5.refs_2_), channel_id=1, source_target_pairs={{0,24},{8,16},{16,8},{24,0},{1,25},{9,17},{17,9},{25,1},{2,26},{10... | collective-permute-start | bytes 393224 | tf_op jit(solution)/shard_map/ppermute | solution.py:509
  87.4 8.0 %collective-permute-start.35 = (bf16[512,128]{1,0:T(8,128)(2,1)S(1)}, bf16[512,128]{1,0:T(8,128)(2,1)S(1)}, u32[]{:S(2)}, u32[]{:S(2)}) collective-permute-start(bf16[512,128]{1,0:T(8,128)(2,1)S(1)} %pick.5.refs_2_), channel_id=1, source_target_pairs={{0,8},{8,0},{16,24},{24,16},{1,9},{9,1},{17,25},{25,17},{2,10},{10... | collective-permute-start | bytes 393224 | tf_op jit(solution)/shard_map/ppermute | solution.py:509
  87.4 8.0 %collective-permute-start.34 = (bf16[512,128]{1,0:T(8,128)(2,1)S(1)}, bf16[512,128]{1,0:T(8,128)(2,1)S(1)}, u32[]{:S(2)}, u32[]{:S(2)}) collective-permute-start(bf16[512,128]{1,0:T(8,128)(2,1)S(1)} %pick.5.refs_2_), channel_id=1, source_target_pairs={{0,16},{8,24},{16,0},{24,8},{1,17},{9,25},{17,1},{25,9},{2,18},{10... | collective-permute-start | bytes 393224 | tf_op jit(solution)/shard_map/ppermute | solution.py:509
  91.8 9.2 %collective-permute-start.19 = (bf16[512,128]{1,0:T(8,128)(2,1)S(1)}, bf16[512,128]{1,0:T(8,128)(2,1)S(1)}, u32[]{:S(2)}, u32[]{:S(2)}) collective-permute-start(bf16[512,128]{1,0:T(8,128)(2,1)S(1)} %get-tuple-element.93), channel_id=1, source_target_pairs={{0,2},{1,3},{2,0},{3,1},{4,6},{5,7},{6,4},{7,5},{8,10},{9,11},{10,... | collective-permute-start | bytes 393224 | tf_op jit(solution)/shard_map/ppermute | solution.py:506
  93.0 8.9 %collective-permute-start.20 = (bf16[512,128]{1,0:T(8,128)(2,1)S(1)}, bf16[512,128]{1,0:T(8,128)(2,1)S(1)}, u32[]{:S(2)}, u32[]{:S(2)}) collective-permute-start(bf16[512,128]{1,0:T(8,128)(2,1)S(1)} %get-tuple-element.94), channel_id=1, source_target_pairs={{0,4},{1,5},{2,6},{3,7},{4,0},{5,1},{6,2},{7,3},{8,12},{9,13},{10,... | collective-permute-start | bytes 393224 | tf_op jit(solution)/shard_map/ppermute | solution.py:506
  94.5 7.4 %collective-permute-start.21 = (bf16[512,128]{1,0:T(8,128)(2,1)S(1)}, bf16[512,128]{1,0:T(8,128)(2,1)S(1)}, u32[]{:S(2)}, u32[]{:S(2)}) collective-permute-start(bf16[512,128]{1,0:T(8,128)(2,1)S(1)} %get-tuple-element.95), channel_id=1, source_target_pairs={{0,6},{1,7},{2,4},{3,5},{4,2},{5,3},{6,0},{7,1},{8,14},{9,15},{10,... | collective-permute-start | bytes 393224 | tf_op jit(solution)/shard_map/ppermute | solution.py:506
  101.0 5.9 %collective-permute-start.39 = (bf16[512,128]{1,0:T(8,128)(2,1)S(1)}, bf16[512,128]{1,0:T(8,128)(2,1)S(1)}, u32[]{:S(2)}, u32[]{:S(2)}) collective-permute-start(bf16[512,128]{1,0:T(8,128)(2,1)S(1)} %get-tuple-element.113), channel_id=1, source_target_pairs={{0,6},{1,7},{2,4},{3,5},{4,2},{5,3},{6,0},{7,1},{8,14},{9,15},{10,... | collective-permute-start | bytes 393224 | tf_op jit(solution)/shard_map/ppermute | solution.py:506
  (23 other events, 172.4 us)
